TPU v7x, 128 devices: a whole 4x4x4 slice. The times are simulated.
128 devices in a mesh: ctx: 32 (over y, x_hi, z), fsdp: 4 (over x_lo, core).
Axes of the slice: x: 4 (x_hi: 2, x_lo: 2; x = x_hi * 2 + x_lo), y: 4, z: 4, core: 2. Of those that a mesh axis runs over, the one named last changes fastest.
Arguments:
- tokens: bfloat16 [4, 4096, 1536], P('fsdp', 'ctx'), may hold values from -6 to 6
- block_order: int32 [64], replicated, may hold values from 0 to 63, as said below
- gain_attn: bfloat16 [1536], P('fsdp'), may hold values from 0.5 to 1.5
- gain_mlp: bfloat16 [1536], P('fsdp'), may hold values from 0.5 to 1.5
- w_query: bfloat16 [1536, 1536], P('fsdp'), may hold values from -0.15625 to 0.15625
- w_key: bfloat16 [1536, 768], P('fsdp'), may hold values from -0.15625 to 0.15625
- w_value: bfloat16 [1536, 768], P('fsdp'), may hold values from -0.15625 to 0.15625
- w_out: bfloat16 [1536, 1536], P('fsdp'), may hold values from -0.875 to 0.875
- w_gate: bfloat16 [1536, 4096], P(None, 'fsdp'), may hold values from -0.15625 to 0.15625
- w_up: bfloat16 [1536, 4096], P(None, 'fsdp'), may hold values from -0.15625 to 0.15625
- w_down: bfloat16 [4096, 1536], P('fsdp'), may hold values from -0.09375 to 0.09375
- cotangent: bfloat16 [4, 4096, 1536], P('fsdp', 'ctx'), may hold values from -6 to 6
Outputs:
- layer_out: bfloat16 [4, 4096, 1536], P('fsdp', 'ctx')
- d_tokens: float32 [4, 4096, 1536], P('fsdp', 'ctx')
- grad_gain_attn: float32 [1536], P('fsdp')
- grad_gain_mlp: float32 [1536], P('fsdp')
- query_weight_gradient: float32 [1536, 1536], P('fsdp')
- grad_w_key: float32 [1536, 768], P('fsdp')
- grad_w_value: float32 [1536, 768], P('fsdp')
- grad_w_out: float32 [1536, 1536], P('fsdp')
- grad_w_gate: float32 [1536, 4096], P(None, 'fsdp')
- grad_w_up: float32 [1536, 4096], P(None, 'fsdp')
- grad_w_down: float32 [4096, 1536], P('fsdp')
Inputs may be any that keep to these rules, and one draw needn't show every extreme that they name: `block_order`: places 2c and 2c+1 hold two blocks b and 63 - b (in either order); every block appears once.
All inputs are finite; a program needn't handle non-finite values.
Results may differ from a plain program's by a relative error of at most 0.03.
Values may be sent and summed in bfloat16 or wider, within the bound.
No kernel may reach another device: no remote copies, remote signals or barrier semaphores. Data moves between devices by JAX's collectives and lax.ppermute only.
A program may use at most 256 MiB of HBM per device.

v0:
```python
import jax
import jax.numpy as jnp
from jax import lax
from jax.sharding import PartitionSpec as P

HEADS = 16
KV_HEADS = 8
HEAD_DIM = 96


EPS = 1e-05
ROPE_BASE = 10000.0
MASKED = -1e30


def rope_tables(positions, head_size):
    half = head_size // 2
    freqs = ROPE_BASE ** (-jnp.arange(half).astype(jnp.float32) * 2.0 / head_size)
    angles = positions.astype(jnp.float32)[:, None] * freqs[None, :]
    angles = jnp.concatenate([angles, angles], axis=1)
    return (jnp.cos(angles), jnp.sin(angles))


def rotate(values, cosine, sine):
    half = values.shape[-1] // 2
    turned = jnp.concatenate([-values[..., half:], values[..., :half]], axis=-1)
    return values * cosine + turned * sine


def rotate_back(grads, cosine, sine):
    half = grads.shape[-1] // 2
    scaled = grads * sine
    turned = jnp.concatenate([scaled[..., half:], -scaled[..., :half]], axis=-1)
    return grads * cosine + turned


def row_norm(values, gain):
    factor = lax.rsqrt(jnp.mean(values * values, axis=-1, keepdims=True) + EPS)
    return (values * factor * gain, factor)


def norm_back(values, factor, gain, grads):
    weighted = grads * gain
    inner = jnp.mean(weighted * values, axis=-1, keepdims=True)
    d_values = factor * weighted - values * (factor * factor * factor) * inner
    d_gain = jnp.sum(grads * values * factor, axis=0)
    return (d_values, d_gain)


def visible_positions(query_pos, key_pos, block, window):
    query_blk = query_pos // block
    key_blk = key_pos // block
    same = query_blk[:, None] == key_blk[None, :]
    earlier = (key_blk[None, :] < query_blk[:, None]) & (
        query_pos[:, None] - key_pos[None, :] < window
    )
    return same | earlier


def group_forward(queries, keys, values, allowed, scale):
    raw = jnp.einsum("tjrd,ljd->jrtl", queries, keys, preferred_element_type=jnp.float32)
    scores = jnp.where(allowed, raw * scale, MASKED)
    top = jnp.max(scores, axis=-1, keepdims=True)
    expo = jnp.exp(scores - top)
    total = jnp.sum(expo, axis=-1, keepdims=True)
    probs = (expo / total).astype(jnp.bfloat16)
    result = jnp.einsum("jrtl,ljd->tjrd", probs, values, preferred_element_type=jnp.float32)
    return (result, (top + jnp.log(total))[..., 0])


def group_backward(queries, keys, values, log_total, d_result, allowed, scale):
    raw = jnp.einsum("tjrd,ljd->jrtl", queries, keys, preferred_element_type=jnp.float32)
    scores = jnp.where(allowed, raw * scale, MASKED)
    probs = jnp.exp(scores - log_total[..., None])
    d_probs = jnp.einsum("tjrd,ljd->jrtl", d_result, values, preferred_element_type=jnp.float32)
    inner = jnp.sum(probs * d_probs, axis=-1, keepdims=True)
    d_raw = (probs * (d_probs - inner) * scale).astype(jnp.bfloat16)
    d_queries = jnp.einsum("jrtl,ljd->tjrd", d_raw, keys, preferred_element_type=jnp.float32)
    d_keys = jnp.einsum("jrtl,tjrd->ljd", d_raw, queries, preferred_element_type=jnp.float32)
    d_values = jnp.einsum(
        "jrtl,tjrd->ljd", probs.astype(jnp.bfloat16), d_result, preferred_element_type=jnp.float32
    )
    return (d_queries, d_keys, d_values)


def body(
    tokens,
    block_order,
    gain_attn,
    gain_mlp,
    w_query,
    w_key,
    w_value,
    w_out,
    w_gate,
    w_up,
    w_down,
    cotangent,
):
    rows = tokens.shape[1]
    block = rows // 2
    window = rows * lax.axis_size("ctx") // 2
    repeat = HEADS // KV_HEADS
    pairs = KV_HEADS // 2
    query_width = HEADS * HEAD_DIM
    kv_width = KV_HEADS * HEAD_DIM
    scale = HEAD_DIM ** (-0.5)
    inputs = tokens[0].astype(jnp.float32)
    d_output = cotangent[0].astype(jnp.float32)
    offsets = jnp.arange(block)
    own_blocks = lax.dynamic_slice_in_dim(block_order, 2 * lax.axis_index("ctx"), 2)
    query_pos = (own_blocks[:, None] * block + offsets[None, :]).reshape(-1)
    key_pos = (block_order[:, None] * block + offsets[None, :]).reshape(-1)
    allowed = visible_positions(query_pos, key_pos, block, window)
    cosine, sine = rope_tables(query_pos, HEAD_DIM)
    cosine = cosine[:, None, :]
    sine = sine[:, None, :]
    gain_a, gain_m, full_query, full_key, full_value, full_out = (
        lax.all_gather(gain_attn, "fsdp", axis=0, tiled=True),
        lax.all_gather(gain_mlp, "fsdp", axis=0, tiled=True),
        lax.all_gather(w_query, "fsdp", axis=0, tiled=True),
        lax.all_gather(w_key, "fsdp", axis=0, tiled=True),
        lax.all_gather(w_value, "fsdp", axis=0, tiled=True),
        lax.all_gather(w_out, "fsdp", axis=0, tiled=True),
    )
    gain_a = gain_a.astype(jnp.float32)
    gain_m = gain_m.astype(jnp.float32)
    normed_a, factor_a = row_norm(inputs, gain_a)
    x_attn = normed_a.astype(jnp.bfloat16)
    q_lin = jnp.dot(x_attn, full_query, preferred_element_type=jnp.float32)
    k_lin = jnp.dot(x_attn, full_key, preferred_element_type=jnp.float32)
    v_own = jnp.dot(x_attn, full_value, preferred_element_type=jnp.float32).astype(jnp.bfloat16)
    q_lin = q_lin.reshape(rows, HEADS, HEAD_DIM)
    k_lin = k_lin.reshape(rows, KV_HEADS, HEAD_DIM)
    queries = rotate(q_lin, cosine, sine).astype(jnp.bfloat16)
    k_own = rotate(k_lin, cosine, sine).reshape(rows, kv_width).astype(jnp.bfloat16)
    keys_all, values_all = (
        lax.all_gather(k_own, "ctx", axis=0, tiled=True),
        lax.all_gather(v_own, "ctx", axis=0, tiled=True),
    )
    length = keys_all.shape[0]

    def query_groups(values):
        return values.reshape(rows, pairs, 2, repeat, HEAD_DIM).transpose(1, 0, 2, 3, 4)

    def key_groups(values):
        return values.reshape(length, pairs, 2, HEAD_DIM).transpose(1, 0, 2, 3)

    grouped_q = query_groups(queries)
    grouped_k = key_groups(keys_all)
    grouped_v = key_groups(values_all)

    def forward_group(items):
        return group_forward(items[0], items[1], items[2], allowed, scale)

    mixed, log_total = lax.map(forward_group, (grouped_q, grouped_k, grouped_v))
    attn_mix = mixed.transpose(1, 0, 2, 3, 4).reshape(rows, query_width).astype(jnp.bfloat16)
    hidden = inputs + jnp.dot(attn_mix, full_out, preferred_element_type=jnp.float32)
    normed_m, factor_m = row_norm(hidden, gain_m)
    x_mlp = normed_m.astype(jnp.bfloat16)
    full_gate, full_up, full_down = (
        lax.all_gather(w_gate, "fsdp", axis=1, tiled=True),
        lax.all_gather(w_up, "fsdp", axis=1, tiled=True),
        lax.all_gather(w_down, "fsdp", axis=0, tiled=True),
    )
    gate = jnp.dot(x_mlp, full_gate, preferred_element_type=jnp.float32)
    upper = jnp.dot(x_mlp, full_up, preferred_element_type=jnp.float32)
    activ = (jax.nn.silu(gate) * upper).astype(jnp.bfloat16)
    mlp_out = jnp.dot(activ, full_down, preferred_element_type=jnp.float32)
    d_mlp = cotangent[0]
    d_activ = jnp.einsum("td,fd->tf", d_mlp, full_down, preferred_element_type=jnp.float32)
    sigmoid_gate = jax.nn.sigmoid(gate)
    d_gate = (d_activ * upper * sigmoid_gate * (1.0 + gate * (1.0 - sigmoid_gate))).astype(
        jnp.bfloat16
    )
    d_up = (d_activ * gate * sigmoid_gate).astype(jnp.bfloat16)
    d_x_mlp = jnp.einsum("tf,df->td", d_gate, full_gate, preferred_element_type=jnp.float32)
    d_x_mlp = d_x_mlp + jnp.einsum("tf,df->td", d_up, full_up, preferred_element_type=jnp.float32)
    grad_gate = jnp.einsum("td,tf->df", x_mlp, d_gate, preferred_element_type=jnp.float32)
    grad_up = jnp.einsum("td,tf->df", x_mlp, d_up, preferred_element_type=jnp.float32)
    grad_down = jnp.einsum("tf,td->fd", activ, d_mlp, preferred_element_type=jnp.float32)
    grad_gate, grad_up, grad_down = (
        lax.psum_scatter(
            grad_gate.astype(jnp.bfloat16), "fsdp", scatter_dimension=1, tiled=True
        ).astype(jnp.float32),
        lax.psum_scatter(
            grad_up.astype(jnp.bfloat16), "fsdp", scatter_dimension=1, tiled=True
        ).astype(jnp.float32),
        lax.psum_scatter(
            grad_down.astype(jnp.bfloat16), "fsdp", scatter_dimension=0, tiled=True
        ).astype(jnp.float32),
    )
    layer_out = (hidden + mlp_out).astype(jnp.bfloat16)
    d_norm_m, d_gain_m = norm_back(hidden, factor_m, gain_m, d_x_mlp)
    d_hidden = d_output + d_norm_m
    d_branch = d_hidden.astype(jnp.bfloat16)
    d_mix = jnp.einsum("td,ed->te", d_branch, full_out, preferred_element_type=jnp.float32).astype(
        jnp.bfloat16
    )
    grad_out = jnp.einsum("te,td->ed", attn_mix, d_branch, preferred_element_type=jnp.float32)

    def backward_group(items):
        return group_backward(items[0], items[1], items[2], items[3], items[4], allowed, scale)

    d_queries, d_keys, d_values = lax.map(
        backward_group, (grouped_q, grouped_k, grouped_v, log_total, query_groups(d_mix))
    )
    d_queries = d_queries.transpose(1, 0, 2, 3, 4).reshape(rows, HEADS, HEAD_DIM)
    d_keys = d_keys.transpose(1, 0, 2, 3).reshape(length, kv_width)
    d_values = d_values.transpose(1, 0, 2, 3).reshape(length, kv_width)
    d_k_own, d_v_own = (
        lax.psum_scatter(
            d_keys.astype(jnp.bfloat16), "ctx", scatter_dimension=0, tiled=True
        ).astype(jnp.float32),
        lax.psum_scatter(
            d_values.astype(jnp.bfloat16), "ctx", scatter_dimension=0, tiled=True
        ).astype(jnp.float32),
    )
    d_q_lin = rotate_back(d_queries, cosine, sine).reshape(rows, query_width).astype(jnp.bfloat16)
    d_k_lin = rotate_back(d_k_own.reshape(rows, KV_HEADS, HEAD_DIM), cosine, sine)
    d_k_lin = d_k_lin.reshape(rows, kv_width).astype(jnp.bfloat16)
    d_v_lin = d_v_own.astype(jnp.bfloat16)
    d_x_attn = jnp.einsum("te,de->td", d_q_lin, full_query, preferred_element_type=jnp.float32)
    d_x_attn = d_x_attn + jnp.einsum(
        "te,de->td", d_k_lin, full_key, preferred_element_type=jnp.float32
    )
    d_x_attn = d_x_attn + jnp.einsum(
        "te,de->td", d_v_lin, full_value, preferred_element_type=jnp.float32
    )
    grad_query = jnp.einsum("td,te->de", x_attn, d_q_lin, preferred_element_type=jnp.float32)
    grad_key = jnp.einsum("td,te->de", x_attn, d_k_lin, preferred_element_type=jnp.float32)
    grad_value = jnp.einsum("td,te->de", x_attn, d_v_lin, preferred_element_type=jnp.float32)
    d_norm_a, d_gain_a = norm_back(inputs, factor_a, gain_a, d_x_attn)
    d_inputs = d_hidden + d_norm_a
    shards = (
        lax.psum_scatter(
            d_gain_a.astype(jnp.bfloat16), "fsdp", scatter_dimension=0, tiled=True
        ).astype(jnp.float32),
        lax.psum_scatter(
            d_gain_m.astype(jnp.bfloat16), "fsdp", scatter_dimension=0, tiled=True
        ).astype(jnp.float32),
        lax.psum_scatter(
            grad_query.astype(jnp.bfloat16), "fsdp", scatter_dimension=0, tiled=True
        ).astype(jnp.float32),
        lax.psum_scatter(
            grad_key.astype(jnp.bfloat16), "fsdp", scatter_dimension=0, tiled=True
        ).astype(jnp.float32),
        lax.psum_scatter(
            grad_value.astype(jnp.bfloat16), "fsdp", scatter_dimension=0, tiled=True
        ).astype(jnp.float32),
        lax.psum_scatter(
            grad_out.astype(jnp.bfloat16), "fsdp", scatter_dimension=0, tiled=True
        ).astype(jnp.float32),
    )
    totals = (
        lax.psum(shards[0].astype(jnp.bfloat16), "ctx").astype(jnp.float32),
        lax.psum(shards[1].astype(jnp.bfloat16), "ctx").astype(jnp.float32),
        lax.psum(shards[2].astype(jnp.bfloat16), "ctx").astype(jnp.float32),
        lax.psum(shards[3].astype(jnp.bfloat16), "ctx").astype(jnp.float32),
        lax.psum(shards[4].astype(jnp.bfloat16), "ctx").astype(jnp.float32),
        lax.psum(shards[5].astype(jnp.bfloat16), "ctx").astype(jnp.float32),
        lax.psum(grad_gate.astype(jnp.bfloat16), "ctx").astype(jnp.float32),
        lax.psum(grad_up.astype(jnp.bfloat16), "ctx").astype(jnp.float32),
        lax.psum(grad_down.astype(jnp.bfloat16), "ctx").astype(jnp.float32),
    )
    return (
        layer_out[None],
        d_inputs[None],
        totals[0],
        totals[1],
        totals[2],
        totals[3],
        totals[4],
        totals[5],
        totals[6],
        totals[7],
        totals[8],
    )


def solution(mesh):
    return jax.shard_map(
        body,
        mesh=mesh,
        in_specs=(
            P("fsdp", "ctx", None),
            P(),
            P("fsdp"),
            P("fsdp"),
            P("fsdp", None),
            P("fsdp", None),
            P("fsdp", None),
            P("fsdp", None),
            P(None, "fsdp"),
            P(None, "fsdp"),
            P("fsdp", None),
            P("fsdp", "ctx", None),
        ),
        out_specs=(
            P("fsdp", "ctx", None),
            P("fsdp", "ctx", None),
            P("fsdp"),
            P("fsdp"),
            P("fsdp", None),
            P("fsdp", None),
            P("fsdp", None),
            P("fsdp", None),
            P(None, "fsdp"),
            P(None, "fsdp"),
            P("fsdp", None),
        ),
        check_vma=False,
    )
```

profile of v0, /device:TPU:32, one launch (start us, length us, event | category | flops | bytes accessed | tf_op | source)
XLA Modules:
  0.0 2410.6 jit_solution(5320763824543542704)
XLA Ops:
  10.1 5.1 all-gather
  17.0 25.8 %all-gather.12.cloned.1.call-done = bf16[1536,768]{1,0:T(8,128)(2,1)} async-done(((bf16[384,768]{1,0:T(8,128)(2,1)}), bf16[1536,768]{1,0:T(8,128)(2,1)}) %all-gather.12.cloned.1.call-update) | async-done | bytes 2359312 | tf_op jit(solution)/shard_map/all_gather | solution.py:123
  47.1 29.6 %all-gather.16.cloned.1.call-done = bf16[1536,768]{1,0:T(8,128)(2,1)} async-done(((bf16[384,768]{1,0:T(8,128)(2,1)}), bf16[1536,768]{1,0:T(8,128)(2,1)}) %all-gather.16.cloned.1.call-update) | async-done | bytes 2359312 | tf_op jit(solution)/shard_map/all_gather | solution.py:122
  76.6 4.3 copy.44
  87.3 5.2 all-gather.1
  92.5 37.1 %all-gather.20.cloned.1.call-done = bf16[1536,1536]{1,0:T(8,128)(2,1)} async-done(((bf16[384,1536]{1,0:T(8,128)(2,1)}), bf16[1536,1536]{1,0:T(8,128)(2,1)}) %all-gather.20.cloned.1.call-update) | async-done | bytes 4718608 | tf_op jit(solution)/shard_map/all_gather | solution.py:121
  129.7 6.6 copy.45
  136.3 3.8 fusion.97
  140.3 86.3 %all-gather.14.cloned.1.call-done = bf16[4096,768]{1,0:T(8,128)(2,1)} async-done(((bf16[128,768]{1,0:T(8,128)(2,1)}), bf16[4096,768]{1,0:T(8,128)(2,1)}) %all-gather.14.cloned.1.call-update) | async-done | bytes 6291472 | tf_op jit(solution)/shard_map/all_gather | solution.py:139
  226.6 8.6 copy.43
  235.2 102.4 %all-gather.18.cloned.1.call-done = bf16[4096,768]{0,1:T(8,128)(2,1)} async-done(((bf16[128,768]{0,1:T(8,128)(2,1)}), bf16[4096,768]{0,1:T(8,128)(2,1)}) %all-gather.18.cloned.1.call-update) | async-done | bytes 6291472 | tf_op jit(solution)/shard_map/all_gather | solution.py:138
  337.6 34.7 %while.30 = (s32[]{:T(128)}, bf16[4,128,2,2,96]{1,4,3,2,0:T(8,128)(2,1)S(1)}, f32[4,2,2,128]{3,2,1,0:T(2,128)S(1)}, bf16[4,4096,2,96]{1,3,2,0:T(8,128)(2,1)}, bf...) while((s32[]{:T(128)}, ...), condition=%wide.region_4.5_spmd.clone.clone, body=%wide.region_1.4_spmd.clone.sunk.clone | while | flops 825228800 | bytes 29707376 | solution.py:156
  372.4 16.2 all-gather.22.cloned.1.call-done
  392.0 114.4 %all-gather.24.cloned.1.call-done = bf16[1536,4096]{1,0:T(8,128)(2,1)} async-done(((bf16[1536,1024]{1,0:T(8,128)(2,1)}), bf16[1536,4096]{1,0:T(8,128)(2,1)}) %all-gather.24.cloned.1.call-update) | async-done | bytes 12582928 | tf_op jit(solution)/shard_map/all_gather | solution.py:162
  506.3 7.7 fusion.117
  514.0 111.1 %all-gather.26.cloned.1.call-done = bf16[1536,4096]{1,0:T(8,128)(2,1)} async-done(((bf16[1536,1024]{1,0:T(8,128)(2,1)}), bf16[1536,4096]{1,0:T(8,128)(2,1)}) %all-gather.26.cloned.1.call-update) | async-done | bytes 12582928 | tf_op jit(solution)/shard_map/all_gather | solution.py:163
  625.2 7.7 fusion.118
  632.8 111.1 %all-gather.28.cloned.1.call-done = bf16[4096,1536]{1,0:T(8,128)(2,1)} async-done(((bf16[1024,1536]{1,0:T(8,128)(2,1)}), bf16[4096,1536]{1,0:T(8,128)(2,1)}) %all-gather.28.cloned.1.call-update) | async-done | bytes 12582928 | tf_op jit(solution)/shard_map/all_gather | solution.py:164
  744.0 11.7 multiply_convert_fusion
  755.7 10.2 fusion.119
  765.9 6.8 multiply_reduce_fusion
  774.2 4.7 convolution_convert_fusion.7
  780.2 192.6 %while.31 = (s32[]{:T(128)}, f32[4,128,2,2,96]{1,4,3,2,0:T(8,128)}, bf16[4,4096,2,96]{1,3,2,0:T(8,128)(2,1)}, bf16[4,4096,2,96]{1,3,2,0:T(8,128)(2,1)}, bf16[4,4...) while((s32[]{:T(128)}, f32[4,128,2,2,96]{1,4,3,2,0:T(8,128)}, ...), condition=%wide.region_9.10_spmd.clone.clone, body=%wide.region_7.9_spmd.clone.sunk.clone | while | flops 2045780992 | bytes 104968328 | solution.py:205
  781.6 6.7 fusion.208
  788.3 6.0 fusion.209
  794.3 13.9 fusion.210
  808.2 14.3 fusion.211
  822.4 5.9 fusion.212
  829.7 6.7 fusion.208
  836.5 6.0 fusion.209
  842.4 13.9 fusion.210
  856.3 14.3 fusion.211
  870.6 5.9 fusion.212
  877.9 6.7 fusion.208
  884.6 6.0 fusion.209
  890.6 13.9 fusion.210
  904.5 14.3 fusion.211
  918.7 5.9 fusion.212
  926.0 6.7 fusion.208
  932.7 6.0 fusion.209
  938.7 13.9 fusion.210
  952.6 14.3 fusion.211
  966.9 5.9 fusion.212
  972.8 8.6 copy.57
  981.4 8.6 copy.59
  994.3 3.7 convolution_convert_fusion.4
  1001.6 212.2 %reduce-scatter.28.cloned.1.call-done = bf16[128,768]{1,0:T(8,128)(2,1)} async-done(((bf16[4096,768]{1,0:T(8,128)(2,1)}), bf16[128,768]{1,0:T(8,128)(2,1)}) %reduce-scatter.28.cloned.1.call-update) | async-done | bytes 196624
  1217.5 230.3 %reduce-scatter.30.cloned.1.call-done = bf16[128,768]{1,0:T(8,128)(2,1)} async-done(((bf16[4096,768]{1,0:T(8,128)(2,1)}), bf16[128,768]{1,0:T(8,128)(2,1)}) %reduce-scatter.30.cloned.1.call-update) | async-done | bytes 196624
  1451.0 7.9 convolution_convert_fusion.2
  1459.0 7.7 convolution_convert_fusion.1
  1467.7 7.8 convolution_convert_fusion
  1475.8 22.8 reduce-scatter.14.cloned.1.call-done
  1498.6 53.0 %reduce-scatter.20.cloned.1.call-done = bf16[384,1536]{1,0:T(8,128)(2,1)} async-done(((bf16[1536,1536]{1,0:T(8,128)(2,1)}), bf16[384,1536]{1,0:T(8,128)(2,1)}) %reduce-scatter.20.cloned.1.call-update) | async-done | bytes 1179664 | tf_op jit(solution)/shard_map/reduce_scatter | solution.py:251
  1551.6 34.2 %reduce-scatter.16.cloned.1.call-done = bf16[384,768]{1,0:T(8,128)(2,1)} async-done(((bf16[1536,768]{1,0:T(8,128)(2,1)}), bf16[384,768]{1,0:T(8,128)(2,1)}) %reduce-scatter.16.cloned.1.call-update) | async-done | bytes 589840 | tf_op jit(solution)/shard_map/reduce_scatter | solution.py:245
  1585.8 34.2 %reduce-scatter.18.cloned.1.call-done = bf16[384,768]{1,0:T(8,128)(2,1)} async-done(((bf16[1536,768]{1,0:T(8,128)(2,1)}), bf16[384,768]{1,0:T(8,128)(2,1)}) %reduce-scatter.18.cloned.1.call-update) | async-done | bytes 589840 | tf_op jit(solution)/shard_map/reduce_scatter | solution.py:248
  1619.9 116.3 %reduce-scatter.22.cloned.1.call-done = bf16[1536,1024]{1,0:T(8,128)(2,1)} async-done(((bf16[1536,4096]{1,0:T(8,128)(2,1)}), bf16[1536,1024]{1,0:T(8,128)(2,1)}) %reduce-scatter.22.cloned.1.call-update) | async-done | bytes 3145744 | tf_op jit(solution)/shard_map/reduce_scatter | solution.py:183
  1736.2 116.3 %reduce-scatter.24.cloned.1.call-done = bf16[1536,1024]{1,0:T(8,128)(2,1)} async-done(((bf16[1536,4096]{1,0:T(8,128)(2,1)}), bf16[1536,1024]{1,0:T(8,128)(2,1)}) %reduce-scatter.24.cloned.1.call-update) | async-done | bytes 3145744 | tf_op jit(solution)/shard_map/reduce_scatter | solution.py:186
  1852.6 116.3 %reduce-scatter.26.cloned.1.call-done = bf16[1024,1536]{1,0:T(8,128)(2,1)} async-done(((bf16[4096,1536]{1,0:T(8,128)(2,1)}), bf16[1024,1536]{1,0:T(8,128)(2,1)}) %reduce-scatter.26.cloned.1.call-update) | async-done | bytes 3145744 | tf_op jit(solution)/shard_map/reduce_scatter | solution.py:189
  1972.1 4.0 fusion.120
  1976.2 7.6 fusion.67
  1985.8 6.5 all-reduce.4
  1992.4 90.0 %all-reduce.2 = (bf16[384]{0:T(512)(128)(2,1)S(1)}, bf16[384]{0:T(512)(128)(2,1)S(1)}) all-reduce(bf16[384]{0:T(512)(128)(2,1)S(1)} %dynamic-slice.1, bf16[384]{0:T(512)(128)(2,1)S(1)} %dynamic-slice.3), channel_id=1, replica_groups=mesh['ctx'=32,'fsdp'=4] {'ctx'}, use_global_device_ids=true, to_apply=%region_15.16 | all-reduce | flops 768 | bytes 3072 | tf_op jit(solution)/shard_map/psum | solution.py:256
  2084.8 299.2 %all-reduce.7.cloned.1.call-done = (bf16[384,1536]{1,0:T(8,128)(2,1)}, bf16[384,768]{1,0:T(8,128)(2,1)}, bf16[384,768]{1,0:T(8,128)(2,1)}, bf16[384,1536]{1,0:T(...) async-done(((bf16[384,1536]{1,0:T(8,128)(2,1)}, bf16[384,768]{1,0:T(8,128)(2,1)}, bf16[384,768]{1,0:T(8,128)(2,1)}, ...) | async-done | bytes 12976144 | tf_op jit(solution)/shard_map/psum | solution.py:258
  2400.0 3.6 convert_element_type.260
  (179 shorter events, 100.4 us)
Async XLA Ops:
  7.2 73.7 %copy-start.1 = (bf16[1,128,1536]{2,1,0:T(8,128)(2,1)S(1)}, bf16[1,128,1536]{2,1,0:T(8,128)(2,1)}, u32[]{:S(2)}) copy-start(bf16[1,128,1536]{2,1,0:T(8,128)(2,1)} %param.16) | copy-start | bytes 1179652
  7.2 35.6 %all-gather.12.cloned.1.call-start = ((), (), s32[]{:S(2)}) async-start(), calls=%async_computation.9 | async-start | bytes 2949120 | tf_op jit(solution)/shard_map/all_gather | solution.py:123
  7.9 68.7 %all-gather.16.cloned.1.call-start = ((), (), s32[]{:S(2)}) async-start(), calls=%async_computation.11 | async-start | bytes 2949120 | tf_op jit(solution)/shard_map/all_gather | solution.py:122
  8.7 121.0 %all-gather.20.cloned.1.call-start = ((), (), s32[]{:S(2)}) async-start(), calls=%async_computation.13 | async-start | bytes 5898240 | tf_op jit(solution)/shard_map/all_gather | solution.py:121
  9.4 217.2 %all-gather.14.cloned.1.call-start = ((), (), s32[]{:S(2)}) async-start(), calls=%async_computation.10 | async-start | bytes 6488064 | tf_op jit(solution)/shard_map/all_gather | solution.py:139
  15.3 121.0 %copy-start.16 = (f32[1536]{0:T(1024)}, f32[1536]{0:T(1024)S(1)}, u32[]{:S(2)}) copy-start(f32[1536]{0:T(1024)S(1)} %reshape.340) | copy-start | bytes 18436
  17.0 119.3 %copy-start.19 = (f32[128]{0:T(128)}, f32[128]{0:T(128)S(1)}, u32[]{:S(2)}) copy-start(f32[128]{0:T(128)S(1)} %get-tuple-element.245) | copy-start | bytes 1540
  45.8 291.8 %all-gather.18.cloned.1.call-start = ((), (), s32[]{:S(2)}) async-start(), calls=%async_computation.12 | async-start | bytes 6488064 | tf_op jit(solution)/shard_map/all_gather | solution.py:138
  47.0 93.1 %copy-start.9 = (f32[128,96]{0,1:T(8,128)}, f32[128,96]{0,1:T(8,128)S(1)}, u32[]{:S(2)}) copy-start(f32[128,96]{0,1:T(8,128)S(1)} %get-tuple-element.242) | copy-start | bytes 147460
  47.0 93.1 %copy-start.13 = (f32[128,96]{0,1:T(8,128)}, f32[128,96]{0,1:T(8,128)S(1)}, u32[]{:S(2)}) copy-start(f32[128,96]{0,1:T(8,128)S(1)} %get-tuple-element.243) | copy-start | bytes 147460
  83.4 3.7 copy-start.23
  83.4 3.9 copy-start.21
  84.2 304.4 %all-gather.22.cloned.1.call-start = ((), (), s32[]{:S(2)}) async-start(), calls=%async_computation.14 | async-start | bytes 5898240 | tf_op jit(solution)/shard_map/all_gather | solution.py:124
  84.8 421.6 %all-gather.24.cloned.1.call-start = ((), (), s32[]{:S(2)}) async-start(), calls=%async_computation.15 | async-start | bytes 15728640 | tf_op jit(solution)/shard_map/all_gather | solution.py:162
  85.5 539.6 %all-gather.26.cloned.1.call-start = ((), (), s32[]{:S(2)}) async-start(), calls=%async_computation.16 | async-start | bytes 15728640 | tf_op jit(solution)/shard_map/all_gather | solution.py:163
  86.3 657.7 %all-gather.28.cloned.1.call-start = ((), (), s32[]{:S(2)}) async-start(), calls=%async_computation.17 | async-start | bytes 15728640 | tf_op jit(solution)/shard_map/all_gather | solution.py:164
  87.0 1126.8 %reduce-scatter.28.cloned.1.call-start = ((), (), s32[]{:S(2)}) async-start(), calls=%async_computation.25 | async-start | bytes 6488064
  372.4 16.2 copy-start.8
  514.0 229.9 %copy-start.11 = (bf16[1,128,1536]{2,1,0:T(8,128)(2,1)S(1)}, bf16[1,128,1536]{2,1,0:T(8,128)(2,1)}, u32[]{:S(2)}) copy-start(bf16[1,128,1536]{2,1,0:T(8,128)(2,1)} %param.27) | copy-start | bytes 1179652
  755.7 10.2 copy-start
  981.4 466.3 %reduce-scatter.30.cloned.1.call-start = ((), (), s32[]{:S(2)}) async-start(), calls=%async_computation.26 | async-start | bytes 6488064
  990.1 0.8 copy-start.14
  990.1 2.1 copy-start.10
  990.1 4.2 copy-start.17
  990.1 4.2 copy-start.20
  990.1 508.5 %reduce-scatter.14.cloned.1.call-start = ((), (), s32[]{:S(2)}) async-start(), calls=%async_computation.18 | async-start | bytes 5898240 | tf_op jit(solution)/shard_map/reduce_scatter | solution.py:242
  998.0 553.6 %reduce-scatter.20.cloned.1.call-start = ((), (), s32[]{:S(2)}) async-start(), calls=%async_computation.21 | async-start | bytes 5898240 | tf_op jit(solution)/shard_map/reduce_scatter | solution.py:251
  1001.6 584.2 %reduce-scatter.16.cloned.1.call-start = ((), (), s32[]{:S(2)}) async-start(), calls=%async_computation.19 | async-start | bytes 2949120 | tf_op jit(solution)/shard_map/reduce_scatter | solution.py:245
  1217.4 402.5 %reduce-scatter.18.cloned.1.call-start = ((), (), s32[]{:S(2)}) async-start(), calls=%async_computation.20 | async-start | bytes 2949120 | tf_op jit(solution)/shard_map/reduce_scatter | solution.py:248
  1451.0 285.3 %reduce-scatter.22.cloned.1.call-start = ((), (), s32[]{:S(2)}) async-start(), calls=%async_computation.22 | async-start | bytes 15728640 | tf_op jit(solution)/shard_map/reduce_scatter | solution.py:183
  1459.0 393.6 %reduce-scatter.24.cloned.1.call-start = ((), (), s32[]{:S(2)}) async-start(), calls=%async_computation.23 | async-start | bytes 15728640 | tf_op jit(solution)/shard_map/reduce_scatter | solution.py:186
  1466.7 1.0 copy-start.12
  1466.7 502.2 %reduce-scatter.26.cloned.1.call-start = ((), (), s32[]{:S(2)}) async-start(), calls=%async_computation.24 | async-start | bytes 15728640 | tf_op jit(solution)/shard_map/reduce_scatter | solution.py:189
  1475.5 908.5 %all-reduce.7.cloned.1.call-start = ((), (), s32[]{:S(2)}) async-start(), calls=%async_computation.27 | async-start | bytes 25952256 | tf_op jit(solution)/shard_map/psum | solution.py:258
  1968.9 0.7 copy-start.24
  1968.9 1.9 copy-start.4
  1976.2 7.6 copy-start.3
  1976.2 8.5 copy-start.2
  1976.2 8.5 copy-start.18
  1983.8 99.8 %copy-start.22 = (f32[128]{0:T(128)S(1)}, f32[128]{0:T(128)}, u32[]{:S(2)}) copy-start(f32[128]{0:T(128)} %get-tuple-element.244) | copy-start | bytes 1540
  2384.0 7.4 copy-start.15
  2384.0 9.1 copy-start.7
  2391.4 5.2 copy-start.6
  2396.6 3.5 copy-start.5
Sparse Core Ops, SparseCore 0:
  9.7 33.0 all-gather.11
  44.4 32.1 all-gather.15
  78.3 51.3 all-gather.19
  133.2 93.3 all-gather.13
  229.8 107.8 all-gather.17
  339.2 49.3 all-gather.21
  390.2 116.0 all-gather.23
  508.0 117.1 all-gather.25
  626.8 117.1 all-gather.27
  981.5 232.2 reduce-scatter.27
  1219.5 228.1 reduce-scatter.29
  1450.6 47.9 reduce-scatter.13
  1501.0 50.5 reduce-scatter.19
  1554.4 31.3 reduce-scatter.15
  1588.6 31.2 reduce-scatter.17
  1622.3 113.9 reduce-scatter.21
  1738.6 113.9 reduce-scatter.23
  1854.9 113.9 reduce-scatter.25
  1972.0 411.9 all-reduce.6
where the time goes:
time: 2420 us; the launch traced here: 2410 us
  waiting for transfers between devices  1870 us (77%)
  matrix products  322 us (13%)
  blocking collectives  107 us (4%)
  other arithmetic  48.2 us (2%)
  local copies, waits for them, and re-layouts  42.8 us (2%)
    unnamed x21, waiting for transfers between devices  447 us
    psum x1, waiting for transfers between devices, body(): lax.psum(shards[2].astype(jnp.bfloat16), 'ctx').astype(jnp.float32)  299 us
    reduce_scatter x1, waiting for transfers between devices, body(): lax.psum_scatter(grad_down.astype(jnp.bfloat16), 'fsdp', scatter_dimensio...  116 us
    reduce_scatter x1, waiting for transfers between devices, body(): lax.psum_scatter(grad_up.astype(jnp.bfloat16), 'fsdp', scatter_dimension=...  116 us
    reduce_scatter x1, waiting for transfers between devices, body(): lax.psum_scatter(grad_gate.astype(jnp.bfloat16), 'fsdp', scatter_dimensio...  116 us
    all_gather x1, waiting for transfers between devices, body(): lax.all_gather(w_gate, 'fsdp', axis=1, tiled=True)  114 us
    all_gather x1, waiting for transfers between devices, body(): lax.all_gather(w_down, 'fsdp', axis=0, tiled=True)  111 us
    all_gather x1, waiting for transfers between devices, body(): lax.all_gather(w_up, 'fsdp', axis=1, tiled=True)  111 us
  transfers between devices with their start and end apart: 19, of which 19 were waited for; matrix products, arithmetic and copies ran while one was open for 6% of the time, Pallas kernels for 0%

commit v1 on v0

v1 whole, which is shorter than its diff:
```python
import functools

import jax
import jax.numpy as jnp
from jax import lax
from jax.experimental import pallas as pl
from jax.experimental.pallas import tpu as pltpu
from jax.sharding import Mesh, PartitionSpec as P

D = 1536
HEADS = 16
KV_HEADS = 8
HEAD_DIM = 96
HALF = HEAD_DIM // 2
FF = 4096
BLOCK = 64
SEQ = 4096
WINDOW_BLOCKS = 32
SHARDS = 4
ROWS = 128
TOK = SHARDS * ROWS
DS = D // SHARDS
FS = FF // SHARDS
EPS = 1e-05
ROPE_BASE = 10000.0
MASKED = -1e30
SCALE = HEAD_DIM ** (-0.5)
LOG2E = 1.4426950408889634
BF = jnp.bfloat16
F32 = jnp.float32

CHUNK_BLOCKS = 8
CHUNK = CHUNK_BLOCKS * BLOCK

SMEM_SPEC = pl.BlockSpec(memory_space=pltpu.SMEM)
VMEM_SPEC = pl.BlockSpec(memory_space=pltpu.VMEM)


def params(mib):
    return pltpu.CompilerParams(vmem_limit_bytes=mib * 1024 * 1024)


def call(kernel, outs, n_smem, n_vmem, mib, scratch=(), flops=0, nbytes=0):
    return pl.pallas_call(
        kernel,
        out_shape=outs,
        in_specs=[SMEM_SPEC] * n_smem + [VMEM_SPEC] * n_vmem,
        out_specs=jax.tree.map(lambda _: VMEM_SPEC, outs),
        scratch_shapes=list(scratch),
        compiler_params=params(mib),
        cost_estimate=pl.CostEstimate(flops=flops, bytes_accessed=nbytes, transcendentals=0),
    )


def sds(shape, dtype=BF):
    return jax.ShapeDtypeStruct(shape, dtype)


def dot(a, b):
    return jnp.dot(a, b, preferred_element_type=F32)


def dot_t(a, b):
    return lax.dot_general(a, b, (((1,), (1,)), ((), ())), preferred_element_type=F32)


def t_dot(a, b):
    return lax.dot_general(a, b, (((0,), (0,)), ((), ())), preferred_element_type=F32)


def swap_c(x):
    return lax.ppermute(x, "c", [(0, 1), (1, 0)])


def swap_xl(x):
    return lax.ppermute(x, "xl", [(0, 1), (1, 0)])


def swap_both(x):
    return lax.ppermute(x, ("xl", "c"), [(i, i ^ 3) for i in range(4)])


def swap_far(x):
    pairs = []
    for xh in range(2):
        for xl in range(2):
            place = 2 * xh + xl
            other = (place + 1) % 4 if xl else (place + 3) % 4
            for c in range(2):
                pairs.append((place * 2 + c, other * 2 + 1 - c))
    return lax.ppermute(x, ("xh", "xl", "c"), pairs)


def swap_e(x):
    return lax.ppermute(x, "xh", [(0, 1), (1, 0)])


NEAR = [(0, 1), (1, 0), (2, 3), (3, 2)]
AROUND = [(1, 2), (2, 1), (0, 3), (3, 0)]
CUBE = (("y", NEAR), ("y", AROUND), ("z", NEAR), ("z", AROUND))


def swap_cube(x, dim):
    axis, pairs = CUBE[dim % 4]
    return lax.ppermute(x, axis, pairs)


def from_z(x, m):
    return lax.ppermute(x, "z", [((i + m) % 4, i) for i in range(4)])


def to_z(x, m):
    return lax.ppermute(x, "z", [(i, (i + m) % 4) for i in range(4)])


def gather_slots(own):
    far = swap_xl(own)
    return own, swap_c(own), far, swap_c(far)


def scatter_slots(keep, send):
    got = swap_c(send)
    pair = keep.astype(F32) + got.astype(F32)
    far = swap_xl(pair[1].astype(BF))
    return pair[0], far.astype(F32)


def cube_reduce(keeps, sends):
    keeps, sends = list(keeps), list(sends)
    for step in range(4):
        for p in range(4):
            got = swap_cube(sends[p], p + step)
            total = (keeps[p].astype(F32) + got.astype(F32)).astype(BF)
            half = total.shape[0] // 2
            keeps[p], sends[p] = (total[:half], total[half:]) if step < 3 else (total, None)
    return [(k.astype(F32) + swap_e(k).astype(F32)).astype(BF) for k in keeps]


def cube_gather(parts):
    owns, gots = list(parts), [None] * 4
    for step in (3, 2, 1, 0):
        for p in range(4):
            if gots[p] is not None:
                owns[p] = jnp.concatenate([owns[p], gots[p]], axis=0)
            gots[p] = swap_cube(owns[p], p + step)
    return owns, gots


def cube_index(portion, bits):
    out = 0
    for t in range(4):
        out = out * 2 + bits[(portion + t) % 4]
    return out


def pack_weights_kernel(sc, wq, wk, wv, o0, o1, o2, o3, tmp):
    f = sc[0]
    for g in range(4):
        tmp[g, :, 0:DS] = wq[:, DS * g : DS * (g + 1)]
        tmp[g, :, DS : DS + 192] = wk[:, 192 * g : 192 * (g + 1)]
        tmp[g, :, DS + 192 : 768] = wv[:, 192 * g : 192 * (g + 1)]
    for k, out in enumerate((o0, o1, o2, o3)):
        out[...] = tmp[f ^ k]


def qkv_kernel(sc, x0, x1, x2, x3, gain, w0, w1, w2, w3, cos, sin, xa, qkv):
    f = sc[0]
    for k, x in enumerate((x0, x1, x2, x3)):
        u = x[...].astype(F32)
        r = lax.rsqrt(jnp.mean(u * u, axis=-1, keepdims=True) + EPS)
        xa[ROWS * k : ROWS * (k + 1), :] = (u * r * gain[...]).astype(BF)
    lin = jnp.zeros((TOK, 768), F32)
    for k, w in enumerate((w0, w1, w2, w3)):
        at = pl.multiple_of((f ^ k) * DS, 128)
        lin = lin + dot(xa[:, pl.ds(at, DS)], w[...])
    co, si = cos[...], sin[...]
    for k in range(4):
        part = lin[ROWS * k : ROWS * (k + 1)]
        for j in range(2):
            for n, at in enumerate((192 * j, 192 * j + 96, DS + 96 * j)):
                u = part[:, at : at + HEAD_DIM]
                turned = jnp.concatenate([-u[:, HALF:], u[:, :HALF]], axis=1)
                qkv[2 * k + j, :, 96 * n : 96 * (n + 1)] = (u * co + turned * si).astype(BF)
            at = DS + 192 + 96 * j
            qkv[2 * k + j, :, 288:384] = part[:, at : at + 96].astype(BF)


def attention_kernel(qb, kb, qkv, kv1, kv2, kv3, o, lse, ks, vs):
    def place(b, _):
        src = pl.multiple_of(b * BLOCK, BLOCK)
        for m, ref in enumerate((qkv, kv1, kv2, kv3)):
            at = 192 if m == 0 else 0
            dst = pl.multiple_of(kb[m * 16 + b] * BLOCK, BLOCK)
            ks[pl.ds(dst, BLOCK), :] = ref[pl.ds(src, BLOCK), at : at + 96]
            vs[pl.ds(dst, BLOCK), :] = ref[pl.ds(src, BLOCK), at + 96 : at + 192]
        return 0

    lax.fori_loop(0, 16, place, 0)
    two = SCALE * LOG2E

    def one(n, _):
        i = qb[n]
        row = pl.multiple_of(n * BLOCK, BLOCK)
        q2 = jnp.concatenate(
            [qkv[pl.ds(row, BLOCK), 0:96], qkv[pl.ds(row, BLOCK), 96:192]], axis=0
        )
        first = jnp.maximum(i - (WINDOW_BLOCKS - 1), 0)

        def update(carry, s, v):
            top, total, acc = carry
            new = jnp.maximum(top, jnp.max(s, axis=1, keepdims=True))
            p = jnp.exp2((s - new) * two)
            back = jnp.exp2((top - new) * two)
            total = total * back + jnp.sum(p, axis=1, keepdims=True)
            return new, total, acc * back + dot(p.astype(BF), v)

        def chunk(t, carry):
            at = pl.multiple_of((first + t * CHUNK_BLOCKS) * BLOCK, BLOCK)
            s = dot_t(q2, ks[pl.ds(at, CHUNK), :])
            key = lax.broadcasted_iota(jnp.int32, s.shape, 1)
            s = jnp.where(key < (i + 1) * BLOCK - at, s, MASKED)
            return update(carry, s, vs[pl.ds(at, CHUNK), :])

        def edge(t, carry):
            at = pl.multiple_of((i - WINDOW_BLOCKS) * BLOCK, BLOCK)
            s = dot_t(q2, ks[pl.ds(at, BLOCK), :])
            key = lax.broadcasted_iota(jnp.int32, s.shape, 1)
            query = lax.broadcasted_iota(jnp.int32, s.shape, 0) % BLOCK
            s = jnp.where(key > query, s, MASKED)
            return update(carry, s, vs[pl.ds(at, BLOCK), :])

        carry = (
            jnp.full((ROWS, 1), MASKED, F32),
            jnp.zeros((ROWS, 1), F32),
            jnp.zeros((ROWS, HEAD_DIM), F32),
        )
        carry = lax.fori_loop(0, (i - first) // CHUNK_BLOCKS + 1, chunk, carry)
        carry = lax.fori_loop(0, jnp.where(i >= WINDOW_BLOCKS, 1, 0), edge, carry)
        top, total, acc = carry
        out = (acc / total).astype(BF)
        o[pl.ds(row, BLOCK), 0:96] = out[:BLOCK]
        o[pl.ds(row, BLOCK), 96:192] = out[BLOCK:]
        tall = jnp.broadcast_to(top * two + jnp.log2(total), (ROWS, ROWS))
        lse[n] = tall.T[0:8]
        return 0

    lax.fori_loop(0, 16, one, 0)


def attention_back_kernel(
    qb, kb, qkv, d_o, o, lse, ks, vs, dq, g0, g1, g2, g3, dks, dvs
):
    dks[...] = jnp.zeros_like(dks)
    dvs[...] = jnp.zeros_like(dvs)
    two = SCALE * LOG2E

    def one(n, _):
        i = qb[n]
        row = pl.multiple_of(n * BLOCK, BLOCK)
        rows = pl.ds(row, BLOCK)
        q2 = jnp.concatenate([qkv[rows, 0:96], qkv[rows, 96:192]], axis=0)
        do2 = jnp.concatenate([d_o[rows, 0:96], d_o[rows, 96:192]], axis=0)
        o2 = jnp.concatenate([o[rows, 0:96], o[rows, 96:192]], axis=0)
        inner = do2.astype(F32) * o2.astype(F32)
        inner = jnp.broadcast_to(jnp.sum(inner, axis=1, keepdims=True), (ROWS, ROWS)).T[0:1]
        top = lse[n, 0:1]
        first = jnp.maximum(i - (WINDOW_BLOCKS - 1), 0)

        def update(acc, at, size, allowed):
            span = pl.ds(at, size)
            k, v = ks[span, :], vs[span, :]
            s = dot_t(k, q2)
            p = jnp.where(allowed(s.shape), jnp.exp2(s * two - top), 0.0)
            ds = (p * (dot_t(v, do2) - inner)).astype(BF)
            dks[span, :] += dot(ds, q2)
            dvs[span, :] += dot(p.astype(BF), do2)
            return acc + t_dot(ds, k)

        def chunk(t, acc):
            at = pl.multiple_of((first + t * CHUNK_BLOCKS) * BLOCK, BLOCK)
            limit = (i + 1) * BLOCK - at
            return update(
                acc, at, CHUNK, lambda sh: lax.broadcasted_iota(jnp.int32, sh, 0) < limit
            )

        def edge(t, acc):
            at = pl.multiple_of((i - WINDOW_BLOCKS) * BLOCK, BLOCK)
            return update(
                acc,
                at,
                BLOCK,
                lambda sh: lax.broadcasted_iota(jnp.int32, sh, 0)
                > lax.broadcasted_iota(jnp.int32, sh, 1) % BLOCK,
            )

        acc = jnp.zeros((ROWS, HEAD_DIM), F32)
        acc = lax.fori_loop(0, (i - first) // CHUNK_BLOCKS + 1, chunk, acc)
        acc = lax.fori_loop(0, jnp.where(i >= WINDOW_BLOCKS, 1, 0), edge, acc)
        acc = (acc * SCALE).astype(BF)
        dq[rows, 0:96] = acc[:BLOCK]
        dq[rows, 96:192] = acc[BLOCK:]
        return 0

    lax.fori_loop(0, 16, one, 0)

    def place(b, _):
        dst = pl.ds(pl.multiple_of(b * BLOCK, BLOCK), BLOCK)
        for m, ref in enumerate((g0, g1, g2, g3)):
            src = pl.ds(pl.multiple_of(kb[m * 16 + b] * BLOCK, BLOCK), BLOCK)
            ref[dst, 0:96] = (dks[src, :] * SCALE).astype(BF)
            ref[dst, 96:192] = dvs[src, :].astype(BF)
        return 0

    lax.fori_loop(0, 16, place, 0)


def out_kernel(o, w, keep, send):
    for k in range(4):
        total = dot(o[2 * k], w[0:192, :]) + dot(o[2 * k + 1], w[192:384, :])
        (keep, send)[k % 2][k // 2] = total.astype(BF)


def d_o_kernel(b0, b1, b2, b3, w, d_o):
    for k, b in enumerate((b0, b1, b2, b3)):
        d = dot_t(b[...], w[...]).astype(BF)
        d_o[2 * k] = d[:, 0:192]
        d_o[2 * k + 1] = d[:, 192:384]


FBLOCK = 256


def ffn_kernel(sc, x0, x1, x2, x3, y0, y1, y2, y3, wg, wu, wd, act, dg, du, keep, send, xs, ys, acc):
    n = pl.program_id(0)

    @pl.when(n == 0)
    def _():
        for k, (x, y) in enumerate(zip((x0, x1, x2, x3), (y0, y1, y2, y3))):
            xs[ROWS * k : ROWS * (k + 1), :] = x[...]
            ys[ROWS * k : ROWS * (k + 1), :] = y[...]

    gate = dot(xs[...], wg[...])
    up = dot(xs[...], wu[...])
    da = dot_t(ys[...], wd[...])
    sg = jax.nn.sigmoid(gate)
    act[...] = (gate * sg * up).astype(BF)
    d_gate = (da * up * sg * (1.0 + gate * (1.0 - sg))).astype(BF)
    d_up = (da * gate * sg).astype(BF)
    dg[...] = d_gate
    du[...] = d_up
    dx = dot_t(d_gate, wg[...]) + dot_t(d_up, wu[...])

    @pl.when(n == 0)
    def _():
        acc[...] = dx

    @pl.when(n > 0)
    def _():
        acc[...] += dx

    @pl.when(n == FS // FBLOCK - 1)
    def _():
        for k in range(4):
            (keep, send)[k % 2][k // 2] = acc[ROWS * k : ROWS * (k + 1), :].astype(BF)


def ffn(sc, xs, ys, wg, wu, wd):
    full = pl.BlockSpec((ROWS, D), lambda n, s: (0, 0))
    side = pl.BlockSpec((2, ROWS, D), lambda n, s: (0, 0, 0))
    cols = pl.BlockSpec((D, FBLOCK), lambda n, s: (0, n))
    rel = pl.BlockSpec((TOK, FBLOCK), lambda n, s: (0, n ^ s[2]))
    return pl.pallas_call(
        ffn_kernel,
        grid_spec=pltpu.PrefetchScalarGridSpec(
            num_scalar_prefetch=1,
            grid=(FS // FBLOCK,),
            in_specs=[full] * 8 + [cols, cols, pl.BlockSpec((FBLOCK, D), lambda n, s: (n, 0))],
            out_specs=[rel, rel, rel, side, side],
            scratch_shapes=[
                pltpu.VMEM((TOK, D), BF),
                pltpu.VMEM((TOK, D), BF),
                pltpu.VMEM((TOK, D), F32),
            ],
        ),
        out_shape=[sds((TOK, FS))] * 3 + [sds((2, ROWS, D))] * 2,
        compiler_params=params(44),
        cost_estimate=pl.CostEstimate(
            flops=2 * TOK * D * FS * 5, bytes_accessed=16_000_000, transcendentals=0
        ),
    )(sc, *xs, *ys, wg, wu, wd)


def mlp_out_kernel(sc, act, wd, keep, send):
    gz = sc[2]
    for k in range(4):
        total = jnp.zeros((ROWS, D), F32)
        for b in range(FS // FBLOCK):
            at = pl.multiple_of((b ^ gz) * FBLOCK, FBLOCK)
            total += dot(
                act[ROWS * k : ROWS * (k + 1), pl.ds(at, FBLOCK)],
                wd[FBLOCK * b : FBLOCK * (b + 1), :],
            )
        (keep, send)[k % 2][k // 2] = total.astype(BF)


def ffn_grads_kernel(sc, x0, x1, x2, x3, y0, y1, y2, y3, act, dg, du, *outs):
    gy = sc[1]
    keeps, sends = outs[:4], outs[4:8]

    def put(p, ra, rb, at, tile):
        index = cube_index(p, (ra & 1, ra >> 1, rb & 1, rb >> 1))
        ref = (keeps, sends)[index >> 3][p]
        ref[index & 7, at : at + tile.shape[0], :] = tile.astype(BF)

    for ra in range(4):
        cols = pl.ds(pl.multiple_of((ra ^ gy) * DS, 128), DS)
        xa = jnp.concatenate([x[:, cols] for x in (x0, x1, x2, x3)], axis=0)
        ya = jnp.concatenate([y[:, cols] for y in (y0, y1, y2, y3)], axis=0)
        for n, d in enumerate((dg, du)):
            for rb in range(4):
                tile = t_dot(xa, d[:, 256 * rb : 256 * (rb + 1)])
                for p in range(4):
                    lane, row = 128 * (p // 2), 192 * (p % 2)
                    put(p, ra, rb, 192 * n, tile[row : row + 192, lane : lane + 128])
        for rb in range(4):
            tile = t_dot(act[:, 256 * rb : 256 * (rb + 1)], ya)
            for p in range(4):
                at = 384
                row = 192 * p
                while row < 192 * (p + 1):
                    lane, r = row // 256, row % 256
                    size = min(256 - r, 192 * (p + 1) - row)
                    put(p, ra, rb, at, tile[r : r + size, 128 * lane : 128 * (lane + 1)])
                    at += size
                    row += size


def pick(owns, gots, p, bits, rows):
    index = cube_index(p, bits)
    rest = index & 7
    return jnp.where(index >= 8, gots[p][rest, rows, :], owns[p][rest, rows, :])


def ffn_place_kernel(sc, *refs):
    owns, gots = refs[0:4], refs[4:8]
    wg, wu, gate, up, down, gain = refs[8:]
    gy, gz = sc[1], sc[2]
    ra = pl.program_id(0) ^ gy
    for bb in range(4):
        rb = bb ^ gz
        bits = (ra & 1, ra >> 1, rb & 1, rb >> 1)
        for p in range(4):
            lane, row = 256 * bb + 128 * (p // 2), 192 * (p % 2)
            for n, ref in enumerate((gate, up)):
                tile = pick(owns, gots, p, bits, slice(192 * n, 192 * (n + 1)))
                ref[row : row + 192, lane : lane + 128] = tile.astype(F32)
            at, row = 384, 192 * p
            while row < 192 * (p + 1):
                lane, r = row // 256, row % 256
                size = min(256 - r, 192 * (p + 1) - row)
                tile = pick(owns, gots, p, bits, slice(at, at + size))
                down[256 * bb + r : 256 * bb + r + size, 128 * lane : 128 * (lane + 1)] = (
                    tile.astype(F32)
                )
                at += size
                row += size
    prod = wg[...].astype(F32) * gate[...] + wu[...].astype(F32) * up[...]
    gain[...] = jnp.sum(prod, axis=1, keepdims=True)


def ffn_place(sc, owns, gots, wg, wu):
    whole = pl.BlockSpec((8, 576, 128), lambda n, s: (0, 0, 0))
    rows = pl.BlockSpec((DS, FS), lambda n, s: (n, 0))
    return pl.pallas_call(
        ffn_place_kernel,
        grid_spec=pltpu.PrefetchScalarGridSpec(
            num_scalar_prefetch=1,
            grid=(4,),
            in_specs=[whole] * 8 + [rows, rows],
            out_specs=[
                rows,
                rows,
                pl.BlockSpec((FS, DS), lambda n, s: (0, n)),
                pl.BlockSpec((DS, 1), lambda n, s: (n, 0)),
            ],
        ),
        out_shape=[sds((D, FS), F32), sds((D, FS), F32), sds((FS, D), F32), sds((D, 1), F32)],
        compiler_params=params(56),
        cost_estimate=pl.CostEstimate(flops=0, bytes_accessed=35_000_000, transcendentals=0),
    )(sc, *owns, *gots, wg, wu)


OUT_ROWS = (80, 80, 64, 64)
OUT_AT = (0, 80, 160, 224)
QKV_ROWS = 144


def d_xa_kernel(sc, d, w0, w1, w2, w3, cos, sin, lin, keep, send, dq, dk, dv):
    f = sc[0]
    co, si = cos[...], sin[...]
    for k in range(4):
        rows = slice(ROWS * k, ROWS * (k + 1))
        for j in range(2):
            for n in range(3):
                g = d[2 * k + j, :, 96 * n : 96 * (n + 1)].astype(F32)
                w = g * si
                turned = jnp.concatenate([w[:, HALF:], -w[:, :HALF]], axis=1)
                g = (g * co + turned).astype(BF)
                lin[rows, 384 * j + 96 * n : 384 * j + 96 * (n + 1)] = g
                if n < 2:
                    dq[rows, 192 * j + 96 * n : 192 * j + 96 * (n + 1)] = g
                else:
                    dk[rows, 96 * j : 96 * (j + 1)] = g
            g = d[2 * k + j, :, 288:384]
            lin[rows, 384 * j + 288 : 384 * j + 384] = g
            dv[rows, 96 * j : 96 * (j + 1)] = g
    for k, w in enumerate((w0, w1, w2, w3)):
        cols = pl.ds(pl.multiple_of((f ^ k) * DS, 128), DS)
        total = dot_t(dq[...], w[:, 0:DS])
        total += dot_t(dk[...], w[:, DS : DS + 192])
        total += dot_t(dv[...], w[:, DS + 192 : 768])
        total = total.astype(BF)
        for s in range(4):
            (keep, send)[s % 2][s // 2, :, cols] = total[ROWS * s : ROWS * (s + 1)]


def attn_grads_kernel(sc, xa, lin, o, b0, b1, b2, b3, *refs):
    keeps, sends, tmp = refs[:4], refs[4:8], refs[8]
    f, gy, gz = sc[0], sc[1], sc[2]
    near = gy | ((gz & 1) << 2)
    side = gz >> 1

    def put(p, bits, at, tile):
        index = cube_index(p, bits)
        ref = (keeps, sends)[index >> 3][p]
        ref[index & 7, at : at + tile.shape[0], :] = tile.astype(BF)

    for p in range(4):
        cols = pl.ds(pl.multiple_of((f ^ p) * DS, 128), DS)
        tmp[:, 0:768] = t_dot(xa[:, cols], lin[...])
        for r in range(8):
            row = pl.multiple_of((r ^ near) * 48, 48)
            for c in range(2):
                at = pl.multiple_of((c ^ side) * DS, 128)
                for t in range(3):
                    tile = tmp[pl.ds(row, 48), pl.ds(pl.multiple_of(at + 128 * t, 128), 128)]
                    put(p, (r & 1, (r >> 1) & 1, r >> 2, c), 48 * t, tile)
    bs = jnp.concatenate([b0[...], b1[...], b2[...], b3[...]], axis=0)
    for j in range(2):
        oj = jnp.concatenate([o[2 * k + j] for k in range(4)], axis=0)
        tmp[192 * j : 192 * (j + 1), :] = t_dot(oj, bs)
    for ra in range(4):
        row = pl.multiple_of((ra ^ gy) * 96, 96)
        for rb in range(4):
            at = pl.multiple_of((rb ^ gz) * DS, 128)
            bits = (ra & 1, ra >> 1, rb & 1, rb >> 1)
            for p in range(4):
                start, put_at = OUT_AT[p], QKV_ROWS
                while start < OUT_AT[p] + OUT_ROWS[p]:
                    t, r = start // 96, start % 96
                    size = min(96 - r, OUT_AT[p] + OUT_ROWS[p] - start)
                    tile = tmp[
                        pl.ds(pl.multiple_of(row + r, 16), size),
                        pl.ds(pl.multiple_of(at + 128 * t, 128), 128),
                    ]
                    put(p, bits, put_at, tile)
                    put_at += size
                    start += size


def attn_place_kernel(sc, *refs):
    owns, gots = refs[0:4], refs[4:8]
    wq, wk, wv, gain_in, q, k, v, out, gain, tmp = refs[8:]
    f, gy, gz = sc[0], sc[1], sc[2]
    near = gy | ((gz & 1) << 2)
    side = gz >> 1
    for p in range(4):
        for rr in range(8):
            r = rr ^ near
            for cc in range(2):
                c = cc ^ side
                bits = (r & 1, (r >> 1) & 1, r >> 2, c)
                tile = pick(owns, gots, p, bits, slice(0, QKV_ROWS)).astype(F32)
                for t in range(3):
                    lane = 384 * cc + 128 * t
                    tmp[f ^ p, 48 * rr : 48 * (rr + 1), lane : lane + 128] = tile[
                        48 * t : 48 * (t + 1)
                    ]
    for g in range(4):
        for j in range(2):
            q[:, 384 * g + 192 * j : 384 * g + 192 * (j + 1)] = tmp[g, :, 384 * j : 384 * j + 192]
            k[:, 192 * g + 96 * j : 192 * g + 96 * (j + 1)] = tmp[
                g, :, 384 * j + 192 : 384 * j + 288
            ]
            v[:, 192 * g + 96 * j : 192 * g + 96 * (j + 1)] = tmp[
                g, :, 384 * j + 288 : 384 * j + 384
            ]
    total = jnp.sum(wq[...].astype(F32) * q[...], axis=1, keepdims=True)
    total += jnp.sum(wk[...].astype(F32) * k[...], axis=1, keepdims=True)
    total += jnp.sum(wv[...].astype(F32) * v[...], axis=1, keepdims=True)
    gain[...] = total / gain_in[...]
    for aa in range(4):
        ra = aa ^ gy
        for bb in range(4):
            rb = bb ^ gz
            bits = (ra & 1, ra >> 1, rb & 1, rb >> 1)
            for p in range(4):
                start, at = OUT_AT[p], QKV_ROWS
                while start < OUT_AT[p] + OUT_ROWS[p]:
                    t, r = start // 96, start % 96
                    size = min(96 - r, OUT_AT[p] + OUT_ROWS[p] - start)
                    tile = pick(owns, gots, p, bits, slice(at, at + size))
                    lane = 384 * bb + 128 * t
                    out[96 * aa + r : 96 * aa + r + size, lane : lane + 128] = tile.astype(F32)
                    at += size
                    start += size


def rope_tables(positions):
    freqs = ROPE_BASE ** (-jnp.arange(HALF).astype(F32) * 2.0 / HEAD_DIM)
    angles = positions.astype(F32)[:, None] * freqs[None, :]
    angles = jnp.concatenate([angles, angles], axis=1)
    return jnp.cos(angles), jnp.sin(angles)


def norm_factor(values):
    return lax.rsqrt(jnp.mean(values * values, axis=-1, keepdims=True) + EPS)


def norm_back(values, factor, gain, grads):
    weighted = grads * gain
    inner = jnp.mean(weighted * values, axis=-1, keepdims=True)
    return factor * weighted - values * (factor * factor * factor) * inner


def exchange(x):
    shape = x.shape
    x = x.reshape(-1, shape[-1])
    return lax.all_to_all(x, ("y", "xh"), 0, 0, tiled=True).reshape(shape)


def body(
    tokens,
    block_order,
    gain_attn,
    gain_mlp,
    w_query,
    w_key,
    w_value,
    w_out,
    w_gate,
    w_up,
    w_down,
    cotangent,
):
    y, xh, z = lax.axis_index("y"), lax.axis_index("xh"), lax.axis_index("z")
    xl, c = lax.axis_index("xl"), lax.axis_index("c")
    f = xl * 2 + c
    gy, gz = y ^ (y >> 1), z ^ (z >> 1)
    sc = jnp.stack([f, gy, gz, xh]).astype(jnp.int32)
    own_x, own_dy = tokens[0], cotangent[0]

    blocks = block_order.reshape(8, 4, 2)
    place = (y * 2 + xh) * 4 + z
    own_blocks = lax.dynamic_slice_in_dim(block_order, 2 * place, 2)
    positions = (own_blocks[:, None] * BLOCK + jnp.arange(BLOCK)).reshape(-1)
    cos, sin = rope_tables(positions)
    key_blocks = jnp.stack(
        [
            lax.dynamic_index_in_dim(blocks, (z + m) % 4, axis=1, keepdims=False).reshape(-1)
            for m in range(4)
        ]
    ).reshape(-1)
    query_blocks = key_blocks[:16]

    xs = gather_slots(own_x)
    gains = jnp.stack(gather_slots(jnp.stack([gain_attn, gain_mlp])))
    gains = jnp.where(c == 0, gains, gains[jnp.array([1, 0, 3, 2])])
    gains = jnp.where(xl == 0, gains, gains[jnp.array([2, 3, 0, 1])])
    gains = gains.transpose(1, 0, 2).reshape(2, 1, D).astype(F32)
    gain_a, gain_m = gains[0], gains[1]
    packs = call(
        pack_weights_kernel,
        [sds((DS, 768))] * 4,
        1,
        3,
        16,
        [pltpu.VMEM((4, DS, 768), BF)],
        0,
        5_000_000,
    )(sc, w_query, w_key, w_value)
    ws = (packs[0], swap_c(packs[1]), swap_xl(packs[2]), swap_far(packs[3]))

    xa, qkv = call(
        qkv_kernel,
        [sds((TOK, D)), sds((8, ROWS, 384))],
        1,
        11,
        32,
        (),
        2 * TOK * D * 768,
        6_000_000,
    )(sc, *xs, gain_a, *ws, cos, sin)

    qkv = exchange(qkv).reshape(8 * ROWS, 384)
    kv = qkv[:, 192:]
    kvs = [from_z(kv, m) for m in (1, 2, 3)]
    o, lse, ks, vs = call(
        attention_kernel,
        [sds((1024, 192)), sds((16, 8, ROWS), F32), sds((SEQ, 96)), sds((SEQ, 96))],
        2,
        4,
        32,
        (),
        2 * 1024 * 2 * 1600 * 96 * 2,
        5_000_000,
    )(query_blocks, key_blocks, qkv, *kvs)
    o_tok = exchange(o.reshape(8, ROWS, 192))

    keep, send = call(
        out_kernel, [sds((2, ROWS, D))] * 2, 0, 2, 16, (), 2 * TOK * D * DS, 3_000_000
    )(o_tok, w_out)
    near, far = scatter_slots(keep, send)
    x32 = own_x.astype(F32)
    hidden = x32 + near + far
    factor_m = norm_factor(hidden)
    xm = (hidden * factor_m * gain_m).astype(BF)
    xms = gather_slots(xm)
    dys = gather_slots(own_dy)
    act, dg, du, keep, send = ffn(sc, xms, dys, w_gate, w_up, w_down)
    near, far = scatter_slots(keep, send)
    d_xm = near + far
    d_hidden = own_dy.astype(F32) + norm_back(hidden, factor_m, gain_m, d_xm)
    d_br = d_hidden.astype(BF)
    d_brs = gather_slots(d_br)

    grads = call(
        ffn_grads_kernel,
        [sds((8, 576, 128))] * 8,
        1,
        11,
        44,
        (),
        2 * TOK * D * FS * 3,
        16_000_000,
    )(sc, *xms, *dys, act, dg, du)
    parts = cube_reduce(grads[:4], grads[4:])
    owns, gots = cube_gather(parts)
    g_gate, g_up, g_down, g_gain_m = ffn_place(sc, owns, gots, w_gate, w_up)
    g_gain_m = g_gain_m.reshape(4, 384)
    g_gain_m = [lax.dynamic_index_in_dim(g_gain_m, f ^ k, keepdims=False) for k in range(4)]
    g_gain_m = (
        g_gain_m[0] + swap_c(g_gain_m[1]) + swap_xl(g_gain_m[2]) + swap_both(g_gain_m[3])
    ) / gain_mlp.astype(F32)

    keep, send = call(
        mlp_out_kernel, [sds((2, ROWS, D))] * 2, 1, 2, 24, (), 2 * TOK * D * FS, 6_000_000
    )(sc, act, w_down)
    near, far = scatter_slots(keep, send)
    layer_out = (hidden + near + far).astype(BF)

    d_o = call(
        d_o_kernel, sds((8, ROWS, 192)), 0, 5, 16, (), 2 * TOK * D * DS, 4_000_000
    )(*d_brs, w_out)
    d_o = exchange(d_o).reshape(1024, 192)
    dq, g0, g1, g2, g3 = call(
        attention_back_kernel,
        [sds((1024, 192))] * 5,
        2,
        6,
        44,
        [pltpu.VMEM((SEQ, 96), F32), pltpu.VMEM((SEQ, 96), F32)],
        2 * 1024 * 2 * 1600 * 96 * 5,
        8_000_000,
    )(query_blocks, key_blocks, qkv, d_o, o, lse, ks, vs)
    d_kv = g0.astype(F32)
    for m, g in ((1, g1), (2, g2), (3, g3)):
        d_kv = d_kv + to_z(g, m).astype(F32)
    d_qkv = jnp.concatenate([dq, d_kv.astype(BF)], axis=1)
    d_qkv = exchange(d_qkv.reshape(8, ROWS, 384))

    lin, keep, send = call(
        d_xa_kernel,
        [sds((TOK, 768)), sds((2, ROWS, D)), sds((2, ROWS, D))],
        1,
        7,
        32,
        [pltpu.VMEM((TOK, DS), BF), pltpu.VMEM((TOK, 192), BF), pltpu.VMEM((TOK, 192), BF)],
        2 * TOK * D * 768,
        6_000_000,
    )(sc, d_qkv, *ws, cos, sin)
    near, far = scatter_slots(keep, send)
    d_xa = near + far
    factor_a = norm_factor(x32)
    d_tokens = d_hidden + norm_back(x32, factor_a, gain_a, d_xa)

    shapes = [sds((8, QKV_ROWS + n, 128)) for n in OUT_ROWS]
    grads = call(
        attn_grads_kernel,
        shapes + shapes,
        1,
        7,
        32,
        [pltpu.VMEM((DS, D), F32)],
        2 * TOK * D * (768 + DS),
        10_000_000,
    )(sc, xa, lin, o_tok, *d_brs)
    parts = cube_reduce(grads[:4], grads[4:])
    moved = [parts[0]]
    for p, swap in ((1, swap_c), (2, swap_xl), (3, swap_both)):
        got = swap(parts[p][:, :QKV_ROWS])
        moved.append(jnp.concatenate([got, parts[p][:, QKV_ROWS:]], axis=1))
    owns, gots = cube_gather(moved)
    g_query, g_key, g_value, g_out, g_gain_a = call(
        attn_place_kernel,
        [
            sds((DS, D), F32),
            sds((DS, 768), F32),
            sds((DS, 768), F32),
            sds((DS, D), F32),
            sds((DS, 1), F32),
        ],
        1,
        12,
        40,
        [pltpu.VMEM((4, DS, 768), F32)],
        0,
        16_000_000,
    )(sc, *owns, *gots, w_query, w_key, w_value, gain_attn.astype(F32).reshape(DS, 1))

    return (
        layer_out[None],
        d_tokens[None],
        g_gain_a.reshape(DS),
        g_gain_m.reshape(DS),
        g_query,
        g_key,
        g_value,
        g_out,
        g_gate,
        g_up,
        g_down,
    )


def solution(mesh):
    cube = Mesh(mesh.devices.reshape(4, 2, 4, 2, 2), ("y", "xh", "z", "xl", "c"))
    fsdp, ctx = ("xl", "c"), ("y", "xh", "z")
    return jax.shard_map(
        body,
        mesh=cube,
        in_specs=(
            P(fsdp, ctx, None),
            P(),
            P(fsdp),
            P(fsdp),
            P(fsdp, None),
            P(fsdp, None),
            P(fsdp, None),
            P(fsdp, None),
            P(None, fsdp),
            P(None, fsdp),
            P(fsdp, None),
            P(fsdp, ctx, None),
        ),
        out_specs=(
            P(fsdp, ctx, None),
            P(fsdp, ctx, None),
            P(fsdp),
            P(fsdp),
            P(fsdp, None),
            P(fsdp, None),
            P(fsdp, None),
            P(fsdp, None),
            P(None, fsdp),
            P(None, fsdp),
            P(fsdp, None),
        ),
        check_vma=False,
    )
```

time: 2420 us -> 614 us (0.25)
  waiting for transfers between devices: 1870 us -> 203 us
  matrix products: 322 us -> 0 us
  starting transfers between devices: 1.23 us -> 148 us
  Pallas kernels: 0 us -> 133 us
  blocking collectives: 107 us -> 33.1 us
    all_gather x9 -> x0, waiting for transfers between devices: 634 us -> none  [the longest x1 114 us: body(): lax.all_gather(w_gate, 'fsdp', axis=1, tiled=True)]
    reduce_scatter x7 -> x0, waiting for transfers between devices: 493 us -> none  [the longest x1 116 us: body(): lax.psum_scatter(grad_down.astype(jnp.bfloat16), 'fsdp', scatter_dimensio...]
    unnamed x21 -> x0, waiting for transfers between devices: 447 us -> none
    dot_general x49 -> x0, matrix products: 322 us -> none  [the longest x4 57.1 us: group_backward(): jnp.einsum('jrtl,tjrd->ljd', d_raw, queries, preferred_element_type=jnp.f...]
    psum x1 -> x0, waiting for transfers between devices: 299 us -> none  [body(): lax.psum(shards[2].astype(jnp.bfloat16), 'ctx').astype(jnp.float32)]
    ppermute x0 -> x110, waiting for transfers between devices: none -> 203 us  [the longest x64 119 us: swap_cube(): return lax.ppermute(x, axis, pairs)]
    ppermute x0 -> x110, starting transfers between devices: none -> 138 us  [the longest x64 91.8 us: swap_cube(): return lax.ppermute(x, axis, pairs)]
    pallas_call x0 -> x13, Pallas kernels: none -> 133 us  [the longest x1 34.5 us: body(): call(attention_back_kernel, [sds((1024, 192))] * 5, 2, 6, 44, [pltpu.VMEM...]
  transfers between devices with their start and end apart: 19 -> 112, of which waited for: 19 -> 43; matrix products, arithmetic and copies ran while one was open for 6% -> 10% of each run, Pallas kernels for 0% -> 12%
where the time goes in v1:
time: 614 us; the launch traced here: 602 us
  waiting for transfers between devices  203 us (33%)
  starting transfers between devices  148 us (24%)
  Pallas kernels  133 us (22%)
  other arithmetic  49.8 us (8%)
  blocking collectives  33.1 us (5%)
  local copies, waits for them, and re-layouts  32.6 us (5%)
    ppermute x64, waiting for transfers between devices, swap_cube(): return lax.ppermute(x, axis, pairs)  119 us
    ppermute x64, starting transfers between devices, swap_cube(): return lax.ppermute(x, axis, pairs)  91.8 us
    ppermute x12, waiting for transfers between devices, swap_xl(): return lax.ppermute(x, 'xl', [(0, 1), (1, 0)])  52.1 us
    pallas_call x1, Pallas kernels, body(): call(attention_back_kernel, [sds((1024, 192))] * 5, 2, 6, 44, [pltpu.VMEM...  34.5 us
    all_to_all x2, blocking collectives, exchange(): return lax.all_to_all(x, ('y', 'xh'), 0, 0, tiled=True).reshape(shape)  33.1 us
    pallas_call x1, Pallas kernels, body(): call(attention_kernel, [sds((1024, 192)), sds((16, 8, ROWS), F32), sds((S...  30.6 us
    concatenate x24, other arithmetic, cube_gather(): owns[p] = jnp.concatenate([owns[p], gots[p]], axis=0)  20.9 us
    pallas_call x1, Pallas kernels, ffn(): pl.pallas_call(ffn_kernel, grid_spec=pltpu.PrefetchScalarGridSpec(num_sca...  20 us
  transfers between devices with their start and end apart: 112, of which 43 were waited for; matrix products, arithmetic and copies ran while one was open for 10% of the time, Pallas kernels for 12%

profile of v1, /device:TPU:32, one launch (start us, length us, event | category | flops | bytes accessed | tf_op | source)
XLA Modules:
  0.0 602.0 jit_solution(11421884403755500097)
XLA Ops:
  18.0 10.7 %collective-permute-done.7.w2 = bf16[384,768]{1,0:T(8,128)(2,1)S(1)} collective-permute-done((bf16[384,768]{1,0:T(8,128)(2,1)}, bf16[384,768]{1,0:T(8,128)(2,1)S(1)}, u32[]{:S(2)}, u32[]{:S(2)}) %collective-permute-start.7) | collective-permute-done | bytes 589856 | tf_op jit(solution)/shard_map/ppermute | solution.py:76
  30.7 5.4 shard_map.222
  36.2 20.0 %all_to_all.34 = bf16[8,128,384]{2,1,0:T(8,128)(2,1)S(1)} all-to-all(bf16[8,128,384]{2,1,0:T(8,128)(2,1)S(1)} %get-tuple-element.67), channel_id=1, replica_groups=mesh['y'=4,'xh'=2,'z'=4,'xl'=2,'c'=2] {'y','xh'}, dimensions={0} | all-to-all | bytes 1572864 | tf_op jit(solution)/shard_map/all_to_all | solution.py:639
  56.7 3.3 collective-permute-start.10
  60.0 2.2 collective-permute-start.11
  64.1 6.4 %collective-permute-done.9.kv1 = bf16[1024,192]{1,0:T(8,128)(2,1)S(1)} collective-permute-done((bf16[1024,192]{1,0:T(8,128)(2,1)S(1)}, bf16[1024,192]{1,0:T(8,128)(2,1)S(1)}, u32[]{:S(2)}, u32[]{:S(2)}) %collective-permute-start.9) | collective-permute-done | bytes 393248 | tf_op jit(solution)/shard_map/ppermute | solution.py:109
  70.5 11.2 %collective-permute-done.10.kv2 = bf16[1024,192]{1,0:T(8,128)(2,1)S(1)} collective-permute-done((bf16[1024,192]{1,0:T(8,128)(2,1)S(1)}, bf16[1024,192]{1,0:T(8,128)(2,1)S(1)}, u32[]{:S(2)}, u32[]{:S(2)}) %collective-permute-start.10) | collective-permute-done | bytes 393248 | tf_op jit(solution)/shard_map/ppermute | solution.py:109
  82.5 30.6 %shard_map.223 = (bf16[1024,192]{1,0:T(8,128)(2,1)S(1)}, f32[16,8,128]{2,1,0:T(8,128)S(1)}, bf16[4096,96]{1,0:T(8,128)(2,1)S(1)}, bf16[4096,96]{1,0:T(8,128)(2,1)S(1)}) custom-call(s32[16]{0:T(128)S(1)} %slice.205.qb, s32[64]{0:T(128)S(1)} %reshape.147.kb, bf16[1024,384]{1,0:T(8,128)(2,1)S(1)} %bitcast.78, bf16[1024,192]{1,0:T(8,128)(2,1)S(1)} %collective-permute-done.9.kv1, ...), custom_call_target="tpu_custom_call" | custom-call | flops 1258291200 | bytes 5000000 | tf_op jit(solution)/shard_map/pallas_call | solution.py:708
  116.1 13.0 %all_to_all.35 = bf16[8,128,192]{1,2,0:T(8,128)(2,1)S(1)} all-to-all(bf16[8,128,192]{1,2,0:T(8,128)(2,1)} %copy.29), channel_id=1, replica_groups=mesh['y'=4,'xh'=2,'z'=4,'xl'=2,'c'=2] {'y','xh'}, dimensions={0} | all-to-all | bytes 786432 | tf_op jit(solution)/shard_map/all_to_all | solution.py:639
  132.2 2.3 collective-permute-done.12
  140.1 9.9 %collective-permute-done.13 = bf16[128,1536]{1,0:T(8,128)(2,1)S(1)} collective-permute-done((bf16[128,1536]{1,0:T(8,128)(2,1)}, bf16[128,1536]{1,0:T(8,128)(2,1)S(1)}, u32[]{:S(2)}, u32[]{:S(2)}) %collective-permute-start.13) | collective-permute-done | bytes 393248 | tf_op jit(solution)/shard_map/ppermute | solution.py:76
  153.3 5.1 collective-permute-done.18.y2
  158.9 7.1 %collective-permute-done.15.x2 = bf16[128,1536]{1,0:T(8,128)(2,1)S(1)} collective-permute-done((bf16[128,1536]{1,0:T(8,128)(2,1)S(1)}, bf16[128,1536]{1,0:T(8,128)(2,1)S(1)}, u32[]{:S(2)}, u32[]{:S(2)}) %collective-permute-start.15) | collective-permute-done | bytes 393248 | tf_op jit(solution)/shard_map/ppermute | solution.py:76
  167.7 20.0 %shard_map.225 = (bf16[512,1024]{1,0:T(8,128)(2,1)S(1)}, bf16[512,1024]{1,0:T(8,128)(2,1)S(1)}, bf16[512,1024]{1,0:T(8,128)(2,1)S(1)}, bf16[2,128,1536]{2,1,0:T(8,128)(2,1)S(1)}, bf16[2,128,1536]{2,1,0:T(8,128)(2,1)S(1)}) custom-call(s32[4]{0:T(128)S(1)} %pad_add_fusion.1.sc, bf16[128,1536]{1,0:T(8,128)(2,1)S(1)} %multiply_convert_fusion.x0, ...), custom_call_target="tpu_custom_call" | custom-call | flops 8053063680 | bytes 16000000 | tf_op jit(solution)/shard_map/pallas_call | solution.py:372
  188.0 2.4 shard_map.226
  191.4 9.2 %shard_map.232 = (bf16[8,576,128]{2,1,0:T(8,128)(2,1)S(1)}, bf16[8,576,128]{2,1,0:T(8,128)(2,1)S(1)}, bf16[8,576,128]{2,1,0:T(8,128)(2,1)S(1)}, bf16[8,576,128]{...) custom-call(s32[4]{0:T(128)S(1)} %pad_add_fusion.1.sc, ...), custom_call_target="tpu_custom_call" | custom-call | flops 4831838208 | bytes 16000000 | tf_op jit(solution)/shard_map/pallas_call | solution.py:737
  202.3 4.0 collective-permute-start.87
  210.9 7.2 %collective-permute-done.23 = bf16[128,1536]{1,0:T(8,128)(2,1)S(1)} collective-permute-done((bf16[128,1536]{1,0:T(8,128)(2,1)S(1)}, bf16[128,1536]{1,0:T(8,128)(2,1)S(1)}, u32[]{:S(2)}, u32[]{:S(2)}) %collective-permute-start.23) | collective-permute-done | bytes 393248 | tf_op jit(solution)/shard_map/ppermute | solution.py:76
  220.1 7.5 %collective-permute-done.21 = bf16[128,1536]{1,0:T(8,128)(2,1)S(1)} collective-permute-done((bf16[128,1536]{1,0:T(8,128)(2,1)S(1)}, bf16[128,1536]{1,0:T(8,128)(2,1)S(1)}, u32[]{:S(2)}, u32[]{:S(2)}) %collective-permute-start.21) | collective-permute-done | bytes 393248 | tf_op jit(solution)/shard_map/ppermute | solution.py:76
  227.6 2.4 fusion.25
  238.4 3.1 collective-permute-done.25.b2
  242.1 6.6 %collective-permute-done.72 = bf16[4,576,128]{2,1,0:T(8,128)(2,1)S(1)} collective-permute-done((bf16[4,576,128]{2,1,0:T(8,128)(2,1)S(1)}, bf16[4,576,128]{2,1,0:T(8,128)(2,1)S(1)}, u32[]{:S(2)}, u32[]{:S(2)}) %collective-permute-start.72) | collective-permute-done | bytes 589856 | tf_op jit(solution)/shard_map/ppermute | solution.py:105
  258.0 2.2 collective-permute-start.97
  264.3 4.2 all-to-all-start.2
  281.2 3.0 collective-permute-start.75
  286.1 3.0 collective-permute-start.91
  294.0 34.5 %shard_map.228 = (bf16[1024,192]{1,0:T(8,128)(2,1)S(1)}, bf16[1024,192]{1,0:T(8,128)(2,1)S(1)}, bf16[1024,192]{1,0:T(8,128)(2,1)S(1)}, bf16[1024,192]{1,0:T(8,128)(2,1)S(1)}, bf16[1024,192]{1,0:T(8,128)(2,1)S(1)}) custom-call(s32[16]{0:T(128)S(1)} %slice.205.qb, s32[64]{0:T(128)S(1)} %reshape.147.kb, bf16[1024,384]{1,0:T(8,128)(2,1)S(1)} %bitcast.79, ...), custom_call_target="tpu_custom_call" | custom-call | flops 3145728000 | bytes 8000000 | tf_op jit(solution)/shard_map/pallas_call | solution.py:766
  330.4 2.2 collective-permute-start.27
  338.4 15.0 %collective-permute-done.76 = bf16[1,576,128]{2,1,0:T(8,128)(2,1)S(1)} collective-permute-done((bf16[1,576,128]{2,1,0:T(8,128)(2,1)S(1)}, bf16[1,576,128]{2,1,0:T(8,128)(2,1)S(1)}, u32[]{:S(2)}, u32[]{:S(2)}) %collective-permute-start.76) | collective-permute-done | bytes 147488 | tf_op jit(solution)/shard_map/ppermute | solution.py:105
  354.6 2.5 collective-permute-start.100
  357.9 2.5 collective-permute-done.92
  363.9 4.5 collective-permute-done.77
  371.7 5.9 all-to-all-start.3
  378.3 3.2 collective-permute-start.101
  384.8 2.5 collective-permute-start.94
  387.3 11.8 %collective-permute-done.101 = bf16[2,576,128]{2,1,0:T(8,128)(2,1)} collective-permute-done((bf16[2,576,128]{2,1,0:T(8,128)(2,1)}, bf16[2,576,128]{2,1,0:T(8,128)(2,1)}, u32[]{:S(2)}, u32[]{:S(2)}) %collective-permute-start.101) | collective-permute-done | bytes 294944 | tf_op jit(solution)/shard_map/ppermute | solution.py:105
  401.2 2.2 pad_maximum_fusion.refs_0_
  409.7 4.4 shard_map.229
  415.2 3.5 shard_map.230
  421.2 3.0 collective-permute-start.58
  427.9 2.8 collective-permute-done.58
  432.9 16.2 %collective-permute-done.32 = bf16[8,224,128]{2,1,0:T(8,128)(2,1)S(1)} collective-permute-done((bf16[8,224,128]{2,1,0:T(8,128)(2,1)S(1)}, bf16[8,224,128]{2,1,0:T(8,128)(2,1)S(1)}, u32[]{:S(2)}, u32[]{:S(2)}) %collective-permute-start.32) | collective-permute-done | bytes 458784 | tf_op jit(solution)/shard_map/ppermute | solution.py:105
  449.1 2.5 collective-permute-start.50
  451.7 4.2 collective-permute-done.40
  457.6 5.2 collective-permute-done.59
  465.1 4.3 collective-permute-done.41
  472.9 2.5 collective-permute-done.60
  475.4 2.7 collective-permute-start.42
  480.5 3.4 collective-permute-done.52
  488.2 3.0 collective-permute-start.53
  493.9 3.1 collective-permute-done.62
  498.8 2.2 collective-permute-start.36
  504.7 2.5 collective-permute-start.64
  511.5 3.0 collective-permute-start.105
  518.2 4.5 collective-permute-done.65
  522.7 2.9 collective-permute-start.38
  525.6 17.1 %collective-permute-done.38 = bf16[2,224,128]{2,1,0:T(8,128)(2,1)S(1)} collective-permute-done((bf16[2,224,128]{2,1,0:T(8,128)(2,1)S(1)}, bf16[2,224,128]{2,1,0:T(8,128)(2,1)S(1)}, u32[]{:S(2)}, u32[]{:S(2)}) %collective-permute-start.38) | collective-permute-done | bytes 114720 | tf_op jit(solution)/shard_map/ppermute | solution.py:105
  544.0 3.5 collective-permute-done.47
  555.4 3.6 collective-permute-start.48
  558.9 13.1 %shard_map.233 = (f32[1536,1024]{1,0:T(8,128)}, f32[1536,1024]{1,0:T(8,128)}, f32[1024,1536]{1,0:T(8,128)}, f32[1536,1]{1,0:T(8,128)}) custom-call(s32[4]{0:T(128)} %copy-done.18, bf16[8,576,128]{2,1,0:T(8,128)(2,1)} %pad_maximum_fusion.refs_0_, bf16[8,576,128]{2,1,0:T(8,128)(2,1)} %copy-done.37, bf16[8,576,128]{2,1,0:T(8,128)(2,1)} %copy-done.38, ...), custom_call_target="tpu_custom_call" | custom-call | bytes 35000000 | tf_op jit(solution)/shard_map/pallas_call | solution.py:474
  585.9 3.8 collective-permute-done.69.refs_6_
  590.8 2.3 collective-permute-done.67.refs_4_
  593.1 2.2 collective-permute-done.68.refs_5_
  595.4 5.7 shard_map.231
  (486 shorter events, 183.6 us)
Async XLA Ops:
  0.6 17.3 %collective-permute-start = (bf16[128,1536]{1,0:T(8,128)(2,1)}, bf16[128,1536]{1,0:T(8,128)(2,1)}, u32[]{:S(2)}, u32[]{:S(2)}) collective-permute-start(bf16[128,1536]{1,0:T(8,128)(2,1)} %bitcast.74), channel_id=1, source_target_pairs={{0,1},{1,0},{2,3},{3,2},{4,5},{5,4},{6,7},{7,6},{8,9},{9,8},{10,11... | collective-permute-start | bytes 1179656 | tf_op jit(solution)/shard_map/ppermute | solution.py:72
  0.7 16.8 %collective-permute-start.1 = (bf16[128,1536]{1,0:T(8,128)(2,1)}, bf16[128,1536]{1,0:T(8,128)(2,1)}, u32[]{:S(2)}, u32[]{:S(2)}) collective-permute-start(bf16[128,1536]{1,0:T(8,128)(2,1)} %bitcast.75), channel_id=1, source_target_pairs={{0,2},{2,0},{1,3},{3,1},{4,6},{6,4},{5,7},{7,5},{8,10},{10,8},{9,1... | collective-permute-start | bytes 1179656 | tf_op jit(solution)/shard_map/ppermute | solution.py:76
  12.6 16.0 %collective-permute-start.7 = (bf16[384,768]{1,0:T(8,128)(2,1)}, bf16[384,768]{1,0:T(8,128)(2,1)S(1)}, u32[]{:S(2)}, u32[]{:S(2)}) collective-permute-start(bf16[384,768]{1,0:T(8,128)(2,1)} %get-tuple-element.65), channel_id=1, source_target_pairs={{0,2},{2,0},{1,3},{3,1},{4,6},{6,4},{5,7},{7,5},{8,10},{10,8},{9,1... | collective-permute-start | bytes 1769480 | tf_op jit(solution)/shard_map/ppermute | solution.py:76
  14.2 16.5 %collective-permute-start.8 = (bf16[384,768]{1,0:T(8,128)(2,1)S(1)}, bf16[384,768]{1,0:T(8,128)(2,1)S(1)}, u32[]{:S(2)}, u32[]{:S(2)}) collective-permute-start(bf16[384,768]{1,0:T(8,128)(2,1)S(1)} %get-tuple-element.66), channel_id=1, source_target_pairs={{0,19},{1,18},{2,17},{3,16},{16,3},{17,2},{18,1},{19,0},{4,23},{5,... | collective-permute-start | bytes 1769480 | tf_op jit(solution)/shard_map/ppermute | solution.py:91
  17.5 13.2 %collective-permute-start.2 = (bf16[128,1536]{1,0:T(8,128)(2,1)}, bf16[128,1536]{1,0:T(8,128)(2,1)S(1)}, u32[]{:S(2)}, u32[]{:S(2)}) collective-permute-start(bf16[128,1536]{1,0:T(8,128)(2,1)} %collective-permute-done.1.x2), channel_id=1, source_target_pairs={{0,1},{1,0},{2,3},{3,2},{4,5},{5,4},{6,7},{7,6},{8,9},{9,8},{10,11... | collective-permute-start | bytes 1179656 | tf_op jit(solution)/shard_map/ppermute | solution.py:72
  56.5 13.9 %collective-permute-start.9 = (bf16[1024,192]{1,0:T(8,128)(2,1)S(1)}, bf16[1024,192]{1,0:T(8,128)(2,1)S(1)}, u32[]{:S(2)}, u32[]{:S(2)}) collective-permute-start(bf16[1024,192]{1,0:T(8,128)(2,1)S(1)} %slice.276), channel_id=1, source_target_pairs={{4,0},{8,4},{12,8},{0,12},{5,1},{9,5},{13,9},{1,13},{6,2},{10,6},{... | collective-permute-start | bytes 1179656 | tf_op jit(solution)/shard_map/ppermute | solution.py:109
  56.7 25.0 %collective-permute-start.10 = (bf16[1024,192]{1,0:T(8,128)(2,1)S(1)}, bf16[1024,192]{1,0:T(8,128)(2,1)S(1)}, u32[]{:S(2)}, u32[]{:S(2)}) collective-permute-start(bf16[1024,192]{1,0:T(8,128)(2,1)S(1)} %slice.276), channel_id=1, source_target_pairs={{8,0},{12,4},{0,8},{4,12},{9,1},{13,5},{1,9},{5,13},{10,2},{14,6},... | collective-permute-start | bytes 1179656 | tf_op jit(solution)/shard_map/ppermute | solution.py:109
  60.0 22.5 %collective-permute-start.11 = (bf16[1024,192]{1,0:T(8,128)(2,1)S(1)}, bf16[1024,192]{1,0:T(8,128)(2,1)S(1)}, u32[]{:S(2)}, u32[]{:S(2)}) collective-permute-start(bf16[1024,192]{1,0:T(8,128)(2,1)S(1)} %slice.276), channel_id=1, source_target_pairs={{12,0},{0,4},{4,8},{8,12},{13,1},{1,5},{5,9},{9,13},{14,2},{2,6},{... | collective-permute-start | bytes 1179656 | tf_op jit(solution)/shard_map/ppermute | solution.py:109
  137.8 12.2 %collective-permute-start.13 = (bf16[128,1536]{1,0:T(8,128)(2,1)}, bf16[128,1536]{1,0:T(8,128)(2,1)S(1)}, u32[]{:S(2)}, u32[]{:S(2)}) collective-permute-start(bf16[128,1536]{1,0:T(8,128)(2,1)} %fusion.14), channel_id=1, source_target_pairs={{0,2},{2,0},{1,3},{3,1},{4,6},{6,4},{5,7},{7,5},{8,10},{10,8},{9,1... | collective-permute-start | bytes 1179656 | tf_op jit(solution)/shard_map/ppermute | solution.py:76
  139.5 18.9 %collective-permute-start.18 = (bf16[128,1536]{1,0:T(8,128)(2,1)}, bf16[128,1536]{1,0:T(8,128)(2,1)S(1)}, u32[]{:S(2)}, u32[]{:S(2)}) collective-permute-start(bf16[128,1536]{1,0:T(8,128)(2,1)} %bitcast.15.y0), channel_id=1, source_target_pairs={{0,2},{2,0},{1,3},{3,1},{4,6},{6,4},{5,7},{7,5},{8,10},{10,8},{9,1... | collective-permute-start | bytes 1179656 | tf_op jit(solution)/shard_map/ppermute | solution.py:76
  151.5 14.5 %collective-permute-start.15 = (bf16[128,1536]{1,0:T(8,128)(2,1)S(1)}, bf16[128,1536]{1,0:T(8,128)(2,1)S(1)}, u32[]{:S(2)}, u32[]{:S(2)}) collective-permute-start(bf16[128,1536]{1,0:T(8,128)(2,1)S(1)} %multiply_convert_fusion.x0), channel_id=1, source_target_pairs={{0,2},{2,0},{1,3},{3,1},{4,6},{6,4},{5,7},{7,5},{8,10},{10,8},{9,1... | collective-permute-start | bytes 1179656 | tf_op jit(solution)/shard_map/ppermute | solution.py:76
  153.3 12.7 %collective-permute-start.17 = (bf16[128,1536]{1,0:T(8,128)(2,1)}, bf16[128,1536]{1,0:T(8,128)(2,1)S(1)}, u32[]{:S(2)}, u32[]{:S(2)}) collective-permute-start(bf16[128,1536]{1,0:T(8,128)(2,1)} %bitcast.15.y0), channel_id=1, source_target_pairs={{0,1},{1,0},{2,3},{3,2},{4,5},{5,4},{6,7},{7,6},{8,9},{9,8},{10,11... | collective-permute-start | bytes 1179656 | tf_op jit(solution)/shard_map/ppermute | solution.py:72
  187.8 18.5 %collective-permute-start.22 = (bf16[2,128,1536]{2,1,0:T(8,128)(2,1)S(1)}, bf16[2,128,1536]{2,1,0:T(8,128)(2,1)}, u32[]{:S(2)}, u32[]{:S(2)}) collective-permute-start(bf16[2,128,1536]{2,1,0:T(8,128)(2,1)S(1)} %get-tuple-element.75), channel_id=1, source_target_pairs={{0,1},{1,0},{2,3},{3,2},{4,5},{5,4},{6,7},{7,6},{8,9},{9,8},{10,11... | collective-permute-start | bytes 2359304 | tf_op jit(solution)/shard_map/ppermute | solution.py:72
  190.4 17.4 %collective-permute-start.20 = (bf16[2,128,1536]{2,1,0:T(8,128)(2,1)S(1)}, bf16[2,128,1536]{2,1,0:T(8,128)(2,1)}, u32[]{:S(2)}, u32[]{:S(2)}) collective-permute-start(bf16[2,128,1536]{2,1,0:T(8,128)(2,1)S(1)} %get-tuple-element.73), channel_id=1, source_target_pairs={{0,1},{1,0},{2,3},{3,2},{4,5},{5,4},{6,7},{7,6},{8,9},{9,8},{10,11... | collective-permute-start | bytes 2359304 | tf_op jit(solution)/shard_map/ppermute | solution.py:72
  200.6 29.4 %collective-permute-start.71 = (bf16[8,576,128]{2,1,0:T(8,128)(2,1)}, bf16[8,576,128]{2,1,0:T(8,128)(2,1)S(1)}, u32[]{:S(2)}, u32[]{:S(2)}) collective-permute-start(bf16[8,576,128]{2,1,0:T(8,128)(2,1)} %get-tuple-element.100), channel_id=1, source_target_pairs={{0,32},{32,0},{64,96},{96,64},{1,33},{33,1},{65,97},{97,65},{2,34}... | collective-permute-start | bytes 3538952 | tf_op jit(solution)/shard_map/ppermute | solution.py:105
  201.0 31.1 %collective-permute-start.79 = (bf16[8,576,128]{2,1,0:T(8,128)(2,1)}, bf16[8,576,128]{2,1,0:T(8,128)(2,1)S(1)}, u32[]{:S(2)}, u32[]{:S(2)}) collective-permute-start(bf16[8,576,128]{2,1,0:T(8,128)(2,1)} %get-tuple-element.102), channel_id=1, source_target_pairs={{32,64},{64,32},{0,96},{96,0},{33,65},{65,33},{1,97},{97,1},{34,66... | collective-permute-start | bytes 3538952 | tf_op jit(solution)/shard_map/ppermute | solution.py:105
  202.3 32.1 %collective-permute-start.87 = (bf16[8,576,128]{2,1,0:T(8,128)(2,1)}, bf16[8,576,128]{2,1,0:T(8,128)(2,1)S(1)}, u32[]{:S(2)}, u32[]{:S(2)}) collective-permute-start(bf16[8,576,128]{2,1,0:T(8,128)(2,1)} %get-tuple-element.104), channel_id=1, source_target_pairs={{0,4},{4,0},{8,12},{12,8},{1,5},{5,1},{9,13},{13,9},{2,6},{6,2},{1... | collective-permute-start | bytes 3538952 | tf_op jit(solution)/shard_map/ppermute | solution.py:105
  206.4 30.4 %collective-permute-start.95 = (bf16[8,576,128]{2,1,0:T(8,128)(2,1)}, bf16[8,576,128]{2,1,0:T(8,128)(2,1)S(1)}, u32[]{:S(2)}, u32[]{:S(2)}) collective-permute-start(bf16[8,576,128]{2,1,0:T(8,128)(2,1)} %get-tuple-element.106), channel_id=1, source_target_pairs={{4,8},{8,4},{0,12},{12,0},{5,9},{9,5},{1,13},{13,1},{6,10},{10,6},... | collective-permute-start | bytes 3538952 | tf_op jit(solution)/shard_map/ppermute | solution.py:105
  229.9 28.1 %collective-permute-start.24 = (bf16[128,1536]{1,0:T(8,128)(2,1)S(1)}, bf16[128,1536]{1,0:T(8,128)(2,1)S(1)}, u32[]{:S(2)}, u32[]{:S(2)}) collective-permute-start(bf16[128,1536]{1,0:T(8,128)(2,1)S(1)} %get-tuple-element.126.b0), channel_id=1, source_target_pairs={{0,1},{1,0},{2,3},{3,2},{4,5},{5,4},{6,7},{7,6},{8,9},{9,8},{10,11... | collective-permute-start | bytes 1179656 | tf_op jit(solution)/shard_map/ppermute | solution.py:72
  232.1 16.7 %collective-permute-start.72 = (bf16[4,576,128]{2,1,0:T(8,128)(2,1)S(1)}, bf16[4,576,128]{2,1,0:T(8,128)(2,1)S(1)}, u32[]{:S(2)}, u32[]{:S(2)}) collective-permute-start(bf16[4,576,128]{2,1,0:T(8,128)(2,1)S(1)} %slice.317), channel_id=1, source_target_pairs={{32,64},{64,32},{0,96},{96,0},{33,65},{65,33},{1,97},{97,1},{34,66... | collective-permute-start | bytes 1769480 | tf_op jit(solution)/shard_map/ppermute | solution.py:105
  234.4 15.3 %collective-permute-start.80 = (bf16[4,576,128]{2,1,0:T(8,128)(2,1)S(1)}, bf16[4,576,128]{2,1,0:T(8,128)(2,1)S(1)}, u32[]{:S(2)}, u32[]{:S(2)}) collective-permute-start(bf16[4,576,128]{2,1,0:T(8,128)(2,1)S(1)} %slice.323), channel_id=1, source_target_pairs={{0,4},{4,0},{8,12},{12,8},{1,5},{5,1},{9,13},{13,9},{2,6},{6,2},{1... | collective-permute-start | bytes 1769480 | tf_op jit(solution)/shard_map/ppermute | solution.py:105
  236.8 15.6 %collective-permute-start.88 = (bf16[4,576,128]{2,1,0:T(8,128)(2,1)S(1)}, bf16[4,576,128]{2,1,0:T(8,128)(2,1)S(1)}, u32[]{:S(2)}, u32[]{:S(2)}) collective-permute-start(bf16[4,576,128]{2,1,0:T(8,128)(2,1)S(1)} %slice.329), channel_id=1, source_target_pairs={{4,8},{8,4},{0,12},{12,0},{5,9},{9,5},{1,13},{13,1},{6,10},{10,6},... | collective-permute-start | bytes 1769480 | tf_op jit(solution)/shard_map/ppermute | solution.py:105
  241.5 14.9 %collective-permute-start.96 = (bf16[4,576,128]{2,1,0:T(8,128)(2,1)S(1)}, bf16[4,576,128]{2,1,0:T(8,128)(2,1)S(1)}, u32[]{:S(2)}, u32[]{:S(2)}) collective-permute-start(bf16[4,576,128]{2,1,0:T(8,128)(2,1)S(1)} %slice.335), channel_id=1, source_target_pairs={{0,32},{32,0},{64,96},{96,64},{1,33},{33,1},{65,97},{97,65},{2,34}... | collective-permute-start | bytes 1769480 | tf_op jit(solution)/shard_map/ppermute | solution.py:105
  249.8 18.8 %collective-permute-start.73 = (bf16[2,576,128]{2,1,0:T(8,128)(2,1)}, bf16[2,576,128]{2,1,0:T(8,128)(2,1)}, u32[]{:S(2)}, u32[]{:S(2)}) collective-permute-start(bf16[2,576,128]{2,1,0:T(8,128)(2,1)} %slice.319), channel_id=1, source_target_pairs={{0,4},{4,0},{8,12},{12,8},{1,5},{5,1},{9,13},{13,9},{2,6},{6,2},{1... | collective-permute-start | bytes 884744 | tf_op jit(solution)/shard_map/ppermute | solution.py:105
  252.4 18.9 %collective-permute-start.81 = (bf16[2,576,128]{2,1,0:T(8,128)(2,1)}, bf16[2,576,128]{2,1,0:T(8,128)(2,1)}, u32[]{:S(2)}, u32[]{:S(2)}) collective-permute-start(bf16[2,576,128]{2,1,0:T(8,128)(2,1)} %slice.325), channel_id=1, source_target_pairs={{4,8},{8,4},{0,12},{12,0},{5,9},{9,5},{1,13},{13,1},{6,10},{10,6},... | collective-permute-start | bytes 884744 | tf_op jit(solution)/shard_map/ppermute | solution.py:105
  256.4 18.0 %collective-permute-start.89 = (bf16[2,576,128]{2,1,0:T(8,128)(2,1)}, bf16[2,576,128]{2,1,0:T(8,128)(2,1)}, u32[]{:S(2)}, u32[]{:S(2)}) collective-permute-start(bf16[2,576,128]{2,1,0:T(8,128)(2,1)} %slice.331), channel_id=1, source_target_pairs={{0,32},{32,0},{64,96},{96,64},{1,33},{33,1},{65,97},{97,65},{2,34}... | collective-permute-start | bytes 884744 | tf_op jit(solution)/shard_map/ppermute | solution.py:105
  258.0 19.5 %collective-permute-start.97 = (bf16[2,576,128]{2,1,0:T(8,128)(2,1)}, bf16[2,576,128]{2,1,0:T(8,128)(2,1)}, u32[]{:S(2)}, u32[]{:S(2)}) collective-permute-start(bf16[2,576,128]{2,1,0:T(8,128)(2,1)} %slice.337), channel_id=1, source_target_pairs={{32,64},{64,32},{0,96},{96,0},{33,65},{65,33},{1,97},{97,1},{34,66... | collective-permute-start | bytes 884744 | tf_op jit(solution)/shard_map/ppermute | solution.py:105
  264.3 26.0 %all-to-all-start.2 = ((bf16[8,128,192]{1,2,0:T(8,128)(2,1)}), bf16[8,128,192]{1,2,0:T(8,128)(2,1)}, u32[]{:S(2)}, u32[]{:S(2)}) async-start(bf16[8,128,192]{1,2,0:T(8,128)(2,1)} %copy.31), calls=%async_computation.2 | async-start | bytes 786432 | tf_op jit(solution)/shard_map/all_to_all | solution.py:639
  281.2 48.1 %collective-permute-start.75 = (bf16[1,576,128]{2,1,0:T(8,128)(2,1)}, bf16[1,576,128]{2,1,0:T(8,128)(2,1)}, u32[]{:S(2)}, u32[]{:S(2)}) collective-permute-start(bf16[1,576,128]{2,1,0:T(8,128)(2,1)} %add_convert_fusion.28), channel_id=1, source_target_pairs={{0,16},{16,0},{1,17},{17,1},{2,18},{18,2},{3,19},{19,3},{4,20},{20... | collective-permute-start | bytes 442376 | tf_op jit(solution)/shard_map/ppermute | solution.py:95
  284.9 45.5 %collective-permute-start.83 = (bf16[1,576,128]{2,1,0:T(8,128)(2,1)}, bf16[1,576,128]{2,1,0:T(8,128)(2,1)}, u32[]{:S(2)}, u32[]{:S(2)}) collective-permute-start(bf16[1,576,128]{2,1,0:T(8,128)(2,1)} %add_convert_fusion.26), channel_id=1, source_target_pairs={{0,16},{16,0},{1,17},{17,1},{2,18},{18,2},{3,19},{19,3},{4,20},{20... | collective-permute-start | bytes 442376 | tf_op jit(solution)/shard_map/ppermute | solution.py:95
  286.1 47.5 %collective-permute-start.91 = (bf16[1,576,128]{2,1,0:T(8,128)(2,1)}, bf16[1,576,128]{2,1,0:T(8,128)(2,1)}, u32[]{:S(2)}, u32[]{:S(2)}) collective-permute-start(bf16[1,576,128]{2,1,0:T(8,128)(2,1)} %add_convert_fusion.24), channel_id=1, source_target_pairs={{0,16},{16,0},{1,17},{17,1},{2,18},{18,2},{3,19},{19,3},{4,20},{20... | collective-permute-start | bytes 442376 | tf_op jit(solution)/shard_map/ppermute | solution.py:95
  289.8 46.9 %collective-permute-start.99 = (bf16[1,576,128]{2,1,0:T(8,128)(2,1)}, bf16[1,576,128]{2,1,0:T(8,128)(2,1)}, u32[]{:S(2)}, u32[]{:S(2)}) collective-permute-start(bf16[1,576,128]{2,1,0:T(8,128)(2,1)} %add_convert_fusion.22), channel_id=1, source_target_pairs={{0,16},{16,0},{1,17},{17,1},{2,18},{18,2},{3,19},{19,3},{4,20},{20... | collective-permute-start | bytes 442376 | tf_op jit(solution)/shard_map/ppermute | solution.py:95
  328.5 33.8 %collective-permute-start.29 = (bf16[1024,192]{1,0:T(8,128)(2,1)S(1)}, bf16[1024,192]{1,0:T(8,128)(2,1)S(1)}, u32[]{:S(2)}, u32[]{:S(2)}) collective-permute-start(bf16[1024,192]{1,0:T(8,128)(2,1)S(1)} %get-tuple-element.83), channel_id=1, source_target_pairs={{0,12},{4,0},{8,4},{12,8},{1,13},{5,1},{9,5},{13,9},{2,14},{6,2},{... | collective-permute-start | bytes 1179656 | tf_op jit(solution)/shard_map/ppermute | solution.py:113
  329.3 34.3 %collective-permute-start.28 = (bf16[1024,192]{1,0:T(8,128)(2,1)S(1)}, bf16[1024,192]{1,0:T(8,128)(2,1)S(1)}, u32[]{:S(2)}, u32[]{:S(2)}) collective-permute-start(bf16[1024,192]{1,0:T(8,128)(2,1)S(1)} %get-tuple-element.82), channel_id=1, source_target_pairs={{0,8},{4,12},{8,0},{12,4},{1,9},{5,13},{9,1},{13,5},{2,10},{6,14},... | collective-permute-start | bytes 1179656 | tf_op jit(solution)/shard_map/ppermute | solution.py:113
  330.4 33.2 %collective-permute-start.27 = (bf16[1024,192]{1,0:T(8,128)(2,1)S(1)}, bf16[1024,192]{1,0:T(8,128)(2,1)S(1)}, u32[]{:S(2)}, u32[]{:S(2)}) collective-permute-start(bf16[1024,192]{1,0:T(8,128)(2,1)S(1)} %get-tuple-element.81), channel_id=1, source_target_pairs={{0,4},{4,8},{8,12},{12,0},{1,5},{5,9},{9,13},{13,1},{2,6},{6,10},{... | collective-permute-start | bytes 1179656 | tf_op jit(solution)/shard_map/ppermute | solution.py:113
  333.6 19.7 %collective-permute-start.76 = (bf16[1,576,128]{2,1,0:T(8,128)(2,1)S(1)}, bf16[1,576,128]{2,1,0:T(8,128)(2,1)S(1)}, u32[]{:S(2)}, u32[]{:S(2)}) collective-permute-start(bf16[1,576,128]{2,1,0:T(8,128)(2,1)S(1)} %add_convert_fusion.27), channel_id=1, source_target_pairs={{4,8},{8,4},{0,12},{12,0},{5,9},{9,5},{1,13},{13,1},{6,10},{10,6},... | collective-permute-start | bytes 442376 | tf_op jit(solution)/shard_map/ppermute | solution.py:105
  336.7 17.9 %collective-permute-start.84 = (bf16[1,576,128]{2,1,0:T(8,128)(2,1)S(1)}, bf16[1,576,128]{2,1,0:T(8,128)(2,1)S(1)}, u32[]{:S(2)}, u32[]{:S(2)}) collective-permute-start(bf16[1,576,128]{2,1,0:T(8,128)(2,1)S(1)} %add_convert_fusion.25), channel_id=1, source_target_pairs={{0,32},{32,0},{64,96},{96,64},{1,33},{33,1},{65,97},{97,65},{2,34}... | collective-permute-start | bytes 442376 | tf_op jit(solution)/shard_map/ppermute | solution.py:105
  354.6 23.0 %collective-permute-start.100 = (bf16[1,576,128]{2,1,0:T(8,128)(2,1)S(1)}, bf16[1,576,128]{2,1,0:T(8,128)(2,1)S(1)}, u32[]{:S(2)}, u32[]{:S(2)}) collective-permute-start(bf16[1,576,128]{2,1,0:T(8,128)(2,1)S(1)} %add_convert_fusion.21), channel_id=1, source_target_pairs={{0,4},{4,0},{8,12},{12,8},{1,5},{5,1},{9,13},{13,9},{2,6},{6,2},{1... | collective-permute-start | bytes 442376 | tf_op jit(solution)/shard_map/ppermute | solution.py:105
  362.4 19.4 %collective-permute-start.85 = (bf16[2,576,128]{2,1,0:T(8,128)(2,1)}, bf16[2,576,128]{2,1,0:T(8,128)(2,1)}, u32[]{:S(2)}, u32[]{:S(2)}) collective-permute-start(bf16[2,576,128]{2,1,0:T(8,128)(2,1)} %pad_maximum_fusion.14), channel_id=1, source_target_pairs={{4,8},{8,4},{0,12},{12,0},{5,9},{9,5},{1,13},{13,1},{6,10},{10,6},... | collective-permute-start | bytes 884744 | tf_op jit(solution)/shard_map/ppermute | solution.py:105
  363.6 20.3 %collective-permute-start.93 = (bf16[2,576,128]{2,1,0:T(8,128)(2,1)}, bf16[2,576,128]{2,1,0:T(8,128)(2,1)S(1)}, u32[]{:S(2)}, u32[]{:S(2)}) collective-permute-start(bf16[2,576,128]{2,1,0:T(8,128)(2,1)} %pad_maximum_fusion.15), channel_id=1, source_target_pairs={{0,32},{32,0},{64,96},{96,64},{1,33},{33,1},{65,97},{97,65},{2,34}... | collective-permute-start | bytes 884744 | tf_op jit(solution)/shard_map/ppermute | solution.py:105
  369.3 31.9 %collective-permute-start.78 = (bf16[4,576,128]{2,1,0:T(8,128)(2,1)}, bf16[4,576,128]{2,1,0:T(8,128)(2,1)}, u32[]{:S(2)}, u32[]{:S(2)}) collective-permute-start(bf16[4,576,128]{2,1,0:T(8,128)(2,1)} %pad_maximum_fusion.5), channel_id=1, source_target_pairs={{32,64},{64,32},{0,96},{96,0},{33,65},{65,33},{1,97},{97,1},{34,66... | collective-permute-start | bytes 1769480 | tf_op jit(solution)/shard_map/ppermute | solution.py:105
  371.7 33.8 %all-to-all-start.3 = ((bf16[8,128,384]{2,1,0:T(8,128)(2,1)}), bf16[8,128,384]{2,1,0:T(8,128)(2,1)S(1)}, u32[]{:S(2)}, u32[]{:S(2)}) async-start(bf16[8,128,384]{2,1,0:T(8,128)(2,1)} %bitcast.22), calls=%async_computation.3 | async-start | bytes 1572864 | tf_op jit(solution)/shard_map/all_to_all | solution.py:639
  378.3 20.8 %collective-permute-start.101 = (bf16[2,576,128]{2,1,0:T(8,128)(2,1)}, bf16[2,576,128]{2,1,0:T(8,128)(2,1)}, u32[]{:S(2)}, u32[]{:S(2)}) collective-permute-start(bf16[2,576,128]{2,1,0:T(8,128)(2,1)} %pad_maximum_fusion.16), channel_id=1, source_target_pairs={{32,64},{64,32},{0,96},{96,0},{33,65},{65,33},{1,97},{97,1},{34,66... | collective-permute-start | bytes 884744 | tf_op jit(solution)/shard_map/ppermute | solution.py:105
  383.6 35.2 %collective-permute-start.86 = (bf16[4,576,128]{2,1,0:T(8,128)(2,1)}, bf16[4,576,128]{2,1,0:T(8,128)(2,1)}, u32[]{:S(2)}, u32[]{:S(2)}) collective-permute-start(bf16[4,576,128]{2,1,0:T(8,128)(2,1)} %pad_maximum_fusion.6), channel_id=1, source_target_pairs={{0,4},{4,0},{8,12},{12,8},{1,5},{5,1},{9,13},{13,9},{2,6},{6,2},{1... | collective-permute-start | bytes 1769480 | tf_op jit(solution)/shard_map/ppermute | solution.py:105
  384.8 36.4 %collective-permute-start.94 = (bf16[4,576,128]{2,1,0:T(8,128)(2,1)}, bf16[4,576,128]{2,1,0:T(8,128)(2,1)}, u32[]{:S(2)}, u32[]{:S(2)}) collective-permute-start(bf16[4,576,128]{2,1,0:T(8,128)(2,1)} %pad_maximum_fusion.7), channel_id=1, source_target_pairs={{4,8},{8,4},{0,12},{12,0},{5,9},{9,5},{1,13},{13,1},{6,10},{10,6},... | collective-permute-start | bytes 1769480 | tf_op jit(solution)/shard_map/ppermute | solution.py:105
  401.0 24.5 %collective-permute-start.102 = (bf16[4,576,128]{2,1,0:T(8,128)(2,1)}, bf16[4,576,128]{2,1,0:T(8,128)(2,1)}, u32[]{:S(2)}, u32[]{:S(2)}) collective-permute-start(bf16[4,576,128]{2,1,0:T(8,128)(2,1)} %pad_maximum_fusion.8), channel_id=1, source_target_pairs={{0,32},{32,0},{64,96},{96,64},{1,33},{33,1},{65,97},{97,65},{2,34}... | collective-permute-start | bytes 1769480 | tf_op jit(solution)/shard_map/ppermute | solution.py:105
  403.4 148.0 %collective-permute-start.103 = (bf16[8,576,128]{2,1,0:T(8,128)(2,1)}, bf16[8,576,128]{2,1,0:T(8,128)(2,1)}, u32[]{:S(2)}, u32[]{:S(2)}) collective-permute-start(bf16[8,576,128]{2,1,0:T(8,128)(2,1)} %pad_maximum_fusion.refs_0_), channel_id=1, source_target_pairs={{0,32},{32,0},{64,96},{96,64},{1,33},{33,1},{65,97},{97,65},{2,34}... | collective-permute-start | bytes 3538952 | tf_op jit(solution)/shard_map/ppermute | solution.py:105
  420.1 132.5 %collective-permute-start.104 = (bf16[8,576,128]{2,1,0:T(8,128)(2,1)S(1)}, bf16[8,576,128]{2,1,0:T(8,128)(2,1)S(1)}, u32[]{:S(2)}, u32[]{:S(2)}) collective-permute-start(bf16[8,576,128]{2,1,0:T(8,128)(2,1)S(1)} %pad_maximum_fusion.1.refs_1_), channel_id=1, source_target_pairs={{32,64},{64,32},{0,96},{96,0},{33,65},{65,33},{1,97},{97,1},{34,66... | collective-permute-start | bytes 3538952 | tf_op jit(solution)/shard_map/ppermute | solution.py:105
  427.1 51.0 %collective-permute-start.30 = (bf16[2,128,1536]{2,1,0:T(8,128)(2,1)S(1)}, bf16[2,128,1536]{2,1,0:T(8,128)(2,1)S(1)}, u32[]{:S(2)}, u32[]{:S(2)}) collective-permute-start(bf16[2,128,1536]{2,1,0:T(8,128)(2,1)S(1)} %get-tuple-element.85), channel_id=1, source_target_pairs={{0,1},{1,0},{2,3},{3,2},{4,5},{5,4},{6,7},{7,6},{8,9},{9,8},{10,11... | collective-permute-start | bytes 2359304 | tf_op jit(solution)/shard_map/ppermute | solution.py:72
  427.3 21.8 %collective-permute-start.32 = (bf16[8,224,128]{2,1,0:T(8,128)(2,1)S(1)}, bf16[8,224,128]{2,1,0:T(8,128)(2,1)S(1)}, u32[]{:S(2)}, u32[]{:S(2)}) collective-permute-start(bf16[8,224,128]{2,1,0:T(8,128)(2,1)S(1)} %get-tuple-element.89), channel_id=1, source_target_pairs={{0,32},{32,0},{64,96},{96,64},{1,33},{33,1},{65,97},{97,65},{2,34}... | collective-permute-start | bytes 1376264 | tf_op jit(solution)/shard_map/ppermute | solution.py:105
  430.7 25.3 %collective-permute-start.40 = (bf16[8,224,128]{2,1,0:T(8,128)(2,1)S(1)}, bf16[8,224,128]{2,1,0:T(8,128)(2,1)S(1)}, u32[]{:S(2)}, u32[]{:S(2)}) collective-permute-start(bf16[8,224,128]{2,1,0:T(8,128)(2,1)S(1)} %get-tuple-element.91), channel_id=1, source_target_pairs={{32,64},{64,32},{0,96},{96,0},{33,65},{65,33},{1,97},{97,1},{34,66... | collective-permute-start | bytes 1376264 | tf_op jit(solution)/shard_map/ppermute | solution.py:105
  471.2 20.0 %collective-permute-start.34 = (bf16[2,224,128]{2,1,0:T(8,128)(2,1)S(1)}, bf16[2,224,128]{2,1,0:T(8,128)(2,1)S(1)}, u32[]{:S(2)}, u32[]{:S(2)}) collective-permute-start(bf16[2,224,128]{2,1,0:T(8,128)(2,1)S(1)} %slice.289), channel_id=1, source_target_pairs={{0,4},{4,0},{8,12},{12,8},{1,5},{5,1},{9,13},{13,9},{2,6},{6,2},{1... | collective-permute-start | bytes 344072 | tf_op jit(solution)/shard_map/ppermute | solution.py:105
  475.4 16.5 %collective-permute-start.42 = (bf16[2,224,128]{2,1,0:T(8,128)(2,1)S(1)}, bf16[2,224,128]{2,1,0:T(8,128)(2,1)S(1)}, u32[]{:S(2)}, u32[]{:S(2)}) collective-permute-start(bf16[2,224,128]{2,1,0:T(8,128)(2,1)S(1)} %slice.295), channel_id=1, source_target_pairs={{4,8},{8,4},{0,12},{12,0},{5,9},{9,5},{1,13},{13,1},{6,10},{10,6},... | collective-permute-start | bytes 344072 | tf_op jit(solution)/shard_map/ppermute | solution.py:105
  511.5 41.5 %collective-permute-start.105 = (bf16[8,576,128]{2,1,0:T(8,128)(2,1)S(1)}, bf16[8,576,128]{2,1,0:T(8,128)(2,1)S(1)}, u32[]{:S(2)}, u32[]{:S(2)}) collective-permute-start(bf16[8,576,128]{2,1,0:T(8,128)(2,1)S(1)} %pad_maximum_fusion.2.refs_2_), channel_id=1, source_target_pairs={{0,4},{4,0},{8,12},{12,8},{1,5},{5,1},{9,13},{13,9},{2,6},{6,2},{1... | collective-permute-start | bytes 3538952 | tf_op jit(solution)/shard_map/ppermute | solution.py:105
  515.5 38.9 %collective-permute-start.106 = (bf16[8,576,128]{2,1,0:T(8,128)(2,1)S(1)}, bf16[8,576,128]{2,1,0:T(8,128)(2,1)S(1)}, u32[]{:S(2)}, u32[]{:S(2)}) collective-permute-start(bf16[8,576,128]{2,1,0:T(8,128)(2,1)S(1)} %pad_maximum_fusion.3.refs_3_), channel_id=1, source_target_pairs={{4,8},{8,4},{0,12},{12,0},{5,9},{9,5},{1,13},{13,1},{6,10},{10,6},... | collective-permute-start | bytes 3538952 | tf_op jit(solution)/shard_map/ppermute | solution.py:105
  522.7 20.0 %collective-permute-start.38 = (bf16[2,224,128]{2,1,0:T(8,128)(2,1)S(1)}, bf16[2,224,128]{2,1,0:T(8,128)(2,1)S(1)}, u32[]{:S(2)}, u32[]{:S(2)}) collective-permute-start(bf16[2,224,128]{2,1,0:T(8,128)(2,1)S(1)} %pad_maximum_fusion.21), channel_id=1, source_target_pairs={{0,4},{4,0},{8,12},{12,8},{1,5},{5,1},{9,13},{13,9},{2,6},{6,2},{1... | collective-permute-start | bytes 344072 | tf_op jit(solution)/shard_map/ppermute | solution.py:105
  547.5 26.0 %collective-permute-start.31 = (bf16[128,1536]{1,0:T(8,128)(2,1)}, bf16[128,1536]{1,0:T(8,128)(2,1)S(1)}, u32[]{:S(2)}, u32[]{:S(2)}) collective-permute-start(bf16[128,1536]{1,0:T(8,128)(2,1)} %fusion.18), channel_id=1, source_target_pairs={{0,2},{2,0},{1,3},{3,1},{4,6},{6,4},{5,7},{7,5},{8,10},{10,8},{9,1... | collective-permute-start | bytes 1179656 | tf_op jit(solution)/shard_map/ppermute | solution.py:76
  551.4 22.4 %collective-permute-start.57 = (bf16[4,208,128]{2,1,0:T(8,128)(2,1)}, bf16[4,208,128]{2,1,0:T(8,128)(2,1)}, u32[]{:S(2)}, u32[]{:S(2)}) collective-permute-start(bf16[4,208,128]{2,1,0:T(8,128)(2,1)} %pad_maximum_fusion.19), channel_id=1, source_target_pairs={{4,8},{8,4},{0,12},{12,0},{5,9},{9,5},{1,13},{13,1},{6,10},{10,6},... | collective-permute-start | bytes 638984 | tf_op jit(solution)/shard_map/ppermute | solution.py:105
  552.6 22.7 %collective-permute-start.66 = (bf16[4,208,128]{2,1,0:T(8,128)(2,1)}, bf16[4,208,128]{2,1,0:T(8,128)(2,1)}, u32[]{:S(2)}, u32[]{:S(2)}) collective-permute-start(bf16[4,208,128]{2,1,0:T(8,128)(2,1)} %pad_maximum_fusion.20), channel_id=1, source_target_pairs={{0,32},{32,0},{64,96},{96,64},{1,33},{33,1},{65,97},{97,65},{2,34}... | collective-permute-start | bytes 638984 | tf_op jit(solution)/shard_map/ppermute | solution.py:105
  553.0 24.9 %collective-permute-start.39 = (bf16[4,224,128]{2,1,0:T(8,128)(2,1)}, bf16[4,224,128]{2,1,0:T(8,128)(2,1)}, u32[]{:S(2)}, u32[]{:S(2)}) collective-permute-start(bf16[4,224,128]{2,1,0:T(8,128)(2,1)} %pad_maximum_fusion.17), channel_id=1, source_target_pairs={{32,64},{64,32},{0,96},{96,0},{33,65},{65,33},{1,97},{97,1},{34,66... | collective-permute-start | bytes 688136 | tf_op jit(solution)/shard_map/ppermute | solution.py:105
  555.4 23.6 %collective-permute-start.48 = (bf16[4,224,128]{2,1,0:T(8,128)(2,1)}, bf16[4,224,128]{2,1,0:T(8,128)(2,1)}, u32[]{:S(2)}, u32[]{:S(2)}) collective-permute-start(bf16[4,224,128]{2,1,0:T(8,128)(2,1)} %pad_maximum_fusion.18), channel_id=1, source_target_pairs={{0,4},{4,0},{8,12},{12,8},{1,5},{5,1},{9,13},{13,9},{2,6},{6,2},{1... | collective-permute-start | bytes 688136 | tf_op jit(solution)/shard_map/ppermute | solution.py:105
  578.9 11.9 %collective-permute-start.70 = (bf16[8,208,128]{2,1,0:T(8,128)(2,1)S(1)}, bf16[8,208,128]{2,1,0:T(8,128)(2,1)S(1)}, u32[]{:S(2)}, u32[]{:S(2)}) collective-permute-start(bf16[8,208,128]{2,1,0:T(8,128)(2,1)S(1)} %pad_maximum_fusion.12.refs_3_), channel_id=1, source_target_pairs={{4,8},{8,4},{0,12},{12,0},{5,9},{9,5},{1,13},{13,1},{6,10},{10,6},... | collective-permute-start | bytes 1277960 | tf_op jit(solution)/shard_map/ppermute | solution.py:105
  580.8 12.3 %collective-permute-start.67 = (bf16[8,224,128]{2,1,0:T(8,128)(2,1)S(1)}, bf16[8,224,128]{2,1,0:T(8,128)(2,1)S(1)}, u32[]{:S(2)}, u32[]{:S(2)}) collective-permute-start(bf16[8,224,128]{2,1,0:T(8,128)(2,1)S(1)} %pad_maximum_fusion.9.refs_0_), channel_id=1, source_target_pairs={{0,32},{32,0},{64,96},{96,64},{1,33},{33,1},{65,97},{97,65},{2,34}... | collective-permute-start | bytes 1376264 | tf_op jit(solution)/shard_map/ppermute | solution.py:105
  582.0 13.3 %collective-permute-start.68 = (bf16[8,224,128]{2,1,0:T(8,128)(2,1)S(1)}, bf16[8,224,128]{2,1,0:T(8,128)(2,1)S(1)}, u32[]{:S(2)}, u32[]{:S(2)}) collective-permute-start(bf16[8,224,128]{2,1,0:T(8,128)(2,1)S(1)} %pad_maximum_fusion.10.refs_1_), channel_id=1, source_target_pairs={{32,64},{64,32},{0,96},{96,0},{33,65},{65,33},{1,97},{97,1},{34,66... | collective-permute-start | bytes 1376264 | tf_op jit(solution)/shard_map/ppermute | solution.py:105
  (124 other events, 1538.8 us)

commit v2 on v1

v2 whole, which is shorter than its diff:
```python
import functools

import jax
import jax.numpy as jnp
from jax import lax
from jax.experimental import pallas as pl
from jax.experimental.pallas import tpu as pltpu
from jax.sharding import Mesh, PartitionSpec as P

D = 1536
HEADS = 16
KV_HEADS = 8
HEAD_DIM = 96
HALF = HEAD_DIM // 2
FF = 4096
BLOCK = 64
SEQ = 4096
WINDOW_BLOCKS = 32
SHARDS = 4
ROWS = 128
TOK = SHARDS * ROWS
DS = D // SHARDS
FS = FF // SHARDS
EPS = 1e-05
ROPE_BASE = 10000.0
MASKED = -1e30
SCALE = HEAD_DIM ** (-0.5)
LOG2E = 1.4426950408889634
BF = jnp.bfloat16
F32 = jnp.float32

CHUNK_BLOCKS = 8
CHUNK = CHUNK_BLOCKS * BLOCK

SMEM_SPEC = pl.BlockSpec(memory_space=pltpu.SMEM)
VMEM_SPEC = pl.BlockSpec(memory_space=pltpu.VMEM)
ANY_SPEC = pl.BlockSpec(memory_space=pl.ANY)
PARAMS = pltpu.CompilerParams(vmem_limit_bytes=60 * 1024 * 1024)


def cost(us):
    flops, nbytes = int(us * 1_100_000_000), int(us * 3_000_000)
    return pl.CostEstimate(flops=flops, bytes_accessed=nbytes, transcendentals=0)


def call(kernel, outs, smem, vmem, us, scratch=(), deps=()):
    n, d = len(smem) + len(vmem), len(deps)

    def body(*refs):
        kernel(*refs[:n], *refs[n + d :])

    return pl.pallas_call(
        body,
        out_shape=outs,
        in_specs=[SMEM_SPEC] * len(smem) + [VMEM_SPEC] * len(vmem) + [ANY_SPEC] * d,
        out_specs=jax.tree.map(lambda _: VMEM_SPEC, outs),
        scratch_shapes=list(scratch),
        compiler_params=PARAMS,
        cost_estimate=cost(us),
    )(*smem, *vmem, *deps)


def sds(shape, dtype=BF):
    return jax.ShapeDtypeStruct(shape, dtype)


def dot(a, b):
    return jnp.dot(a, b, preferred_element_type=F32)


def dot_t(a, b):
    return lax.dot_general(a, b, (((1,), (1,)), ((), ())), preferred_element_type=F32)


def t_dot(a, b):
    return lax.dot_general(a, b, (((0,), (0,)), ((), ())), preferred_element_type=F32)


def swap_c(x):
    return lax.ppermute(x, "c", [(0, 1), (1, 0)])


def swap_xl(x):
    return lax.ppermute(x, "xl", [(0, 1), (1, 0)])


def swap_both(x):
    return lax.ppermute(x, ("xl", "c"), [(i, i ^ 3) for i in range(4)])


def swap_far(x, core):
    pairs = []
    for place in range(4):
        other = (place + 1) % 4 if place % 2 else (place + 3) % 4
        for c in range(2):
            pairs.append((place * 2 + c, other * 2 + (c ^ core)))
    return lax.ppermute(x, ("xh", "xl", "c"), pairs)


def swap_e(x):
    return lax.ppermute(x, "xh", [(0, 1), (1, 0)])


NEAR = [(0, 1), (1, 0), (2, 3), (3, 2)]
AROUND = [(1, 2), (2, 1), (0, 3), (3, 0)]
CUBE = (("y", NEAR), ("y", AROUND), ("z", NEAR), ("z", AROUND))


def swap_cube(x, dim):
    axis, pairs = CUBE[dim % 4]
    return lax.ppermute(x, axis, pairs)


def from_z(x, m):
    return lax.ppermute(x, "z", [((i + m) % 4, i) for i in range(4)])


def to_z(x, m):
    return lax.ppermute(x, "z", [(i, (i + m) % 4) for i in range(4)])


def gather_slots(own):
    far = swap_xl(own)
    return own, swap_c(own), far, swap_c(far)


def scatter_slots(keep, send):
    got = swap_c(send)
    other = (keep[1].astype(F32) + got[1].astype(F32)).astype(BF)
    return (keep, got, swap_xl(other)), other


CTX = ("y", "xh", "z")
FSDP = ("xl", "c")


def after(x, other):
    return lax.optimization_barrier((x, other))[0]


def shifts(x, axis):
    return [lax.ppermute(x, axis, [((i + m) % 4, i) for i in range(4)]) for m in (1, 2, 3)]


def exchange(x, axes):
    return lax.all_to_all(x, axes, 0, 0, tiled=True)


def cube_index(portion, bits):
    out = 0
    for t in range(4):
        out = out * 2 + bits[(portion + t) % 4]
    return out


def fold(x):
    tail = jnp.concatenate([x[0:64, 128:192], x[64:128, 128:192]], axis=1)
    return jnp.concatenate([x[:, 0:128], tail], axis=0)


def unfold(x):
    tail = jnp.concatenate([x[128:192, 0:64], x[128:192, 64:128]], axis=0)
    return jnp.concatenate([x[0:128], tail], axis=1)


def pack_kernel(sc, wq, wk, wv, gains, q0, q1, q2, q3, k0, k1, k2, k3, tmp):
    f = sc[0]
    for g in range(4):
        tmp[g, :, 0:192] = wk[:, 192 * g : 192 * (g + 1)]
        tmp[g, :, 192:384] = wv[:, 192 * g : 192 * (g + 1)]
    for k, (q, kv) in enumerate(((q0, k0), (q1, k1), (q2, k2), (q3, k3))):
        q[...] = wq[:, pl.ds(pl.multiple_of((f ^ k) * DS, 128), DS)]
        kv[0:DS] = tmp[f ^ k]
        kv[DS:] = gains[...]


def project(f, xa, ws):
    total = jnp.zeros((TOK, DS), F32)
    for k, w in enumerate(ws):
        at = pl.multiple_of((f ^ k) * DS, 128)
        total = total + dot(xa[:, pl.ds(at, DS)], w[0:DS])
    return total


def rotate(u, co, si):
    turned = jnp.concatenate([-u[:, HALF:], u[:, :HALF]], axis=1)
    return u * co + turned * si


def kv_kernel(sc, x0, x1, x2, x3, k0, k1, k2, k3, cos, sin, xa, kv, gain_a, gain_m):
    f = sc[0]
    for k, w in enumerate((k0, k1, k2, k3)):
        at = pl.ds(pl.multiple_of((f ^ k) * DS, 128), DS)
        rows = w[DS:].astype(F32)
        gain_a[:, at] = rows[0:1]
        gain_m[:, at] = rows[1:2]
    for k, x in enumerate((x0, x1, x2, x3)):
        u = x[...].astype(F32)
        r = lax.rsqrt(jnp.mean(u * u, axis=-1, keepdims=True) + EPS)
        xa[ROWS * k : ROWS * (k + 1), :] = (u * r * gain_a[...]).astype(BF)
    lin = project(f, xa, [w[0:DS] for w in (k0, k1, k2, k3)])
    co, si = cos[...], sin[...]
    for k in range(4):
        part = lin[ROWS * k : ROWS * (k + 1)]
        for j in range(2):
            key = rotate(part[:, 96 * j : 96 * (j + 1)], co, si)
            value = part[:, 192 + 96 * j : 192 + 96 * (j + 1)]
            kv[2 * k + j] = fold(jnp.concatenate([key, value], axis=1)).astype(BF)


def q_kernel(sc, xa, w0, w1, w2, w3, cos, sin, q):
    lin = project(sc[0], xa, (w0, w1, w2, w3))
    co, si = cos[...], sin[...]
    for k in range(4):
        part = lin[ROWS * k : ROWS * (k + 1)]
        heads = [rotate(part[:, 96 * h : 96 * (h + 1)], co, si) for h in range(4)]
        for j in range(2):
            q[2 * k + j] = fold(jnp.concatenate(heads[2 * j : 2 * j + 2], axis=1)).astype(BF)


def widen(x, *tail):
    zeros = jnp.zeros((x.shape[0], 128 - x.shape[1] - len(tail)), x.dtype)
    return jnp.concatenate([x, *tail, zeros], axis=1)


def stacked(x, t):
    rows = slice(BLOCK * t, BLOCK * (t + 1))
    return jnp.concatenate([x[rows, 0:96], x[rows, 96:192]], axis=0)


def side_by_side(a, b):
    rows = [jnp.concatenate([x[0:BLOCK, 0:96], x[BLOCK:, 0:96]], axis=1) for x in (a, b)]
    return fold(jnp.concatenate(rows, axis=0))


def low_high(qb, n):
    swapped = (qb[2 * n] >= WINDOW_BLOCKS).astype(jnp.int32)
    return 2 * n + swapped, 2 * n + 1 - swapped


def attention_kernel(qb, kb, q, kv0, kv1, kv2, kv3, o, o2, q2, lse, kv):
    ones = (lax.broadcasted_iota(jnp.int32, (BLOCK, 32), 1) < 4).astype(F32)

    def place(s, _):
        for m, ref in enumerate((kv0, kv1, kv2, kv3)):
            x = unfold(ref[s].astype(F32))
            for t in range(2):
                dst = pl.ds(pl.multiple_of(kb[m * 16 + 2 * s + t] * BLOCK, BLOCK), BLOCK)
                part = x[BLOCK * t : BLOCK * (t + 1)]
                both = jnp.concatenate([part[:, 0:96], ones, part[:, 96:192], ones], axis=1)
                kv[dst, :] = both.astype(BF)
        x = unfold(q[s].astype(F32))
        for t in range(2):
            q2[2 * s + t] = widen(stacked(x, t)).astype(BF)
        return 0

    lax.fori_loop(0, 8, place, 0)
    two = SCALE * LOG2E

    def scores(n, spans):
        return [dot_t(q2[n], kv[span, 0:128]) for span in spans]

    def finish(n, parts, spans):
        tops = [jnp.max(s, axis=1, keepdims=True) for s in parts]
        top = functools.reduce(jnp.maximum, tops) * two
        acc = jnp.zeros((ROWS, 128), F32)
        for s, span in zip(parts, spans):
            acc += dot(jnp.exp2(s * two - top).astype(BF), kv[span, 128:256])
        total = acc[:, 96:97]
        o2[n] = (acc / total).astype(BF)
        lse[n] = jnp.broadcast_to(top + jnp.log2(total), (ROWS, 8))

    def pair(n, _):
        low, high = low_high(qb, n)
        i_low, i_high = qb[low], qb[high]
        for count in range(1, 5):

            @pl.when(i_low // CHUNK_BLOCKS == count - 1)
            def _():
                edge = pl.ds(pl.multiple_of((i_high - WINDOW_BLOCKS) * BLOCK, BLOCK), BLOCK)
                at = pl.multiple_of((i_high - WINDOW_BLOCKS + 1) * BLOCK, BLOCK)
                spans_h = [edge] + [pl.ds(at + CHUNK * t, CHUNK) for t in range(4)]
                spans_l = [pl.ds(CHUNK * t, CHUNK) for t in range(count)]
                high_s = scores(high, spans_h)
                low_s = scores(low, spans_l)
                key = lax.broadcasted_iota(jnp.int32, (ROWS, BLOCK), 1)
                query = lax.broadcasted_iota(jnp.int32, (ROWS, BLOCK), 0) % BLOCK
                high_s[0] = jnp.where(key > query, high_s[0], MASKED)
                key = lax.broadcasted_iota(jnp.int32, (ROWS, CHUNK), 1)
                limit = (i_low + 1) * BLOCK - CHUNK * (count - 1)
                low_s[-1] = jnp.where(key < limit, low_s[-1], MASKED)
                finish(high, high_s, spans_h)
                finish(low, low_s, spans_l)

        return 0

    lax.fori_loop(0, 8, pair, 0)

    def gather(s, _):
        o[s] = side_by_side(o2[2 * s].astype(F32), o2[2 * s + 1].astype(F32)).astype(BF)
        return 0

    lax.fori_loop(0, 8, gather, 0)


def attention_back_kernel(qb, kb, q2s, d_o, o2s, lse, kv, dq2s, g, dkv, do2s):
    dkv[...] = jnp.zeros_like(dkv)

    def place(s, _):
        x = unfold(d_o[s].astype(F32))
        for t in range(2):
            do2s[2 * s + t] = stacked(x, t).astype(BF)
        return 0

    lax.fori_loop(0, 8, place, 0)
    two = SCALE * LOG2E

    def split(x):
        parts = []
        for _ in range(3):
            parts.append(x.astype(BF))
            x = x - parts[-1].astype(F32)
        return parts

    def weights(n):
        do2 = do2s[n]
        inner = do2.astype(F32) * o2s[n][:, 0:96].astype(F32)
        inner = jnp.sum(inner, axis=1, keepdims=True)
        q2 = widen(q2s[n][:, 0:96], *split(lse[n][:, 0:1] * (-1.0 / two)))
        do2 = widen(do2, *split(-inner))
        none = jnp.zeros((ROWS, 128), BF)
        return jnp.concatenate(
            [jnp.concatenate([q2, none], axis=1), jnp.concatenate([none, do2], axis=1)], axis=0
        )

    def factors(w, spans, masks):
        pairs = []
        for span, mask in zip(spans, masks):
            s = dot_t(kv[span, :], w)
            p = jnp.exp2(s[:, 0:128] * two)
            if mask is not None:
                p = jnp.where(mask, p, 0.0)
            ds = (p * s[:, 128:256]).astype(BF)
            pairs.append(jnp.concatenate([ds, p.astype(BF)], axis=1))
        return pairs

    def add(n, w, spans, pairs):
        acc = jnp.zeros((ROWS, 128), F32)
        for span, both in zip(spans, pairs):
            dkv[span, :] += dot(both, w)
            acc += t_dot(both[:, 0:128], kv[span, 0:128])
        dq2s[n] = (acc * SCALE).astype(BF)

    def pair(n, _):
        low, high = low_high(qb, n)
        i_low, i_high = qb[low], qb[high]
        for count in range(1, 5):

            @pl.when(i_low // CHUNK_BLOCKS == count - 1)
            def _():
                edge = pl.ds(pl.multiple_of((i_high - WINDOW_BLOCKS) * BLOCK, BLOCK), BLOCK)
                at = pl.multiple_of((i_high - WINDOW_BLOCKS + 1) * BLOCK, BLOCK)
                key = lax.broadcasted_iota(jnp.int32, (BLOCK, ROWS), 0)
                query = lax.broadcasted_iota(jnp.int32, (BLOCK, ROWS), 1) % BLOCK
                spans_h = [edge] + [pl.ds(at + CHUNK * t, CHUNK) for t in range(4)]
                masks_h = [key > query] + [None] * 4
                spans_l = [pl.ds(CHUNK * t, CHUNK) for t in range(count)]
                key = lax.broadcasted_iota(jnp.int32, (CHUNK, ROWS), 0)
                limit = (i_low + 1) * BLOCK - CHUNK * (count - 1)
                masks_l = [None] * (count - 1) + [key < limit]
                w_h, w_l = weights(high), weights(low)
                pairs_h = factors(w_h, spans_h, masks_h)
                pairs_l = factors(w_l, spans_l, masks_l)
                add(high, w_h, spans_h, pairs_h)
                add(low, w_l, spans_l, pairs_l)

        return 0

    lax.fori_loop(0, 8, pair, 0)

    def keys(s, _):
        parts = []
        for t in range(2):
            src = pl.ds(pl.multiple_of(kb[2 * s + t] * BLOCK, BLOCK), BLOCK)
            both = dkv[src, :]
            parts.append(jnp.concatenate([both[:, 0:96] * SCALE, both[:, 128:224]], axis=1))
        g[s] = fold(jnp.concatenate(parts, axis=0)).astype(BF)
        return 0

    lax.fori_loop(0, 32, keys, 0)


def fold_dq_kernel(dq2s, dq):
    for s in range(8):
        dq[s] = side_by_side(dq2s[2 * s].astype(F32), dq2s[2 * s + 1].astype(F32)).astype(BF)


def unfolded(o):
    return unfold(o.astype(F32)).astype(BF)


def out_kernel(o, w, keep, send):
    for k in range(4):
        total = dot(unfolded(o[2 * k]), w[0:192, :]) + dot(unfolded(o[2 * k + 1]), w[192:384, :])
        (keep, send)[k % 2][k // 2] = total.astype(BF)


def hidden_kernel(x, keep, got, far, gain, hidden, xm):
    h = x[...].astype(F32) + keep[0].astype(F32) + got[0].astype(F32) + far[...].astype(F32)
    hidden[...] = h
    r = lax.rsqrt(jnp.mean(h * h, axis=-1, keepdims=True) + EPS)
    xm[...] = (h * r * gain[...]).astype(BF)


def norm_back(values, gain, grads):
    factor = lax.rsqrt(jnp.mean(values * values, axis=-1, keepdims=True) + EPS)
    weighted = grads * gain
    inner = jnp.mean(weighted * values, axis=-1, keepdims=True)
    return factor * weighted - values * (factor * factor * factor) * inner


def d_hidden_kernel(dy, keep, got, far, hidden, gain, d_hidden, d_br, d_gain):
    grads = keep[0].astype(F32) + got[0].astype(F32) + far[...].astype(F32)
    h = hidden[...]
    d = dy[...].astype(F32) + norm_back(h, gain[...], grads)
    d_hidden[...] = d
    d_br[...] = d.astype(BF)
    r = lax.rsqrt(jnp.mean(h * h, axis=-1, keepdims=True) + EPS)
    total = jnp.sum(grads * h * r, axis=0, keepdims=True)
    rows = [total[:, 128 * t : 128 * (t + 1)] for t in range(12)]
    d_gain[...] = jnp.concatenate(rows + [jnp.zeros((4, 128), F32)], axis=0).astype(BF)


def d_tokens_kernel(x, keep, got, far, d_hidden, gain, d_tokens):
    grads = keep[0].astype(F32) + got[0].astype(F32) + far[...].astype(F32)
    d_tokens[...] = d_hidden[...] + norm_back(x[...].astype(F32), gain[...], grads)


def layer_out_kernel(hidden, keep, got, far, out):
    total = keep[0].astype(F32) + got[0].astype(F32) + far[...].astype(F32)
    out[...] = (hidden[...] + total).astype(BF)


def d_o_kernel(b0, b1, b2, b3, w, d_o):
    for k, b in enumerate((b0, b1, b2, b3)):
        d = dot_t(b[...], w[...])
        d_o[2 * k] = fold(d[:, 0:192]).astype(BF)
        d_o[2 * k + 1] = fold(d[:, 192:384]).astype(BF)


FBLOCK = 512


def d_act_kernel(y0, y1, y2, y3, wd, da):
    ys = jnp.concatenate([y0[...], y1[...], y2[...], y3[...]], axis=0)
    da[...] = dot_t(ys, wd[...])


def ffn_kernel(sc, x0, x1, x2, x3, da, wg, wu, act, dg, du, keep, send, xs, acc):
    n = pl.program_id(0)

    @pl.when(n == 0)
    def _():
        for k, x in enumerate((x0, x1, x2, x3)):
            xs[ROWS * k : ROWS * (k + 1), :] = x[...]

    gate = dot(xs[...], wg[...])
    up = dot(xs[...], wu[...])
    d = da[...]
    sg = jax.nn.sigmoid(gate)
    both = gate * sg
    a = (both * up).astype(BF)
    d_gate = (d * up * sg * (1.0 + gate * (1.0 - sg))).astype(BF)
    d_up = (d * both).astype(BF)
    for h in range(2):
        at = pl.multiple_of((h ^ (sc[2] & 1)) * 256, 256)
        for ref, tile in ((act, a), (dg, d_gate), (du, d_up)):
            ref[:, pl.ds(at, 256)] = tile[:, 256 * h : 256 * (h + 1)]
    dx = dot_t(d_gate, wg[...]) + dot_t(d_up, wu[...])

    @pl.when(n == 0)
    def _():
        acc[...] = dx

    @pl.when(n > 0)
    def _():
        total = acc[...] + dx
        for k in range(4):
            (keep, send)[k % 2][k // 2] = total[ROWS * k : ROWS * (k + 1), :].astype(BF)


def ffn(sc, xs, da, wg, wu):
    full = pl.BlockSpec((ROWS, D), lambda n, s: (0, 0))
    side = pl.BlockSpec((2, ROWS, D), lambda n, s: (0, 0, 0))
    cols = pl.BlockSpec((D, FBLOCK), lambda n, s: (0, n))
    rel = pl.BlockSpec((TOK, FBLOCK), lambda n, s: (0, n ^ (s[2] >> 1)))
    return pl.pallas_call(
        ffn_kernel,
        grid_spec=pltpu.PrefetchScalarGridSpec(
            num_scalar_prefetch=1,
            grid=(FS // FBLOCK,),
            in_specs=[full] * 4 + [pl.BlockSpec((TOK, FBLOCK), lambda n, s: (0, n)), cols, cols],
            out_specs=[rel, rel, rel, side, side],
            scratch_shapes=[pltpu.VMEM((TOK, D), BF), pltpu.VMEM((TOK, D), F32)],
        ),
        out_shape=[sds((TOK, FS))] * 3 + [sds((2, ROWS, D))] * 2,
        compiler_params=PARAMS,
        cost_estimate=cost(11),
    )(sc, *xs, da, wg, wu)


def mlp_out_kernel(sc, act, wd, keep, send):
    gz = sc[2]
    acts = [
        act[:, pl.ds(pl.multiple_of((b ^ gz) * 256, 256), 256)] for b in range(FS // 256)
    ]
    total = dot(jnp.concatenate(acts, axis=1), wd[...])
    for k in range(4):
        (keep, send)[k % 2][k // 2] = total[ROWS * k : ROWS * (k + 1)].astype(BF)


def ffn_grads_kernel(sc, x0, x1, x2, x3, y0, y1, y2, y3, act, dg, du, *refs):
    gy = sc[1]
    keeps, sends, ys = refs[:4], refs[4:8], refs[8]

    def put(p, ra, rb, at, tile):
        index = cube_index(p, (ra & 1, ra >> 1, rb & 1, rb >> 1))
        ref = (keeps, sends)[index >> 3][p]
        ref[index & 7, at : at + tile.shape[0], :] = tile.astype(BF)

    for ra in range(4):
        cols = pl.ds(pl.multiple_of((ra ^ gy) * DS, 128), DS)
        xa = jnp.concatenate([x[:, cols] for x in (x0, x1, x2, x3)], axis=0)
        for k, y in enumerate((y0, y1, y2, y3)):
            ys[ROWS * k : ROWS * (k + 1), DS * ra : DS * (ra + 1)] = y[:, cols]
        for n, d in enumerate((dg, du)):
            wide = t_dot(xa, d[...])
            for rb in range(4):
                for p in range(4):
                    lane, row = 256 * rb + 128 * (p // 2), 192 * (p % 2)
                    put(p, ra, rb, 192 * n, wide[row : row + 192, lane : lane + 128])
    for rb in range(4):
        wide = t_dot(act[:, 256 * rb : 256 * (rb + 1)], ys[...])
        for ra in range(4):
            for p in range(4):
                at = 384
                row = 192 * p
                while row < 192 * (p + 1):
                    lane, r = DS * ra + 128 * (row // 256), row % 256
                    size = min(256 - r, 192 * (p + 1) - row)
                    put(p, ra, rb, at, wide[r : r + size, lane : lane + 128])
                    at += size
                    row += size


OUT_ROWS = 288
OUT_SPLIT = (80, 80, 64, 64)
OUT_AT = (0, 80, 160, 224)
PART_ROWS = tuple(576 + n for n in OUT_SPLIT)
PART_AT = (0, 656, 1312, 1952)
GAIN_AT = 2592


def step_kernel(*refs):
    for p in range(4):
        kl, ku, gl, gu = refs[4 * p : 4 * p + 4]
        keep, send = refs[16 + 2 * p : 18 + 2 * p]
        keep[...] = (kl[...].astype(F32) + gl[...].astype(F32)).astype(BF)
        send[...] = (ku[...].astype(F32) + gu[...].astype(F32)).astype(BF)


def cube_step(keeps, gots, deps, us):
    half = keeps[0].shape[0] // 2
    lower = pl.BlockSpec((1, 576, 128), lambda n: (n, 0, 0))
    upper = pl.BlockSpec((1, 576, 128), lambda n: (n + half, 0, 0))

    def body(*refs):
        step_kernel(*refs[:16], *refs[16 + len(deps) :])

    args = []
    for k, g in zip(keeps, gots):
        args += [k, k, g, g]
    outs = pl.pallas_call(
        body,
        grid=(half,),
        in_specs=[lower, upper] * 8 + [ANY_SPEC] * len(deps),
        out_specs=[lower] * 8,
        out_shape=[sds((half, 576, 128))] * 8,
        compiler_params=PARAMS,
        cost_estimate=cost(us),
    )(*args, *deps)
    return outs[0::2], outs[1::2]


def last_step_kernel(k0, k1, k2, k3, g0, g1, g2, g3, out, total):
    for p, (k, g) in enumerate(((k0, g0), (k1, g1), (k2, g2), (k3, g3))):
        at = PART_AT[p]
        total[at : at + 576, :] = (k[0].astype(F32) + g[0].astype(F32)).astype(BF)
        total[at + 576 : at + PART_ROWS[p], :] = out[OUT_AT[p] : OUT_AT[p] + OUT_SPLIT[p]]
    total[GAIN_AT:, :] = out[OUT_ROWS:]


def join_kernel(own, got, p0, p1, p2, p3, gains):
    total = own[...].astype(F32) + got[...].astype(F32)
    for p, ref in enumerate((p0, p1, p2, p3)):
        ref[0] = total[PART_AT[p] : PART_AT[p] + PART_ROWS[p]].astype(BF)
    gains[...] = total[GAIN_AT:]


def stack_kernel(a0, a1, a2, a3, b0, b1, b2, b3, o0, o1, o2, o3):
    for a, b, o in ((a0, b0, o0), (a1, b1, o1), (a2, b2, o2), (a3, b3, o3)):
        o[0 : a.shape[0]] = a[...]
        o[a.shape[0] :] = b[...]


def cube_gather(owns, gots, us, deps):
    outs = [sds((2 * o.shape[0], *o.shape[1:])) for o in owns]
    return call(stack_kernel, outs, [], [*owns, *gots], us, deps=deps)


def pick(owns, gots, p, bits, rows):
    index = cube_index(p, bits)
    rest = index & 7
    return jnp.where(index >= 8, gots[p][rest, rows, :], owns[p][rest, rows, :])


def ffn_place_kernel(sc, *refs):
    owns, gots = refs[0:4], refs[4:8]
    gate, up, down, out, tmp = refs[8:]
    gy, gz = sc[1], sc[2]
    ra = pl.program_id(0) ^ gy
    for bb in range(4):
        rb = bb ^ gz
        bits = (ra & 1, ra >> 1, rb & 1, rb >> 1)
        for p in range(4):
            lane, row = 256 * bb + 128 * (p // 2), 192 * (p % 2)
            for n, ref in enumerate((gate, up)):
                tile = pick(owns, gots, p, bits, slice(192 * n, 192 * (n + 1)))
                ref[row : row + 192, lane : lane + 128] = tile.astype(F32)
            at, row = 384, 192 * p
            while row < 192 * (p + 1):
                lane, r = row // 256, row % 256
                size = min(256 - r, 192 * (p + 1) - row)
                tile = pick(owns, gots, p, bits, slice(at, at + size))
                down[256 * bb + r : 256 * bb + r + size, 128 * lane : 128 * (lane + 1)] = (
                    tile.astype(F32)
                )
                at += size
                row += size
            at = OUT_ROWS * (bb ^ (bb >> 1)) + OUT_AT[p]
            tile = pick(owns, gots, p, bits, slice(576, PART_ROWS[p]))
            tmp[at : at + OUT_SPLIT[p], :] = tile.astype(F32)
    for t in range(3):
        out[:, 128 * t : 128 * (t + 1)] = tmp[DS * t : DS * (t + 1), :]


def ffn_place(sc, owns, gots, deps):
    def body(*refs):
        ffn_place_kernel(*refs[:9], *refs[9 + len(deps) :])

    whole = [pl.BlockSpec((8, n, 128), lambda n, s: (0, 0, 0)) for n in PART_ROWS]
    rows = pl.BlockSpec((DS, FS), lambda n, s: (n, 0))
    return pl.pallas_call(
        body,
        grid_spec=pltpu.PrefetchScalarGridSpec(
            num_scalar_prefetch=1,
            grid=(4,),
            in_specs=whole * 2 + [ANY_SPEC] * len(deps),
            out_specs=[
                rows,
                rows,
                pl.BlockSpec((FS, DS), lambda n, s: (0, n)),
                pl.BlockSpec((DS, DS), lambda n, s: (0, n ^ (n >> 1))),
            ],
            scratch_shapes=[pltpu.VMEM((4 * OUT_ROWS, 128), F32)],
        ),
        out_shape=[sds((D, FS), F32), sds((D, FS), F32), sds((FS, D), F32), sds((DS, D), F32)],
        compiler_params=PARAMS,
        cost_estimate=cost(12),
    )(sc, *owns, *gots, *deps)


def out_grads_kernel(o, b0, b1, b2, b3, d_gain, pieces, tmp):
    bs = jnp.concatenate([b0[...], b1[...], b2[...], b3[...]], axis=0)
    for j in range(2):
        oj = jnp.concatenate([unfolded(o[2 * k + j]) for k in range(4)], axis=0)
        tmp[192 * j : 192 * (j + 1), :] = t_dot(oj, bs)
    for s in range(16):
        pieces[s, OUT_ROWS:, :] = d_gain[...]
        start, at = OUT_ROWS * s, 0
        while start < OUT_ROWS * (s + 1):
            lane, r = 128 * (start // DS), start % DS
            size = min(DS - r, OUT_ROWS * (s + 1) - start)
            pieces[s, at : at + size, :] = tmp[r : r + size, lane : lane + 128].astype(BF)
            at += size
            start += size


def sum_kernel(parts, out):
    out[...] = jnp.sum(parts[...].astype(F32), axis=0).astype(BF)


def repeat_kernel(part, out):
    for n in range(32):
        out[n] = part[...]


QKV_ROWS = 72
QKV_PAD = 80


def d_xa_kernel(sc, d_q, d_kv, q0, q1, q2, q3, k0, k1, k2, k3, cos, sin, lin, keep, send, dq, dkv):
    f = sc[0]
    co, si = cos[...], sin[...]

    def back(g):
        w = g * si
        turned = jnp.concatenate([w[:, HALF:], -w[:, :HALF]], axis=1)
        return (g * co + turned).astype(BF)

    for k in range(4):
        rows = slice(ROWS * k, ROWS * (k + 1))
        for j in range(2):
            i = 2 * k + j
            gq = unfold(d_q[i].astype(F32))
            gkv = d_kv[4 * i].astype(F32)
            for z in range(1, 4):
                gkv += d_kv[4 * i + z].astype(F32)
            gkv = unfold(gkv)
            for n in range(2):
                g = back(gq[:, 96 * n : 96 * (n + 1)])
                lin[rows, 384 * j + 96 * n : 384 * j + 96 * (n + 1)] = g
                dq[rows, 192 * j + 96 * n : 192 * j + 96 * (n + 1)] = g
            g = back(gkv[:, 0:96])
            lin[rows, 384 * j + 192 : 384 * j + 288] = g
            dkv[rows, 96 * j : 96 * (j + 1)] = g
            g = gkv[:, 96:192].astype(BF)
            lin[rows, 384 * j + 288 : 384 * j + 384] = g
            dkv[rows, 192 + 96 * j : 192 + 96 * (j + 1)] = g
    for k, (wq, wkv) in enumerate(((q0, k0), (q1, k1), (q2, k2), (q3, k3))):
        cols = pl.ds(pl.multiple_of((f ^ k) * DS, 128), DS)
        total = (dot_t(dq[...], wq[...]) + dot_t(dkv[...], wkv[0:DS])).astype(BF)
        for s in range(4):
            (keep, send)[s % 2][s // 2, :, cols] = total[ROWS * s : ROWS * (s + 1)]


def flat_pieces(n):
    out, start = [], QKV_ROWS * n
    while start < QKV_ROWS * (n + 1):
        r = start % DS
        size = min(DS - r, QKV_ROWS * (n + 1) - start)
        out.append((128 * (start // DS), r, size))
        start += size
    return out


def qkv_grads_kernel(xa, lin, pieces, tmp):
    zeros = jnp.zeros((QKV_PAD - QKV_ROWS, 128), F32)
    for g in range(4):
        tmp[...] = t_dot(xa[:, DS * g : DS * (g + 1)], lin[...])
        for n in range(32):
            tiles = [tmp[r : r + size, lane : lane + 128] for lane, r, size in flat_pieces(n)]
            pieces[n, g] = jnp.concatenate(tiles + [zeros], axis=0).astype(BF)


def attn_place_kernel(got, wq, wk, wv, gain_in, q, k, v, gain, tmp):
    for g in range(4):
        for n in range(32):
            tile, at = got[n, g].astype(F32), 0
            for lane, r, size in flat_pieces(n):
                tmp[r : r + size, lane : lane + 128] = tile[at : at + size]
                at += size
        for j in range(2):
            at = 384 * j
            q[:, 384 * g + 192 * j : 384 * g + 192 * (j + 1)] = tmp[:, at : at + 192]
            k[:, 192 * g + 96 * j : 192 * g + 96 * (j + 1)] = tmp[:, at + 192 : at + 288]
            v[:, 192 * g + 96 * j : 192 * g + 96 * (j + 1)] = tmp[:, at + 288 : at + 384]
    total = jnp.sum(wq[...].astype(F32) * q[...], axis=1, keepdims=True)
    total += jnp.sum(wk[...].astype(F32) * k[...], axis=1, keepdims=True)
    total += jnp.sum(wv[...].astype(F32) * v[...], axis=1, keepdims=True)
    gain[...] = total / gain_in[...]


def rope_tables(positions):
    freqs = ROPE_BASE ** (-jnp.arange(HALF).astype(F32) * 2.0 / HEAD_DIM)
    angles = positions.astype(F32)[:, None] * freqs[None, :]
    angles = jnp.concatenate([angles, angles], axis=1)
    return jnp.cos(angles), jnp.sin(angles)


def body(
    tokens,
    block_order,
    gain_attn,
    gain_mlp,
    w_query,
    w_key,
    w_value,
    w_out,
    w_gate,
    w_up,
    w_down,
    cotangent,
):
    y, xh, z = lax.axis_index("y"), lax.axis_index("xh"), lax.axis_index("z")
    xl, c = lax.axis_index("xl"), lax.axis_index("c")
    f = xl * 2 + c
    gy, gz = y ^ (y >> 1), z ^ (z >> 1)
    sc = jnp.stack([f, gy, gz]).astype(jnp.int32)
    own_x, own_dy = tokens[0], cotangent[0]

    place = (y * 2 + xh) * 4 + z
    own_blocks = lax.dynamic_slice_in_dim(block_order, 2 * place, 2)
    positions = (own_blocks[:, None] * BLOCK + jnp.arange(BLOCK)).reshape(-1)
    cos, sin = rope_tables(positions)
    blocks = block_order.reshape(8, 4, 2)
    key_blocks = jnp.stack(
        [
            lax.dynamic_index_in_dim(blocks, (z + m) % 4, axis=1, keepdims=False).reshape(-1)
            for m in range(4)
        ]
    ).reshape(-1)
    query_blocks = key_blocks[:16]

    xs = gather_slots(own_x)
    packs = call(
        pack_kernel,
        [sds((DS, DS))] * 4 + [sds((DS + 16, DS))] * 4,
        [sc],
        [w_query, w_key, w_value, jnp.pad(jnp.stack([gain_attn, gain_mlp]), ((0, 14), (0, 0)))],
        3,
        [pltpu.VMEM((4, DS, DS), BF)],
    )
    wkvs = (packs[4], swap_c(packs[5]), swap_xl(packs[6]), swap_far(packs[7], 1))
    wqs = (packs[0], swap_c(packs[1]), swap_far(packs[2], 0), swap_far(packs[3], 1))

    folded, heads = (8, 192, 128), ("y", "xh")
    xa, kv, gain_a, gain_m = call(
        kv_kernel,
        [sds((TOK, D)), sds(folded), sds((1, D), F32), sds((1, D), F32)],
        [sc],
        [*xs, *wkvs, cos, sin],
        5,
    )
    q = call(q_kernel, sds(folded), [sc], [xa, *wqs, cos, sin], 4)
    kv = exchange(kv, heads)
    kvs = shifts(kv, "z")
    q = exchange(q, heads)
    o, o2, q2, lse, kv_sorted = call(
        attention_kernel,
        [
            sds(folded),
            sds((16, ROWS, 128)),
            sds((16, ROWS, 128)),
            sds((16, ROWS, 8), F32),
            sds((SEQ, 256)),
        ],
        [query_blocks, key_blocks],
        [q, kv, *kvs],
        13,
    )
    o_tok = exchange(o, heads)

    dys = gather_slots(own_dy)
    d_act = call(d_act_kernel, sds((TOK, FS), F32), [], [*dys, w_down], 4, deps=[o])
    side = [sds((2, ROWS, D))] * 2
    keep, send = call(out_kernel, side, [], [o_tok, w_out], 2, deps=[d_act])
    terms, _ = scatter_slots(keep, send)
    hidden, xm = call(
        hidden_kernel, [sds((ROWS, D), F32), sds((ROWS, D))], [], [own_x, *terms, gain_m], 2
    )
    xms = gather_slots(xm)
    act, dg, du, keep, send = ffn(sc, xms, d_act, w_gate, w_up)
    terms, moving = scatter_slots(keep, send)

    grads = call(
        ffn_grads_kernel,
        [sds((8, 576, 128))] * 8,
        [sc],
        [*xms, *dys, act, dg, du],
        9,
        [pltpu.VMEM((TOK, D), BF)],
        [moving],
    )
    keeps, sends = grads[:4], grads[4:]
    gots = [swap_cube(s, p) for p, s in enumerate(sends)]
    d_hidden, d_br, d_gain = call(
        d_hidden_kernel,
        [sds((ROWS, D), F32), sds((ROWS, D)), sds((16, 128))],
        [],
        [own_dy, *terms, hidden, gain_m],
        2,
        deps=[sends[0]],
    )
    d_brs = gather_slots(d_br)
    d_o = call(d_o_kernel, sds(folded), [], [*d_brs, w_out], 2)
    d_o_att = exchange(d_o, heads)
    out_pieces = call(
        out_grads_kernel,
        sds((16, OUT_ROWS + 16, 128)),
        [],
        [o_tok, *d_brs, d_gain],
        2,
        [pltpu.VMEM((DS, D), F32)],
        [d_o],
    )
    keeps, sends = cube_step(keeps, gots, [out_pieces], 5)
    gots = [swap_cube(s, p + 1) for p, s in enumerate(sends)]
    out_got = exchange(out_pieces, ("y", "z"))
    dq2, dkv = call(
        attention_back_kernel,
        [sds((16, ROWS, 128)), sds((32, 192, 128))],
        [query_blocks, block_order],
        [q2, d_o_att, o2, lse, kv_sorted],
        24,
        [pltpu.VMEM((SEQ, 256), F32), pltpu.VMEM((16, ROWS, 96), BF)],
        [sends[0]],
    )
    dkv_tok = exchange(dkv, CTX)
    keeps, sends = cube_step(keeps, gots, [dq2], 4)
    gots = [swap_cube(s, p + 2) for p, s in enumerate(sends)]
    out_sum = call(
        sum_kernel, sds((OUT_ROWS + 16, 128)), [], [out_got], 2, deps=[sends[0]]
    )
    keeps, sends = cube_step(keeps, gots, [out_sum], 3)
    gots = [swap_cube(s, p + 3) for p, s in enumerate(sends)]
    dq = call(fold_dq_kernel, sds(folded), [], [dq2], 2, deps=[sends[0], dkv_tok])
    dq_tok = exchange(dq, heads)
    keep, send = call(mlp_out_kernel, side, [sc], [act, w_down], 5, deps=[dq])
    mlp_terms, _ = scatter_slots(keep, send)
    total = call(
        last_step_kernel, sds((GAIN_AT + 16, 128)), [], [*keeps, *gots, out_sum], 2, deps=[keep]
    )
    total_got = swap_e(total)

    lin, keep, send = call(
        d_xa_kernel,
        [sds((TOK, 768)), *side],
        [sc],
        [dq_tok, dkv_tok, *wqs, *wkvs, cos, sin],
        7,
        [pltpu.VMEM((TOK, DS), BF), pltpu.VMEM((TOK, DS), BF)],
        [total],
    )
    *owns, gains_sum = call(
        join_kernel,
        [sds((1, n, 128)) for n in PART_ROWS] + [sds((16, 128), F32)],
        [],
        [total, total_got],
        2,
        deps=[lin],
    )
    gots = [swap_cube(o, p + 3) for p, o in enumerate(owns)]
    terms, moving = scatter_slots(keep, send)
    pieces = call(
        qkv_grads_kernel,
        sds((32, 4, QKV_PAD, 128)),
        [],
        [xa, lin],
        5,
        [pltpu.VMEM((DS, 768), F32)],
        [owns[0]],
    )
    pieces_got = exchange(pieces, CTX)
    owns = cube_gather(owns, gots, 2, [pieces])
    gots = [swap_cube(o, p + 2) for p, o in enumerate(owns)]
    layer_out = call(
        layer_out_kernel, sds((ROWS, D)), [], [hidden, *mlp_terms], 2, deps=[owns[0]]
    )
    d_tokens = call(
        d_tokens_kernel,
        sds((ROWS, D), F32),
        [],
        [own_x, *terms, d_hidden, gain_a],
        2,
        deps=[layer_out],
    )
    owns = cube_gather(owns, gots, 3, [d_tokens])
    gots = [swap_cube(o, p + 1) for p, o in enumerate(owns)]

    part = call(sum_kernel, sds((4, QKV_PAD, 128)), [], [pieces_got], 3, deps=[owns[0]])
    owns = cube_gather(owns, gots, 5, [part])
    gots = [swap_cube(o, p) for p, o in enumerate(owns)]
    part = exchange(part, FSDP)
    parts = call(repeat_kernel, sds((32, 4, QKV_PAD, 128)), [], [part], 3, deps=[owns[0]])
    parts = exchange(parts, CTX)
    g_gain_m = gains_sum[0:12].reshape(4, DS)
    g_gain_m = [lax.dynamic_index_in_dim(g_gain_m, f ^ k, keepdims=False) for k in range(4)]
    g_gain_m = g_gain_m[0] + swap_c(g_gain_m[1]) + swap_xl(g_gain_m[2]) + swap_both(g_gain_m[3])
    g_query, g_key, g_value, g_gain_a = call(
        attn_place_kernel,
        [sds((DS, D), F32), sds((DS, 768), F32), sds((DS, 768), F32), sds((DS, 1), F32)],
        [],
        [parts, w_query, w_key, w_value, gain_attn.astype(F32).reshape(DS, 1)],
        5,
        [pltpu.VMEM((DS, 768), F32)],
    )
    g_gate, g_up, g_down, g_out = ffn_place(sc, owns, gots, [g_gain_a])

    return (
        layer_out[None],
        d_tokens[None],
        g_gain_a.reshape(DS),
        g_gain_m.reshape(DS),
        g_query,
        g_key,
        g_value,
        g_out,
        g_gate,
        g_up,
        g_down,
    )


def solution(mesh):
    cube = Mesh(mesh.devices.reshape(4, 2, 4, 2, 2), ("y", "xh", "z", "xl", "c"))
    fsdp, ctx = ("xl", "c"), ("y", "xh", "z")
    return jax.shard_map(
        body,
        mesh=cube,
        in_specs=(
            P(fsdp, ctx, None),
            P(),
            P(fsdp),
            P(fsdp),
            P(fsdp, None),
            P(fsdp, None),
            P(fsdp, None),
            P(fsdp, None),
            P(None, fsdp),
            P(None, fsdp),
            P(fsdp, None),
            P(fsdp, ctx, None),
        ),
        out_specs=(
            P(fsdp, ctx, None),
            P(fsdp, ctx, None),
            P(fsdp),
            P(fsdp),
            P(fsdp, None),
            P(fsdp, None),
            P(fsdp, None),
            P(fsdp, None),
            P(None, fsdp),
            P(None, fsdp),
            P(fsdp, None),
        ),
        check_vma=False,
    )
```

time: 614 us -> 516 us (0.84)
  Pallas kernels: 133 us -> 175 us
  other arithmetic: 49.8 us -> 9.65 us
  waiting for transfers between devices: 203 us -> 166 us
  blocking collectives: 33.1 us -> 0 us
  starting transfers between devices: 148 us -> 128 us
    all_to_all x2 -> x10, starting transfers between devices: 10.1 us -> 58.7 us  [exchange(): return lax.all_to_all(x, axes, 0, 0, tiled=True)]
    pallas_call x12 -> x31, Pallas kernels: 113 us -> 161 us  [the longest x27 136 us: call(): pl.pallas_call(body, out_shape=outs, in_specs=[SMEM_SPEC] * len(smem) + [...]
    ppermute x64 -> x32, starting transfers between devices: 91.8 us -> 43.8 us  [swap_cube(): return lax.ppermute(x, axis, pairs)]
    ppermute x64 -> x32, waiting for transfers between devices: 119 us -> 73.6 us  [swap_cube(): return lax.ppermute(x, axis, pairs)]
    all_to_all x2 -> x0, blocking collectives: 33.1 us -> none  [exchange(): return lax.all_to_all(x, ('y', 'xh'), 0, 0, tiled=True).reshape(shape)]
    concatenate x28 -> x0, other arithmetic: 22.1 us -> none  [the longest x24 20.9 us: cube_gather(): owns[p] = jnp.concatenate([owns[p], gots[p]], axis=0)]
    ppermute x12 -> x10, waiting for transfers between devices: 52.1 us -> 33 us  [swap_xl(): return lax.ppermute(x, 'xl', [(0, 1), (1, 0)])]
    ppermute x2 -> x1, waiting for transfers between devices: 0.01 us -> 18.9 us  [swap_both(): return lax.ppermute(x, ('xl', 'c'), [(i, i ^ 3) for i in range(4)])]
  transfers between devices with their start and end apart: 112 -> 75, of which waited for: 43 -> 34; matrix products, arithmetic and copies ran while one was open for 10% -> 2% of each run, Pallas kernels for 12% -> 26%
where the time goes in v2:
time: 516 us; the launch traced here: 507 us
  Pallas kernels  175 us (34%)
  waiting for transfers between devices  166 us (32%)
  starting transfers between devices  128 us (25%)
  local copies, waits for them, and re-layouts  27 us (5%)
  other arithmetic  9.65 us (2%)
    pallas_call x27, Pallas kernels, call(): pl.pallas_call(body, out_shape=outs, in_specs=[SMEM_SPEC] * len(smem) + [...  136 us
    ppermute x32, waiting for transfers between devices, swap_cube(): return lax.ppermute(x, axis, pairs)  73.6 us
    all_to_all x10, starting transfers between devices, exchange(): return lax.all_to_all(x, axes, 0, 0, tiled=True)  58.7 us
    ppermute x32, starting transfers between devices, swap_cube(): return lax.ppermute(x, axis, pairs)  43.8 us
    ppermute x10, waiting for transfers between devices, swap_xl(): return lax.ppermute(x, 'xl', [(0, 1), (1, 0)])  33 us
    unnamed x120, local copies, waits for them, and re-layouts  21.9 us
    ppermute x1, waiting for transfers between devices, swap_both(): return lax.ppermute(x, ('xl', 'c'), [(i, i ^ 3) for i in range(4)])  18.9 us
    all_to_all x10, waiting for transfers between devices, exchange(): return lax.all_to_all(x, axes, 0, 0, tiled=True)  17.9 us
  transfers between devices with their start and end apart: 75, of which 34 were waited for; matrix products, arithmetic and copies ran while one was open for 2% of the time, Pallas kernels for 26%

profile of v2, /device:TPU:32, one launch (start us, length us, event | category | flops | bytes accessed | tf_op | source)
XLA Modules:
  0.0 506.8 jit_solution(13863673696528582023)
XLA Ops:
  4.8 3.3 shard_map.203
  13.3 5.1 %collective-permute-done.4.refs_7_.refs_9_ = bf16[400,384]{1,0:T(8,128)(2,1)S(1)} collective-permute-done((bf16[400,384]{1,0:T(8,128)(2,1)}, bf16[400,384]{1,0:T(8,128)(2,1)S(1)}, u32[]{:S(2)}, u32[]{:S(2)}) %collective-permute-start.4) | collective-permute-done | bytes 307232 | tf_op jit(solution)/shard_map/ppermute | solution.py:84
  21.0 5.1 shard_map.204
  26.0 5.8 %all-to-all-start.1 = ((bf16[8,192,128]{2,1,0:T(8,128)(2,1)}), bf16[8,192,128]{2,1,0:T(8,128)(2,1)S(1)}, u32[]{:S(2)}, u32[]{:S(2)}) async-start(bf16[8,192,128]{2,1,0:T(8,128)(2,1)} %get-tuple-element.113), calls=%async_computation.1 | async-start | bytes 786432 | tf_op jit(solution)/shard_map/all_to_all | solution.py:146
  31.8 4.5 collective-permute-start.7
  36.4 5.9 %all-to-all-done.1.refs_3_ = bf16[8,192,128]{2,1,0:T(8,128)(2,1)S(1)} async-done(((bf16[8,192,128]{2,1,0:T(8,128)(2,1)}), bf16[8,192,128]{2,1,0:T(8,128)(2,1)S(1)}, u32[]{:S(2)}, u32[]{:S(2)}) %all-to-all-start.1) | async-done | bytes 393248 | tf_op jit(solution)/shard_map/all_to_all | solution.py:146
  47.9 4.8 collective-permute-done.8.refs_5_.refs_6_
  53.4 4.6 shard_map.205
  58.0 4.8 all-to-all-start
  66.4 6.4 %all-to-all-done.refs_2_ = bf16[8,192,128]{2,1,0:T(8,128)(2,1)S(1)} async-done(((bf16[8,192,128]{2,1,0:T(8,128)(2,1)}), bf16[8,192,128]{2,1,0:T(8,128)(2,1)S(1)}, u32[]{:S(2)}, u32[]{:S(2)}) %all-to-all-start) | async-done | bytes 393248 | tf_op jit(solution)/shard_map/all_to_all | solution.py:146
  74.6 14.0 %shard_map.206 = (bf16[8,192,128]{2,1,0:T(8,128)(2,1)}, bf16[16,128,128]{2,1,0:T(8,128)(2,1)}, bf16[16,128,128]{2,1,0:T(8,128)(2,1)}, f32[16,128,8]{2,1,0:T(8,128)}, bf16[4096,256]{1,0:T(8,128)(2,1)}) custom-call(s32[16]{0:T(128)} %slice.31.refs_0_, s32[64]{0:T(128)} %reshape.86.refs_1_, bf16[8,192,128]{2,1,0:T(8,128)(2,1)} %copy-done.5, ...), custom_call_target="tpu_custom_call" | custom-call | flops 14300000256 | bytes 39000000 | tf_op jit(solution)/shard_map/pallas_call | solution.py:52
  88.6 3.5 all-to-all-start.2
  92.9 5.5 %shard_map.207.refs_2_.da = f32[512,1024]{1,0:T(8,128)} custom-call(bf16[128,1536]{1,0:T(8,128)(2,1)} %bitcast.19, bf16[128,1536]{1,0:T(8,128)(2,1)} %copy-done.25, bf16[128,1536]{1,0:T(8,128)(2,1)} %copy-done.24, bf16[128,1536]{1,0:T(8,128)(2,1)} %collective-permute-done.14.refs_3_.refs_8_, bf16[1024,1536]{1,0:T(8,128)(2,1)} %refs_2_.4, ...), custom_call_target="tpu_custom_call" | custom-call | flops 4400000000 | bytes 12000000 | tf_op jit(solution)/shard_map/pallas_call | solution.py:52
  98.4 3.1 all-to-all-done.2.refs_0_
  102.3 3.3 shard_map.208
  105.6 2.5 collective-permute-done.15.refs_2_
  111.3 9.4 %collective-permute-done.16.refs_3_ = bf16[128,1536]{1,0:T(8,128)(2,1)S(1)} collective-permute-done((bf16[128,1536]{1,0:T(8,128)(2,1)S(1)}, bf16[128,1536]{1,0:T(8,128)(2,1)S(1)}, u32[]{:S(2)}, u32[]{:S(2)}) %collective-permute-start.16) | collective-permute-done | bytes 393248 | tf_op jit(solution)/shard_map/ppermute | solution.py:84
  121.5 2.9 shard_map.209
  126.2 8.9 %collective-permute-done.18.x2.refs_3_ = bf16[128,1536]{1,0:T(8,128)(2,1)S(1)} collective-permute-done((bf16[128,1536]{1,0:T(8,128)(2,1)}, bf16[128,1536]{1,0:T(8,128)(2,1)S(1)}, u32[]{:S(2)}, u32[]{:S(2)}) %collective-permute-start.18) | collective-permute-done | bytes 393248 | tf_op jit(solution)/shard_map/ppermute | solution.py:84
  137.5 13.5 %shard_map.210 = (bf16[512,1024]{1,0:T(8,128)(2,1)}, bf16[512,1024]{1,0:T(8,128)(2,1)}, bf16[512,1024]{1,0:T(8,128)(2,1)}, bf16[2,128,1536]{2,1,0:T(8,128)(2,1)}, bf16[2,128,1536]{2,1,0:T(8,128)(2,1)}) custom-call(s32[3]{0:T(128)} %pad_add_fusion.1.refs_0_.sc, bf16[128,1536]{1,0:T(8,128)(2,1)} %get-tuple-element.119.x0.refs_1_, ...), custom_call_target="tpu_custom_call" | custom-call | flops 12099999744 | bytes 33000000 | tf_op jit(solution)/shard_map/pallas_call | solution.py:497
  157.1 11.1 %shard_map.211 = (bf16[8,576,128]{2,1,0:T(8,128)(2,1)}, bf16[8,576,128]{2,1,0:T(8,128)(2,1)}, bf16[8,576,128]{2,1,0:T(8,128)(2,1)}, bf16[8,576,128]{2,1,0:T(8,12...) custom-call(s32[3]{0:T(128)} %pad_add_fusion.1.refs_0_.sc, ...), custom_call_target="tpu_custom_call" | custom-call | flops 9900000256 | bytes 27000000 | tf_op jit(solution)/shard_map/pallas_call | solution.py:52
  169.0 3.7 shard_map.212
  174.0 3.7 collective-permute-start.28
  177.7 6.1 %collective-permute-done.23.refs_2_.refs_3_ = bf16[128,1536]{1,0:T(8,128)(2,1)S(1)} collective-permute-done((bf16[128,1536]{1,0:T(8,128)(2,1)}, bf16[128,1536]{1,0:T(8,128)(2,1)S(1)}, u32[]{:S(2)}, u32[]{:S(2)}) %collective-permute-start.23) | collective-permute-done | bytes 393248 | tf_op jit(solution)/shard_map/ppermute | solution.py:84
  186.5 4.2 shard_map.213.refs_6_
  190.7 5.4 %all-to-all-start.3 = ((bf16[8,192,128]{2,1,0:T(8,128)(2,1)}), bf16[8,192,128]{2,1,0:T(8,128)(2,1)S(1)}, u32[]{:S(2)}, u32[]{:S(2)}) async-start(bf16[8,192,128]{2,1,0:T(8,128)(2,1)} %shard_map.213.refs_6_), calls=%async_computation.3 | async-start | bytes 786432 | tf_op jit(solution)/shard_map/all_to_all | solution.py:146
  196.1 3.4 shard_map.214.refs_16_
  199.5 3.8 collective-permute-done.26.refs_6_.refs_7_
  203.9 10.1 %collective-permute-done.25.refs_2_.refs_3_ = bf16[8,576,128]{2,1,0:T(8,128)(2,1)} collective-permute-done((bf16[8,576,128]{2,1,0:T(8,128)(2,1)S(1)}, bf16[8,576,128]{2,1,0:T(8,128)(2,1)}, u32[]{:S(2)}, u32[]{:S(2)}) %collective-permute-start.25) | collective-permute-done | bytes 1179680 | tf_op jit(solution)/shard_map/ppermute | solution.py:111
  214.0 6.4 %shard_map.215 = (bf16[4,576,128]{2,1,0:T(8,128)(2,1)}, bf16[4,576,128]{2,1,0:T(8,128)(2,1)}, bf16[4,576,128]{2,1,0:T(8,128)(2,1)}, bf16[4,576,128]{2,1,0:T(8,12...) custom-call(bf16[8,576,128]{2,1,0:T(8,128)(2,1)} %get-tuple-element., ...), custom_call_target="tpu_custom_call" | custom-call | flops 5500000256 | bytes 15000000 | tf_op jit(solution)/shard_map/pallas_call | solution.py:583
  220.5 3.7 collective-permute-start.31
  225.7 5.6 %all-to-all-start.4 = ((bf16[16,304,128]{2,1,0:T(8,128)(2,1)}), bf16[16,304,128]{2,1,0:T(8,128)(2,1)S(1)}, u32[]{:S(2)}, u32[]{:S(2)}) async-start(bf16[16,304,128]{2,1,0:T(8,128)(2,1)} %shard_map.214.refs_16_), calls=%async_computation.4 | async-start | bytes 2490368 | tf_op jit(solution)/shard_map/all_to_all | solution.py:146
  231.4 22.4 %shard_map.216 = (bf16[16,128,128]{2,1,0:T(8,128)(2,1)}, bf16[32,192,128]{2,1,0:T(8,128)(2,1)}) custom-call(s32[16]{0:T(128)} %slice.31.refs_0_, s32[64]{0:T(128)} %refs_1_.6, bf16[16,128,128]{2,1,0:T(8,128)(2,1)} %get-tuple-element.121.refs_2_, bf16[8,192,128]{2,1,0:T(8,128)(2,1)} %copy-done.7, bf16[16,128,128]{2,1,0:T(8,128)(2,1)} %get-tuple-element.128.refs_4_, ...), custom_call_target="tpu_custom_call" | custom-call | flops 26400000000 | bytes 72000000 | tf_op jit(solution)/shard_map/pallas_call | solution.py:52
  254.8 8.8 %all-to-all-start.5 = ((bf16[32,192,128]{2,1,0:T(8,128)(2,1)}), bf16[32,192,128]{2,1,0:T(8,128)(2,1)S(1)}, u32[]{:S(2)}, u32[]{:S(2)}) async-start(bf16[32,192,128]{2,1,0:T(8,128)(2,1)} %get-tuple-element.157), calls=%async_computation.5 | async-start | bytes 3145728 | tf_op jit(solution)/shard_map/all_to_all | solution.py:146
  264.4 3.6 shard_map.217
  277.0 9.0 %collective-permute-done.34.refs_6_.refs_7_ = bf16[2,576,128]{2,1,0:T(8,128)(2,1)S(1)} collective-permute-done((bf16[2,576,128]{2,1,0:T(8,128)(2,1)}, bf16[2,576,128]{2,1,0:T(8,128)(2,1)S(1)}, u32[]{:S(2)}, u32[]{:S(2)}) %collective-permute-start.34) | collective-permute-done | bytes 294944 | tf_op jit(solution)/shard_map/ppermute | solution.py:111
  287.0 2.7 shard_map.219
  298.1 4.7 all-to-all-start.6
  302.8 5.1 %shard_map.221 = (bf16[2,128,1536]{2,1,0:T(8,128)(2,1)}, bf16[2,128,1536]{2,1,0:T(8,128)(2,1)}) custom-call(s32[3]{0:T(128)} %pad_add_fusion.1.refs_0_.sc, bf16[512,1024]{1,0:T(8,128)(2,1)} %get-tuple-element.120.refs_9_.refs_1_, bf16[1024,1536]{1,0:T(8,128)(2,1)} %refs_2_.4, bf16[8,192,128]{2,1,0:T(8,128)(2,1)} %shard_map.220.refs_3_), custom_call_target="tpu_custom_call" | custom-call | flops 5500000256 | bytes 15000000 | tf_op jit(solution)/shard_map/pallas_call | solution.py:52
  311.1 3.5 collective-permute-start.43
  315.6 6.8 %shard_map.223 = (bf16[512,768]{1,0:T(8,128)(2,1)}, bf16[2,128,1536]{2,1,0:T(8,128)(2,1)}, bf16[2,128,1536]{2,1,0:T(8,128)(2,1)}) custom-call(s32[3]{0:T(128)} %pad_add_fusion.1.refs_0_.sc, bf16[8,192,128]{2,1,0:T(8,128)(2,1)} %copy-done.8, bf16[32,192,128]{2,1,0:T(8,128)(2,1)} %copy-done.2, bf16[384,384]{1,0:T(8,128)(2,1)} %get-tuple-element.109.refs_2_.refs_3_, ...), custom_call_target="tpu_custom_call" | custom-call | flops 7699999744 | bytes 21000000 | tf_op jit(solution)/shard_map/pallas_call | solution.py:52
  322.9 5.3 %collective-permute-done.43.refs_1_ = bf16[2608,128]{1,0:T(8,128)(2,1)S(1)} collective-permute-done((bf16[2608,128]{1,0:T(8,128)(2,1)}, bf16[2608,128]{1,0:T(8,128)(2,1)S(1)}, u32[]{:S(2)}, u32[]{:S(2)}) %collective-permute-start.43) | collective-permute-done | bytes 667680 | tf_op jit(solution)/shard_map/ppermute | solution.py:101
  331.2 4.5 shard_map.225.refs_8_
  335.7 10.0 %all-to-all-start.7 = ((bf16[32,4,80,128]{3,2,1,0:T(8,128)(2,1)}), bf16[32,4,80,128]{3,2,1,0:T(8,128)(2,1)S(1)}, u32[]{:S(2)}, u32[]{:S(2)}) async-start(bf16[32,4,80,128]{3,2,1,0:T(8,128)(2,1)} %shard_map.225.refs_8_), calls=%async_computation.7 | async-start | bytes 5242880 | tf_op jit(solution)/shard_map/all_to_all | solution.py:146
  347.3 2.7 collective-permute-start.46
  355.3 22.5 %collective-permute-done.46.refs_6_ = bf16[1,640,128]{2,1,0:T(8,128)(2,1)S(1)} collective-permute-done((bf16[1,640,128]{2,1,0:T(8,128)(2,1)}, bf16[1,640,128]{2,1,0:T(8,128)(2,1)S(1)}, u32[]{:S(2)}, u32[]{:S(2)}) %collective-permute-start.46) | collective-permute-done | bytes 163872 | tf_op jit(solution)/shard_map/ppermute | solution.py:111
  380.6 2.5 shard_map.226
  385.6 3.0 collective-permute-start.50
  388.5 2.6 shard_map.227.refs_6_
  391.9 3.2 shard_map.228.refs_8_
  396.8 3.2 shard_map.229
  405.7 2.7 shard_map.230.refs_8_
  408.4 3.3 all-to-all-start.8
  411.7 5.6 %collective-permute-done.56.refs_6_ = bf16[4,640,128]{2,1,0:T(8,128)(2,1)} collective-permute-done((bf16[4,640,128]{2,1,0:T(8,128)(2,1)}, bf16[4,640,128]{2,1,0:T(8,128)(2,1)}, u32[]{:S(2)}, u32[]{:S(2)}) %collective-permute-start.56) | collective-permute-done | bytes 655392 | tf_op jit(solution)/shard_map/ppermute | solution.py:111
  419.0 5.0 shard_map.231
  424.6 2.7 shard_map.232
  427.4 6.9 %all-to-all-start.9 = ((bf16[32,4,80,128]{3,2,1,0:T(8,128)(2,1)}), bf16[32,4,80,128]{3,2,1,0:T(8,128)(2,1)S(1)}, u32[]{:S(2)}, u32[]{:S(2)}) async-start(bf16[32,4,80,128]{3,2,1,0:T(8,128)(2,1)} %shard_map.232), calls=%async_computation.9 | async-start | bytes 5242880 | tf_op jit(solution)/shard_map/all_to_all | solution.py:146
  434.2 2.8 collective-permute-start.62
  441.2 18.9 %collective-permute-done.60 = f32[384]{0:T(512)S(1)} collective-permute-done((f32[384]{0:T(512)S(1)}, f32[384]{0:T(512)S(1)}, u32[]{:S(2)}, u32[]{:S(2)}) %collective-permute-start.60) | collective-permute-done | bytes 1568 | tf_op jit(solution)/shard_map/ppermute | solution.py:88
  460.9 2.8 collective-permute-done.59
  464.3 2.4 all-to-all-done.9.refs_0_
  468.2 5.6 %shard_map.233 = (f32[384,1536]{1,0:T(8,128)}, f32[384,768]{1,0:T(8,128)}, f32[384,768]{1,0:T(8,128)}, f32[384,1]{1,0:T(8,128)}) custom-call(bf16[32,4,80,128]{3,2,1,0:T(8,128)(2,1)} %copy-done.1, bf16[384,1536]{1,0:T(8,128)(2,1)} %refs_1_.7, bf16[384,768]{1,0:T(8,128)(2,1)} %refs_2_.5, bf16[384,768]{1,0:T(8,128)(2,1)} %refs_3_.3, f32[384,1]{1,0:T(8,128)} %reshape.93.refs_4_), custom_call_target="tpu_custom_call" | custom-call | flops 5500000256 | bytes 15000000 | tf_op jit(solution)/shard_map/pallas_call | solution.py:52
  475.5 14.7 %collective-permute-done.63.refs_7_ = bf16[8,640,128]{2,1,0:T(8,128)(2,1)} collective-permute-done((bf16[8,640,128]{2,1,0:T(8,128)(2,1)}, bf16[8,640,128]{2,1,0:T(8,128)(2,1)}, u32[]{:S(2)}, u32[]{:S(2)}) %collective-permute-start.63) | collective-permute-done | bytes 1310752 | tf_op jit(solution)/shard_map/ppermute | solution.py:111
  493.7 12.6 %shard_map.234 = (f32[1536,1024]{1,0:T(8,128)}, f32[1536,1024]{1,0:T(8,128)}, f32[1024,1536]{1,0:T(8,128)}, f32[384,1536]{1,0:T(8,128)}) custom-call(s32[3]{0:T(128)} %pad_add_fusion.1.refs_0_.sc, bf16[8,656,128]{2,1,0:T(8,128)(2,1)} %get-tuple-element.184.refs_1_, bf16[8,656,128]{2,1,0:T(8,128)(2,1)} %get-tuple-element.190.refs_2_, ...), custom_call_target="tpu_custom_call" | custom-call | flops 13200000000 | bytes 36000000 | tf_op jit(solution)/shard_map/pallas_call | solution.py:663
  (267 shorter events, 108.8 us)
Async XLA Ops:
  0.6 11.5 %collective-permute-start.1 = (bf16[128,1536]{1,0:T(8,128)(2,1)}, bf16[128,1536]{1,0:T(8,128)(2,1)S(1)}, u32[]{:S(2)}, u32[]{:S(2)}) collective-permute-start(bf16[128,1536]{1,0:T(8,128)(2,1)} %bitcast.24), channel_id=1, source_target_pairs={{0,2},{2,0},{1,3},{3,1},{4,6},{6,4},{5,7},{7,5},{8,10},{10,8},{9,1... | collective-permute-start | bytes 1179656 | tf_op jit(solution)/shard_map/ppermute | solution.py:84
  2.2 17.8 %collective-permute-start = (bf16[128,1536]{1,0:T(8,128)(2,1)}, bf16[128,1536]{1,0:T(8,128)(2,1)S(1)}, u32[]{:S(2)}, u32[]{:S(2)}) collective-permute-start(bf16[128,1536]{1,0:T(8,128)(2,1)} %bitcast.25), channel_id=1, source_target_pairs={{0,1},{1,0},{2,3},{3,2},{4,5},{5,4},{6,7},{7,6},{8,9},{9,8},{10,11... | collective-permute-start | bytes 1179656 | tf_op jit(solution)/shard_map/ppermute | solution.py:80
  9.1 10.9 %collective-permute-start.5 = (bf16[400,384]{1,0:T(8,128)(2,1)}, bf16[400,384]{1,0:T(8,128)(2,1)S(1)}, u32[]{:S(2)}, u32[]{:S(2)}) collective-permute-start(bf16[400,384]{1,0:T(8,128)(2,1)} %get-tuple-element.107), channel_id=1, source_target_pairs={{0,19},{1,18},{2,17},{3,16},{16,3},{17,2},{18,1},{19,0},{4,23},{5,... | collective-permute-start | bytes 921608 | tf_op jit(solution)/shard_map/ppermute | solution.py:97
  26.0 16.3 %all-to-all-start.1 = ((bf16[8,192,128]{2,1,0:T(8,128)(2,1)}), bf16[8,192,128]{2,1,0:T(8,128)(2,1)S(1)}, u32[]{:S(2)}, u32[]{:S(2)}) async-start(bf16[8,192,128]{2,1,0:T(8,128)(2,1)} %get-tuple-element.113), calls=%async_computation.1 | async-start | bytes 786432 | tf_op jit(solution)/shard_map/all_to_all | solution.py:146
  31.8 12.4 %collective-permute-start.6 = (bf16[384,384]{1,0:T(8,128)(2,1)}, bf16[384,384]{1,0:T(8,128)(2,1)S(1)}, u32[]{:S(2)}, u32[]{:S(2)}) collective-permute-start(bf16[384,384]{1,0:T(8,128)(2,1)} %get-tuple-element.110), channel_id=1, source_target_pairs={{0,1},{1,0},{2,3},{3,2},{4,5},{5,4},{6,7},{7,6},{8,9},{9,8},{10,11... | collective-permute-start | bytes 884744 | tf_op jit(solution)/shard_map/ppermute | solution.py:80
  31.8 14.6 %collective-permute-start.7 = (bf16[384,384]{1,0:T(8,128)(2,1)S(1)}, bf16[384,384]{1,0:T(8,128)(2,1)S(1)}, u32[]{:S(2)}, u32[]{:S(2)}) collective-permute-start(bf16[384,384]{1,0:T(8,128)(2,1)S(1)} %copy-done.48), channel_id=1, source_target_pairs={{0,18},{1,19},{2,16},{3,17},{16,2},{17,3},{18,0},{19,1},{4,22},{5,... | collective-permute-start | bytes 884744 | tf_op jit(solution)/shard_map/ppermute | solution.py:97
  36.4 16.4 %collective-permute-start.8 = (bf16[384,384]{1,0:T(8,128)(2,1)}, bf16[384,384]{1,0:T(8,128)(2,1)S(1)}, u32[]{:S(2)}, u32[]{:S(2)}) collective-permute-start(bf16[384,384]{1,0:T(8,128)(2,1)} %get-tuple-element.112), channel_id=1, source_target_pairs={{0,19},{1,18},{2,17},{3,16},{16,3},{17,2},{18,1},{19,0},{4,23},{5,... | collective-permute-start | bytes 884744 | tf_op jit(solution)/shard_map/ppermute | solution.py:97
  36.4 29.3 %collective-permute-start.13 = (bf16[128,1536]{1,0:T(8,128)(2,1)S(1)}, bf16[128,1536]{1,0:T(8,128)(2,1)S(1)}, u32[]{:S(2)}, u32[]{:S(2)}) collective-permute-start(bf16[128,1536]{1,0:T(8,128)(2,1)S(1)} %bitcast.22), channel_id=1, source_target_pairs={{0,2},{2,0},{1,3},{3,1},{4,6},{6,4},{5,7},{7,5},{8,10},{10,8},{9,1... | collective-permute-start | bytes 1179656 | tf_op jit(solution)/shard_map/ppermute | solution.py:84
  42.3 30.5 %collective-permute-start.11 = (bf16[8,192,128]{2,1,0:T(8,128)(2,1)S(1)}, bf16[8,192,128]{2,1,0:T(8,128)(2,1)S(1)}, u32[]{:S(2)}, u32[]{:S(2)}) collective-permute-start(bf16[8,192,128]{2,1,0:T(8,128)(2,1)S(1)} %all-to-all-done.1.refs_3_), channel_id=1, source_target_pairs={{12,0},{0,4},{4,8},{8,12},{13,1},{1,5},{5,9},{9,13},{14,2},{2,6},{... | collective-permute-start | bytes 1179656 | tf_op jit(solution)/shard_map/ppermute | solution.py:142
  44.2 28.6 %collective-permute-start.10 = (bf16[8,192,128]{2,1,0:T(8,128)(2,1)S(1)}, bf16[8,192,128]{2,1,0:T(8,128)(2,1)S(1)}, u32[]{:S(2)}, u32[]{:S(2)}) collective-permute-start(bf16[8,192,128]{2,1,0:T(8,128)(2,1)S(1)} %all-to-all-done.1.refs_3_), channel_id=1, source_target_pairs={{8,0},{12,4},{0,8},{4,12},{9,1},{13,5},{1,9},{5,13},{10,2},{14,6},... | collective-permute-start | bytes 1179656 | tf_op jit(solution)/shard_map/ppermute | solution.py:142
  46.4 26.4 %collective-permute-start.9 = (bf16[8,192,128]{2,1,0:T(8,128)(2,1)S(1)}, bf16[8,192,128]{2,1,0:T(8,128)(2,1)S(1)}, u32[]{:S(2)}, u32[]{:S(2)}) collective-permute-start(bf16[8,192,128]{2,1,0:T(8,128)(2,1)S(1)} %all-to-all-done.1.refs_3_), channel_id=1, source_target_pairs={{4,0},{8,4},{12,8},{0,12},{5,1},{9,5},{13,9},{1,13},{6,2},{10,6},{... | collective-permute-start | bytes 1179656 | tf_op jit(solution)/shard_map/ppermute | solution.py:142
  58.0 14.8 %all-to-all-start = ((bf16[8,192,128]{2,1,0:T(8,128)(2,1)}), bf16[8,192,128]{2,1,0:T(8,128)(2,1)S(1)}, u32[]{:S(2)}, u32[]{:S(2)}) async-start(bf16[8,192,128]{2,1,0:T(8,128)(2,1)} %shard_map.205), calls=%async_computation | async-start | bytes 786432 | tf_op jit(solution)/shard_map/all_to_all | solution.py:146
  62.8 29.3 %collective-permute-start.12 = (bf16[128,1536]{1,0:T(8,128)(2,1)S(1)}, bf16[128,1536]{1,0:T(8,128)(2,1)S(1)}, u32[]{:S(2)}, u32[]{:S(2)}) collective-permute-start(bf16[128,1536]{1,0:T(8,128)(2,1)S(1)} %bitcast.23), channel_id=1, source_target_pairs={{0,1},{1,0},{2,3},{3,2},{4,5},{5,4},{6,7},{7,6},{8,9},{9,8},{10,11... | collective-permute-start | bytes 1179656 | tf_op jit(solution)/shard_map/ppermute | solution.py:80
  65.7 26.4 %collective-permute-start.14 = (bf16[128,1536]{1,0:T(8,128)(2,1)S(1)}, bf16[128,1536]{1,0:T(8,128)(2,1)}, u32[]{:S(2)}, u32[]{:S(2)}) collective-permute-start(bf16[128,1536]{1,0:T(8,128)(2,1)S(1)} %collective-permute-done.13.refs_2_.refs_7_), channel_id=1, source_target_pairs={{0,1},{1,0},{2,3},{3,2},{4,5},{5,4},{6,7},{7,6},{8,9},{9,8},{10,11... | collective-permute-start | bytes 1179656 | tf_op jit(solution)/shard_map/ppermute | solution.py:80
  88.6 12.9 %all-to-all-start.2 = ((bf16[8,192,128]{2,1,0:T(8,128)(2,1)}), bf16[8,192,128]{2,1,0:T(8,128)(2,1)S(1)}, u32[]{:S(2)}, u32[]{:S(2)}) async-start(bf16[8,192,128]{2,1,0:T(8,128)(2,1)} %get-tuple-element.114.refs_5_), calls=%async_computation.2 | async-start | bytes 786432 | tf_op jit(solution)/shard_map/all_to_all | solution.py:146
  109.4 11.3 %collective-permute-start.16 = (bf16[128,1536]{1,0:T(8,128)(2,1)S(1)}, bf16[128,1536]{1,0:T(8,128)(2,1)S(1)}, u32[]{:S(2)}, u32[]{:S(2)}) collective-permute-start(bf16[128,1536]{1,0:T(8,128)(2,1)S(1)} %fusion), channel_id=1, source_target_pairs={{0,2},{2,0},{1,3},{3,1},{4,6},{6,4},{5,7},{7,5},{8,10},{10,8},{9,1... | collective-permute-start | bytes 1179656 | tf_op jit(solution)/shard_map/ppermute | solution.py:84
  124.4 10.6 %collective-permute-start.18 = (bf16[128,1536]{1,0:T(8,128)(2,1)}, bf16[128,1536]{1,0:T(8,128)(2,1)S(1)}, u32[]{:S(2)}, u32[]{:S(2)}) collective-permute-start(bf16[128,1536]{1,0:T(8,128)(2,1)} %get-tuple-element.119.x0.refs_1_), channel_id=1, source_target_pairs={{0,2},{2,0},{1,3},{3,1},{4,6},{6,4},{5,7},{7,5},{8,10},{10,8},{9,1... | collective-permute-start | bytes 1179656 | tf_op jit(solution)/shard_map/ppermute | solution.py:84
  155.0 13.3 %collective-permute-start.21 = (bf16[128,1536]{1,0:T(8,128)(2,1)S(1)}, bf16[128,1536]{1,0:T(8,128)(2,1)S(1)}, u32[]{:S(2)}, u32[]{:S(2)}) collective-permute-start(bf16[128,1536]{1,0:T(8,128)(2,1)S(1)} %fusion.1.refs_12_), channel_id=1, source_target_pairs={{0,2},{2,0},{1,3},{3,1},{4,6},{6,4},{5,7},{7,5},{8,10},{10,8},{9,1... | collective-permute-start | bytes 1179656 | tf_op jit(solution)/shard_map/ppermute | solution.py:84
  172.7 11.1 %collective-permute-start.23 = (bf16[128,1536]{1,0:T(8,128)(2,1)}, bf16[128,1536]{1,0:T(8,128)(2,1)S(1)}, u32[]{:S(2)}, u32[]{:S(2)}) collective-permute-start(bf16[128,1536]{1,0:T(8,128)(2,1)} %get-tuple-element.127.refs_0_.refs_1_), channel_id=1, source_target_pairs={{0,2},{2,0},{1,3},{3,1},{4,6},{6,4},{5,7},{7,5},{8,10},{10,8},{9,1... | collective-permute-start | bytes 1179656 | tf_op jit(solution)/shard_map/ppermute | solution.py:84
  173.0 11.0 %collective-permute-start.22 = (bf16[128,1536]{1,0:T(8,128)(2,1)}, bf16[128,1536]{1,0:T(8,128)(2,1)S(1)}, u32[]{:S(2)}, u32[]{:S(2)}) collective-permute-start(bf16[128,1536]{1,0:T(8,128)(2,1)} %get-tuple-element.127.refs_0_.refs_1_), channel_id=1, source_target_pairs={{0,1},{1,0},{2,3},{3,2},{4,5},{5,4},{6,7},{7,6},{8,9},{9,8},{10,11... | collective-permute-start | bytes 1179656 | tf_op jit(solution)/shard_map/ppermute | solution.py:80
  173.1 30.3 %collective-permute-start.26 = (bf16[8,576,128]{2,1,0:T(8,128)(2,1)}, bf16[8,576,128]{2,1,0:T(8,128)(2,1)}, u32[]{:S(2)}, u32[]{:S(2)}) collective-permute-start(bf16[8,576,128]{2,1,0:T(8,128)(2,1)} %get-tuple-element.133), channel_id=1, source_target_pairs={{32,64},{64,32},{0,96},{96,0},{33,65},{65,33},{1,97},{97,1},{34,66... | collective-permute-start | bytes 3538952 | tf_op jit(solution)/shard_map/ppermute | solution.py:111
  173.8 29.5 %collective-permute-start.27 = (bf16[8,576,128]{2,1,0:T(8,128)(2,1)}, bf16[8,576,128]{2,1,0:T(8,128)(2,1)}, u32[]{:S(2)}, u32[]{:S(2)}) collective-permute-start(bf16[8,576,128]{2,1,0:T(8,128)(2,1)} %get-tuple-element.135), channel_id=1, source_target_pairs={{0,4},{4,0},{8,12},{12,8},{1,5},{5,1},{9,13},{13,9},{2,6},{6,2},{1... | collective-permute-start | bytes 3538952 | tf_op jit(solution)/shard_map/ppermute | solution.py:111
  174.0 29.8 %collective-permute-start.28 = (bf16[8,576,128]{2,1,0:T(8,128)(2,1)S(1)}, bf16[8,576,128]{2,1,0:T(8,128)(2,1)}, u32[]{:S(2)}, u32[]{:S(2)}) collective-permute-start(bf16[8,576,128]{2,1,0:T(8,128)(2,1)S(1)} %copy-done.19), channel_id=1, source_target_pairs={{4,8},{8,4},{0,12},{12,0},{5,9},{9,5},{1,13},{13,1},{6,10},{10,6},... | collective-permute-start | bytes 3538952 | tf_op jit(solution)/shard_map/ppermute | solution.py:111
  183.8 30.2 %collective-permute-start.25 = (bf16[8,576,128]{2,1,0:T(8,128)(2,1)S(1)}, bf16[8,576,128]{2,1,0:T(8,128)(2,1)}, u32[]{:S(2)}, u32[]{:S(2)}) collective-permute-start(bf16[8,576,128]{2,1,0:T(8,128)(2,1)S(1)} %copy-done.18), channel_id=1, source_target_pairs={{0,32},{32,0},{64,96},{96,64},{1,33},{33,1},{65,97},{97,65},{2,34}... | collective-permute-start | bytes 3538952 | tf_op jit(solution)/shard_map/ppermute | solution.py:111
  190.7 35.0 %all-to-all-start.3 = ((bf16[8,192,128]{2,1,0:T(8,128)(2,1)}), bf16[8,192,128]{2,1,0:T(8,128)(2,1)S(1)}, u32[]{:S(2)}, u32[]{:S(2)}) async-start(bf16[8,192,128]{2,1,0:T(8,128)(2,1)} %shard_map.213.refs_6_), calls=%async_computation.3 | async-start | bytes 786432 | tf_op jit(solution)/shard_map/all_to_all | solution.py:146
  220.4 43.2 %collective-permute-start.30 = (bf16[4,576,128]{2,1,0:T(8,128)(2,1)}, bf16[4,576,128]{2,1,0:T(8,128)(2,1)S(1)}, u32[]{:S(2)}, u32[]{:S(2)}) collective-permute-start(bf16[4,576,128]{2,1,0:T(8,128)(2,1)} %get-tuple-element.143), channel_id=1, source_target_pairs={{0,4},{4,0},{8,12},{12,8},{1,5},{5,1},{9,13},{13,9},{2,6},{6,2},{1... | collective-permute-start | bytes 1769480 | tf_op jit(solution)/shard_map/ppermute | solution.py:111
  220.5 43.1 %collective-permute-start.31 = (bf16[4,576,128]{2,1,0:T(8,128)(2,1)}, bf16[4,576,128]{2,1,0:T(8,128)(2,1)}, u32[]{:S(2)}, u32[]{:S(2)}) collective-permute-start(bf16[4,576,128]{2,1,0:T(8,128)(2,1)} %get-tuple-element.145), channel_id=1, source_target_pairs={{4,8},{8,4},{0,12},{12,0},{5,9},{9,5},{1,13},{13,1},{6,10},{10,6},... | collective-permute-start | bytes 1769480 | tf_op jit(solution)/shard_map/ppermute | solution.py:111
  224.2 39.4 %collective-permute-start.32 = (bf16[4,576,128]{2,1,0:T(8,128)(2,1)}, bf16[4,576,128]{2,1,0:T(8,128)(2,1)}, u32[]{:S(2)}, u32[]{:S(2)}) collective-permute-start(bf16[4,576,128]{2,1,0:T(8,128)(2,1)} %get-tuple-element.147), channel_id=1, source_target_pairs={{0,32},{32,0},{64,96},{96,64},{1,33},{33,1},{65,97},{97,65},{2,34}... | collective-permute-start | bytes 1769480 | tf_op jit(solution)/shard_map/ppermute | solution.py:111
  224.5 39.2 %collective-permute-start.29 = (bf16[4,576,128]{2,1,0:T(8,128)(2,1)}, bf16[4,576,128]{2,1,0:T(8,128)(2,1)}, u32[]{:S(2)}, u32[]{:S(2)}) collective-permute-start(bf16[4,576,128]{2,1,0:T(8,128)(2,1)} %get-tuple-element.139.refs_7_), channel_id=1, source_target_pairs={{32,64},{64,32},{0,96},{96,0},{33,65},{65,33},{1,97},{97,1},{34,66... | collective-permute-start | bytes 1769480 | tf_op jit(solution)/shard_map/ppermute | solution.py:111
  225.7 28.0 %all-to-all-start.4 = ((bf16[16,304,128]{2,1,0:T(8,128)(2,1)}), bf16[16,304,128]{2,1,0:T(8,128)(2,1)S(1)}, u32[]{:S(2)}, u32[]{:S(2)}) async-start(bf16[16,304,128]{2,1,0:T(8,128)(2,1)} %shard_map.214.refs_16_), calls=%async_computation.4 | async-start | bytes 2490368 | tf_op jit(solution)/shard_map/all_to_all | solution.py:146
  254.8 40.1 %all-to-all-start.5 = ((bf16[32,192,128]{2,1,0:T(8,128)(2,1)}), bf16[32,192,128]{2,1,0:T(8,128)(2,1)S(1)}, u32[]{:S(2)}, u32[]{:S(2)}) async-start(bf16[32,192,128]{2,1,0:T(8,128)(2,1)} %get-tuple-element.157), calls=%async_computation.5 | async-start | bytes 3145728 | tf_op jit(solution)/shard_map/all_to_all | solution.py:146
  268.1 17.9 %collective-permute-start.34 = (bf16[2,576,128]{2,1,0:T(8,128)(2,1)}, bf16[2,576,128]{2,1,0:T(8,128)(2,1)S(1)}, u32[]{:S(2)}, u32[]{:S(2)}) collective-permute-start(bf16[2,576,128]{2,1,0:T(8,128)(2,1)} %get-tuple-element.151), channel_id=1, source_target_pairs={{4,8},{8,4},{0,12},{12,0},{5,9},{9,5},{1,13},{13,1},{6,10},{10,6},... | collective-permute-start | bytes 884744 | tf_op jit(solution)/shard_map/ppermute | solution.py:111
  269.6 16.4 %collective-permute-start.35 = (bf16[2,576,128]{2,1,0:T(8,128)(2,1)}, bf16[2,576,128]{2,1,0:T(8,128)(2,1)S(1)}, u32[]{:S(2)}, u32[]{:S(2)}) collective-permute-start(bf16[2,576,128]{2,1,0:T(8,128)(2,1)} %get-tuple-element.153), channel_id=1, source_target_pairs={{0,32},{32,0},{64,96},{96,64},{1,33},{33,1},{65,97},{97,65},{2,34}... | collective-permute-start | bytes 884744 | tf_op jit(solution)/shard_map/ppermute | solution.py:111
  271.1 14.9 %collective-permute-start.36 = (bf16[2,576,128]{2,1,0:T(8,128)(2,1)}, bf16[2,576,128]{2,1,0:T(8,128)(2,1)S(1)}, u32[]{:S(2)}, u32[]{:S(2)}) collective-permute-start(bf16[2,576,128]{2,1,0:T(8,128)(2,1)} %get-tuple-element.155), channel_id=1, source_target_pairs={{32,64},{64,32},{0,96},{96,0},{33,65},{65,33},{1,97},{97,1},{34,66... | collective-permute-start | bytes 884744 | tf_op jit(solution)/shard_map/ppermute | solution.py:111
  273.2 12.9 %collective-permute-start.33 = (bf16[2,576,128]{2,1,0:T(8,128)(2,1)}, bf16[2,576,128]{2,1,0:T(8,128)(2,1)S(1)}, u32[]{:S(2)}, u32[]{:S(2)}) collective-permute-start(bf16[2,576,128]{2,1,0:T(8,128)(2,1)} %get-tuple-element.149.refs_1_), channel_id=1, source_target_pairs={{0,4},{4,0},{8,12},{12,8},{1,5},{5,1},{9,13},{13,9},{2,6},{6,2},{1... | collective-permute-start | bytes 884744 | tf_op jit(solution)/shard_map/ppermute | solution.py:111
  289.7 18.2 %collective-permute-start.40 = (bf16[1,576,128]{2,1,0:T(8,128)(2,1)}, bf16[1,576,128]{2,1,0:T(8,128)(2,1)S(1)}, u32[]{:S(2)}, u32[]{:S(2)}) collective-permute-start(bf16[1,576,128]{2,1,0:T(8,128)(2,1)} %get-tuple-element.164), channel_id=1, source_target_pairs={{0,32},{32,0},{64,96},{96,64},{1,33},{33,1},{65,97},{97,65},{2,34}... | collective-permute-start | bytes 442376 | tf_op jit(solution)/shard_map/ppermute | solution.py:111
  290.1 17.8 %collective-permute-start.41 = (bf16[1,576,128]{2,1,0:T(8,128)(2,1)}, bf16[1,576,128]{2,1,0:T(8,128)(2,1)S(1)}, u32[]{:S(2)}, u32[]{:S(2)}) collective-permute-start(bf16[1,576,128]{2,1,0:T(8,128)(2,1)} %get-tuple-element.165), channel_id=1, source_target_pairs={{32,64},{64,32},{0,96},{96,0},{33,65},{65,33},{1,97},{97,1},{34,66... | collective-permute-start | bytes 442376 | tf_op jit(solution)/shard_map/ppermute | solution.py:111
  292.1 15.9 %collective-permute-start.42 = (bf16[1,576,128]{2,1,0:T(8,128)(2,1)}, bf16[1,576,128]{2,1,0:T(8,128)(2,1)S(1)}, u32[]{:S(2)}, u32[]{:S(2)}) collective-permute-start(bf16[1,576,128]{2,1,0:T(8,128)(2,1)} %get-tuple-element.166), channel_id=1, source_target_pairs={{0,4},{4,0},{8,12},{12,8},{1,5},{5,1},{9,13},{13,9},{2,6},{6,2},{1... | collective-permute-start | bytes 442376 | tf_op jit(solution)/shard_map/ppermute | solution.py:111
  294.3 13.7 %collective-permute-start.39 = (bf16[1,576,128]{2,1,0:T(8,128)(2,1)}, bf16[1,576,128]{2,1,0:T(8,128)(2,1)S(1)}, u32[]{:S(2)}, u32[]{:S(2)}) collective-permute-start(bf16[1,576,128]{2,1,0:T(8,128)(2,1)} %get-tuple-element.156.refs_1_), channel_id=1, source_target_pairs={{4,8},{8,4},{0,12},{12,0},{5,9},{9,5},{1,13},{13,1},{6,10},{10,6},... | collective-permute-start | bytes 442376 | tf_op jit(solution)/shard_map/ppermute | solution.py:111
  298.1 16.7 %all-to-all-start.6 = ((bf16[8,192,128]{2,1,0:T(8,128)(2,1)}), bf16[8,192,128]{2,1,0:T(8,128)(2,1)S(1)}, u32[]{:S(2)}, u32[]{:S(2)}) async-start(bf16[8,192,128]{2,1,0:T(8,128)(2,1)} %shard_map.220.refs_3_), calls=%async_computation.6 | async-start | bytes 786432 | tf_op jit(solution)/shard_map/all_to_all | solution.py:146
  311.1 17.1 %collective-permute-start.43 = (bf16[2608,128]{1,0:T(8,128)(2,1)}, bf16[2608,128]{1,0:T(8,128)(2,1)S(1)}, u32[]{:S(2)}, u32[]{:S(2)}) collective-permute-start(bf16[2608,128]{1,0:T(8,128)(2,1)} %shard_map.222.refs_13_.refs_0_), channel_id=1, source_target_pairs={{0,16},{16,0},{1,17},{17,1},{2,18},{18,2},{3,19},{19,3},{4,20},{20... | collective-permute-start | bytes 2002952 | tf_op jit(solution)/shard_map/ppermute | solution.py:101
  314.6 37.2 %collective-permute-start.37 = (bf16[2,128,1536]{2,1,0:T(8,128)(2,1)}, bf16[2,128,1536]{2,1,0:T(8,128)(2,1)S(1)}, u32[]{:S(2)}, u32[]{:S(2)}) collective-permute-start(bf16[2,128,1536]{2,1,0:T(8,128)(2,1)} %get-tuple-element.159), channel_id=1, source_target_pairs={{0,1},{1,0},{2,3},{3,2},{4,5},{5,4},{6,7},{7,6},{8,9},{9,8},{10,11... | collective-permute-start | bytes 2359304 | tf_op jit(solution)/shard_map/ppermute | solution.py:80
  322.4 31.7 %collective-permute-start.48 = (bf16[2,128,1536]{2,1,0:T(8,128)(2,1)}, bf16[2,128,1536]{2,1,0:T(8,128)(2,1)}, u32[]{:S(2)}, u32[]{:S(2)}) collective-permute-start(bf16[2,128,1536]{2,1,0:T(8,128)(2,1)} %get-tuple-element.174), channel_id=1, source_target_pairs={{0,1},{1,0},{2,3},{3,2},{4,5},{5,4},{6,7},{7,6},{8,9},{9,8},{10,11... | collective-permute-start | bytes 2359304 | tf_op jit(solution)/shard_map/ppermute | solution.py:80
  335.7 68.5 %all-to-all-start.7 = ((bf16[32,4,80,128]{3,2,1,0:T(8,128)(2,1)}), bf16[32,4,80,128]{3,2,1,0:T(8,128)(2,1)S(1)}, u32[]{:S(2)}, u32[]{:S(2)}) async-start(bf16[32,4,80,128]{3,2,1,0:T(8,128)(2,1)} %shard_map.225.refs_8_), calls=%async_computation.7 | async-start | bytes 5242880 | tf_op jit(solution)/shard_map/all_to_all | solution.py:146
  345.7 34.2 %collective-permute-start.44 = (bf16[1,656,128]{2,1,0:T(8,128)(2,1)}, bf16[1,656,128]{2,1,0:T(8,128)(2,1)S(1)}, u32[]{:S(2)}, u32[]{:S(2)}) collective-permute-start(bf16[1,656,128]{2,1,0:T(8,128)(2,1)} %get-tuple-element.168.refs_2_.refs_0_), channel_id=1, source_target_pairs={{4,8},{8,4},{0,12},{12,0},{5,9},{9,5},{1,13},{13,1},{6,10},{10,6},... | collective-permute-start | bytes 503816 | tf_op jit(solution)/shard_map/ppermute | solution.py:111
  347.3 30.5 %collective-permute-start.46 = (bf16[1,640,128]{2,1,0:T(8,128)(2,1)}, bf16[1,640,128]{2,1,0:T(8,128)(2,1)S(1)}, u32[]{:S(2)}, u32[]{:S(2)}) collective-permute-start(bf16[1,640,128]{2,1,0:T(8,128)(2,1)} %get-tuple-element.170.refs_2_), channel_id=1, source_target_pairs={{32,64},{64,32},{0,96},{96,0},{33,65},{65,33},{1,97},{97,1},{34,66... | collective-permute-start | bytes 491528 | tf_op jit(solution)/shard_map/ppermute | solution.py:111
  350.0 27.9 %collective-permute-start.47 = (bf16[1,640,128]{2,1,0:T(8,128)(2,1)}, bf16[1,640,128]{2,1,0:T(8,128)(2,1)S(1)}, u32[]{:S(2)}, u32[]{:S(2)}) collective-permute-start(bf16[1,640,128]{2,1,0:T(8,128)(2,1)} %get-tuple-element.171.refs_3_), channel_id=1, source_target_pairs={{0,4},{4,0},{8,12},{12,8},{1,5},{5,1},{9,13},{13,9},{2,6},{6,2},{1... | collective-permute-start | bytes 491528 | tf_op jit(solution)/shard_map/ppermute | solution.py:111
  352.7 27.3 %collective-permute-start.45 = (bf16[1,656,128]{2,1,0:T(8,128)(2,1)}, bf16[1,656,128]{2,1,0:T(8,128)(2,1)}, u32[]{:S(2)}, u32[]{:S(2)}) collective-permute-start(bf16[1,656,128]{2,1,0:T(8,128)(2,1)} %get-tuple-element.169.refs_1_), channel_id=1, source_target_pairs={{0,32},{32,0},{64,96},{96,64},{1,33},{33,1},{65,97},{97,65},{2,34}... | collective-permute-start | bytes 503816 | tf_op jit(solution)/shard_map/ppermute | solution.py:111
  354.1 31.5 %collective-permute-start.38 = (bf16[128,1536]{1,0:T(8,128)(2,1)S(1)}, bf16[128,1536]{1,0:T(8,128)(2,1)}, u32[]{:S(2)}, u32[]{:S(2)}) collective-permute-start(bf16[128,1536]{1,0:T(8,128)(2,1)S(1)} %fusion.2), channel_id=1, source_target_pairs={{0,2},{2,0},{1,3},{3,1},{4,6},{6,4},{5,7},{7,5},{8,10},{10,8},{9,1... | collective-permute-start | bytes 1179656 | tf_op jit(solution)/shard_map/ppermute | solution.py:84
  377.8 13.3 %collective-permute-start.49 = (bf16[128,1536]{1,0:T(8,128)(2,1)S(1)}, bf16[128,1536]{1,0:T(8,128)(2,1)S(1)}, u32[]{:S(2)}, u32[]{:S(2)}) collective-permute-start(bf16[128,1536]{1,0:T(8,128)(2,1)S(1)} %fusion.3), channel_id=1, source_target_pairs={{0,2},{2,0},{1,3},{3,1},{4,6},{6,4},{5,7},{7,5},{8,10},{10,8},{9,1... | collective-permute-start | bytes 1179656 | tf_op jit(solution)/shard_map/ppermute | solution.py:84
  383.1 12.0 %collective-permute-start.52 = (bf16[2,640,128]{2,1,0:T(8,128)(2,1)}, bf16[2,640,128]{2,1,0:T(8,128)(2,1)}, u32[]{:S(2)}, u32[]{:S(2)}) collective-permute-start(bf16[2,640,128]{2,1,0:T(8,128)(2,1)} %get-tuple-element.178.refs_2_), channel_id=1, source_target_pairs={{0,32},{32,0},{64,96},{96,64},{1,33},{33,1},{65,97},{97,65},{2,34}... | collective-permute-start | bytes 983048 | tf_op jit(solution)/shard_map/ppermute | solution.py:111
  384.1 11.0 %collective-permute-start.53 = (bf16[2,640,128]{2,1,0:T(8,128)(2,1)}, bf16[2,640,128]{2,1,0:T(8,128)(2,1)}, u32[]{:S(2)}, u32[]{:S(2)}) collective-permute-start(bf16[2,640,128]{2,1,0:T(8,128)(2,1)} %get-tuple-element.179.refs_3_), channel_id=1, source_target_pairs={{32,64},{64,32},{0,96},{96,0},{33,65},{65,33},{1,97},{97,1},{34,66... | collective-permute-start | bytes 983048 | tf_op jit(solution)/shard_map/ppermute | solution.py:111
  385.6 10.6 %collective-permute-start.50 = (bf16[2,656,128]{2,1,0:T(8,128)(2,1)}, bf16[2,656,128]{2,1,0:T(8,128)(2,1)S(1)}, u32[]{:S(2)}, u32[]{:S(2)}) collective-permute-start(bf16[2,656,128]{2,1,0:T(8,128)(2,1)} %get-tuple-element.172.refs_4_.refs_0_), channel_id=1, source_target_pairs={{0,4},{4,0},{8,12},{12,8},{1,5},{5,1},{9,13},{13,9},{2,6},{6,2},{1... | collective-permute-start | bytes 1007624 | tf_op jit(solution)/shard_map/ppermute | solution.py:111
  400.1 18.1 %collective-permute-start.55 = (bf16[4,656,128]{2,1,0:T(8,128)(2,1)}, bf16[4,656,128]{2,1,0:T(8,128)(2,1)S(1)}, u32[]{:S(2)}, u32[]{:S(2)}) collective-permute-start(bf16[4,656,128]{2,1,0:T(8,128)(2,1)} %get-tuple-element.181.refs_1_), channel_id=1, source_target_pairs={{0,4},{4,0},{8,12},{12,8},{1,5},{5,1},{9,13},{13,9},{2,6},{6,2},{1... | collective-permute-start | bytes 2015240 | tf_op jit(solution)/shard_map/ppermute | solution.py:111
  401.8 16.7 %collective-permute-start.54 = (bf16[4,656,128]{2,1,0:T(8,128)(2,1)}, bf16[4,656,128]{2,1,0:T(8,128)(2,1)}, u32[]{:S(2)}, u32[]{:S(2)}) collective-permute-start(bf16[4,656,128]{2,1,0:T(8,128)(2,1)} %get-tuple-element.180.refs_1_.refs_0_), channel_id=1, source_target_pairs={{32,64},{64,32},{0,96},{96,0},{33,65},{65,33},{1,97},{97,1},{34,66... | collective-permute-start | bytes 2015240 | tf_op jit(solution)/shard_map/ppermute | solution.py:111
  402.2 15.1 %collective-permute-start.56 = (bf16[4,640,128]{2,1,0:T(8,128)(2,1)}, bf16[4,640,128]{2,1,0:T(8,128)(2,1)}, u32[]{:S(2)}, u32[]{:S(2)}) collective-permute-start(bf16[4,640,128]{2,1,0:T(8,128)(2,1)} %get-tuple-element.182.refs_2_), channel_id=1, source_target_pairs={{4,8},{8,4},{0,12},{12,0},{5,9},{9,5},{1,13},{13,1},{6,10},{10,6},... | collective-permute-start | bytes 1966088 | tf_op jit(solution)/shard_map/ppermute | solution.py:111
  403.2 15.0 %collective-permute-start.57 = (bf16[4,640,128]{2,1,0:T(8,128)(2,1)}, bf16[4,640,128]{2,1,0:T(8,128)(2,1)}, u32[]{:S(2)}, u32[]{:S(2)}) collective-permute-start(bf16[4,640,128]{2,1,0:T(8,128)(2,1)} %get-tuple-element.183.refs_3_), channel_id=1, source_target_pairs={{0,32},{32,0},{64,96},{96,64},{1,33},{33,1},{65,97},{97,65},{2,34}... | collective-permute-start | bytes 1966088 | tf_op jit(solution)/shard_map/ppermute | solution.py:111
  408.4 15.6 %all-to-all-start.8 = ((bf16[4,80,128]{2,1,0:T(8,128)(2,1)}), bf16[4,80,128]{2,1,0:T(8,128)(2,1)S(1)}, u32[]{:S(2)}, u32[]{:S(2)}) async-start(bf16[4,80,128]{2,1,0:T(8,128)(2,1)} %shard_map.230.refs_8_), calls=%async_computation.8 | async-start | bytes 163840 | tf_op jit(solution)/shard_map/all_to_all | solution.py:146
  427.4 39.3 %all-to-all-start.9 = ((bf16[32,4,80,128]{3,2,1,0:T(8,128)(2,1)}), bf16[32,4,80,128]{3,2,1,0:T(8,128)(2,1)S(1)}, u32[]{:S(2)}, u32[]{:S(2)}) async-start(bf16[32,4,80,128]{3,2,1,0:T(8,128)(2,1)} %shard_map.232), calls=%async_computation.9 | async-start | bytes 5242880 | tf_op jit(solution)/shard_map/all_to_all | solution.py:146
  434.2 58.3 %collective-permute-start.62 = (bf16[8,656,128]{2,1,0:T(8,128)(2,1)}, bf16[8,656,128]{2,1,0:T(8,128)(2,1)}, u32[]{:S(2)}, u32[]{:S(2)}) collective-permute-start(bf16[8,656,128]{2,1,0:T(8,128)(2,1)} %get-tuple-element.190.refs_2_), channel_id=1, source_target_pairs={{32,64},{64,32},{0,96},{96,0},{33,65},{65,33},{1,97},{97,1},{34,66... | collective-permute-start | bytes 4030472 | tf_op jit(solution)/shard_map/ppermute | solution.py:111
  437.0 56.7 %collective-permute-start.61 = (bf16[8,656,128]{2,1,0:T(8,128)(2,1)}, bf16[8,656,128]{2,1,0:T(8,128)(2,1)}, u32[]{:S(2)}, u32[]{:S(2)}) collective-permute-start(bf16[8,656,128]{2,1,0:T(8,128)(2,1)} %get-tuple-element.184.refs_1_), channel_id=1, source_target_pairs={{0,32},{32,0},{64,96},{96,64},{1,33},{33,1},{65,97},{97,65},{2,34}... | collective-permute-start | bytes 4030472 | tf_op jit(solution)/shard_map/ppermute | solution.py:111
  437.2 52.9 %collective-permute-start.63 = (bf16[8,640,128]{2,1,0:T(8,128)(2,1)}, bf16[8,640,128]{2,1,0:T(8,128)(2,1)}, u32[]{:S(2)}, u32[]{:S(2)}) collective-permute-start(bf16[8,640,128]{2,1,0:T(8,128)(2,1)} %get-tuple-element.191.refs_3_), channel_id=1, source_target_pairs={{0,4},{4,0},{8,12},{12,8},{1,5},{5,1},{9,13},{13,9},{2,6},{6,2},{1... | collective-permute-start | bytes 3932168 | tf_op jit(solution)/shard_map/ppermute | solution.py:111
  437.8 52.5 %collective-permute-start.64 = (bf16[8,640,128]{2,1,0:T(8,128)(2,1)}, bf16[8,640,128]{2,1,0:T(8,128)(2,1)}, u32[]{:S(2)}, u32[]{:S(2)}) collective-permute-start(bf16[8,640,128]{2,1,0:T(8,128)(2,1)} %get-tuple-element.192.refs_4_), channel_id=1, source_target_pairs={{4,8},{8,4},{0,12},{12,0},{5,9},{9,5},{1,13},{13,1},{6,10},{10,6},... | collective-permute-start | bytes 3932168 | tf_op jit(solution)/shard_map/ppermute | solution.py:111
  441.2 18.9 %collective-permute-start.60 = (f32[384]{0:T(512)S(1)}, f32[384]{0:T(512)S(1)}, u32[]{:S(2)}, u32[]{:S(2)}) collective-permute-start(f32[384]{0:T(512)S(1)} %get-tuple-element.201), channel_id=1, source_target_pairs={{0,3},{1,2},{2,1},{3,0},{4,7},{5,6},{6,5},{7,4},{8,11},{9,10},{10,... | collective-permute-start | bytes 4616 | tf_op jit(solution)/shard_map/ppermute | solution.py:88
  (71 other events, 304.6 us)

commit v3 on v2

--- a/solution.py
+++ b/solution.py
@@ -57,6 +57,7 @@
         scratch_shapes=list(scratch),
         compiler_params=PARAMS,
         cost_estimate=cost(us),
+        name=getattr(kernel, "__name__", "part"),
     )(*smem, *vmem, *deps)
 
 
@@ -431,14 +432,11 @@
     d_gain[...] = jnp.concatenate(rows + [jnp.zeros((4, 128), F32)], axis=0).astype(BF)
 
 
-def d_tokens_kernel(x, keep, got, far, d_hidden, gain, d_tokens):
-    grads = keep[0].astype(F32) + got[0].astype(F32) + far[...].astype(F32)
+def last_kernel(x, keep, got, far, hidden, d_hidden, gain, layer_out, d_tokens):
+    total = keep[0].astype(F32) + got[0].astype(F32) + far[0].astype(F32)
+    layer_out[...] = (hidden[...] + total).astype(BF)
+    grads = keep[1].astype(F32) + got[1].astype(F32) + far[1].astype(F32)
     d_tokens[...] = d_hidden[...] + norm_back(x[...].astype(F32), gain[...], grads)
-
-
-def layer_out_kernel(hidden, keep, got, far, out):
-    total = keep[0].astype(F32) + got[0].astype(F32) + far[...].astype(F32)
-    out[...] = (hidden[...] + total).astype(BF)
 
 
 def d_o_kernel(b0, b1, b2, b3, w, d_o):
@@ -509,14 +507,17 @@
     )(sc, *xs, da, wg, wu)
 
 
-def mlp_out_kernel(sc, act, wd, keep, send):
+def mlp_out_kernel(sc, act, wd, keep_in, send_in, keep, send):
     gz = sc[2]
     acts = [
         act[:, pl.ds(pl.multiple_of((b ^ gz) * 256, 256), 256)] for b in range(FS // 256)
     ]
     total = dot(jnp.concatenate(acts, axis=1), wd[...])
     for k in range(4):
-        (keep, send)[k % 2][k // 2] = total[ROWS * k : ROWS * (k + 1)].astype(BF)
+        (keep, send)[k % 2][2 * (k // 2)] = total[ROWS * k : ROWS * (k + 1)].astype(BF)
+    for k in range(2):
+        keep[2 * k + 1] = keep_in[k]
+        send[2 * k + 1] = send_in[k]
 
 
 def ffn_grads_kernel(sc, x0, x1, x2, x3, y0, y1, y2, y3, act, dg, du, *refs):
@@ -561,29 +562,47 @@
 GAIN_AT = 2592
 
 
-def step_kernel(*refs):
-    for p in range(4):
-        kl, ku, gl, gu = refs[4 * p : 4 * p + 4]
-        keep, send = refs[16 + 2 * p : 18 + 2 * p]
-        keep[...] = (kl[...].astype(F32) + gl[...].astype(F32)).astype(BF)
-        send[...] = (ku[...].astype(F32) + gu[...].astype(F32)).astype(BF)
-
-
-def cube_step(keeps, gots, deps, us):
-    half = keeps[0].shape[0] // 2
+def first_step(keeps, gots, deps, us):
+    def body(*refs):
+        for p in range(4):
+            k, g, out = refs[2 * p], refs[2 * p + 1], refs[8 + len(deps) + p]
+            out[...] = (k[...].astype(F32) + g[...].astype(F32)).astype(BF)
+
+    args = [x for pair in zip(keeps, gots) for x in pair]
+    return pl.pallas_call(
+        body,
+        grid=(4,),
+        in_specs=[pl.BlockSpec((1, 576, 128), lambda n: (n + 4, 0, 0))] * 8
+        + [ANY_SPEC] * len(deps),
+        out_specs=[pl.BlockSpec((1, 576, 128), lambda n: (n, 0, 0))] * 4,
+        out_shape=[sds((4, 576, 128))] * 4,
+        compiler_params=PARAMS,
+        cost_estimate=cost(us),
+    )(*args, *deps)
+
+
+def cube_step(terms, deps, us):
+    count = len(terms[0])
+    half = terms[0][-1].shape[0] // 2
     lower = pl.BlockSpec((1, 576, 128), lambda n: (n, 0, 0))
     upper = pl.BlockSpec((1, 576, 128), lambda n: (n + half, 0, 0))
+    used = 8 * count
 
     def body(*refs):
-        step_kernel(*refs[:16], *refs[16 + len(deps) :])
-
-    args = []
-    for k, g in zip(keeps, gots):
-        args += [k, k, g, g]
+        outs = refs[used + len(deps) :]
+        for p in range(4):
+            mine = refs[2 * count * p : 2 * count * (p + 1)]
+            for side in range(2):
+                total = mine[side][...].astype(F32)
+                for t in range(1, count):
+                    total += mine[2 * t + side][...].astype(F32)
+                outs[2 * p + side][...] = total.astype(BF)
+
+    args = [x for portion in terms for term in portion for x in (term, term)]
     outs = pl.pallas_call(
         body,
         grid=(half,),
-        in_specs=[lower, upper] * 8 + [ANY_SPEC] * len(deps),
+        in_specs=[lower, upper] * (4 * count) + [ANY_SPEC] * len(deps),
         out_specs=[lower] * 8,
         out_shape=[sds((half, 576, 128))] * 8,
         compiler_params=PARAMS,
@@ -700,13 +719,29 @@
     out[...] = jnp.sum(parts[...].astype(F32), axis=0).astype(BF)
 
 
-def repeat_kernel(part, out):
-    for n in range(32):
-        out[n] = part[...]
+def sum_slots_kernel(sc, parts, gains, o0, o1, o2, o3):
+    for k, out in enumerate((o0, o1, o2, o3)):
+        g = sc[0] ^ k
+        total = parts[0, g].astype(F32)
+        for n in range(1, 32):
+            total += parts[n, g].astype(F32)
+        rows = [gains[pl.ds(3 * g + t, 1), :] for t in range(3)]
+        rows = [total, *rows, jnp.zeros((5, 128), F32)]
+        out[...] = jnp.concatenate(rows, axis=0).astype(BF)
+
+
+def repeat_kernel(sc, p0, p1, p2, p3, out, gain):
+    total = jnp.zeros((8, 128), F32)
+    for k, part in enumerate((p0, p1, p2, p3)):
+        whole = part[...].astype(F32)
+        total += whole[QKV_ROWS:]
+        mine = whole[:QKV_ROWS].astype(BF)
+        for n in range(32):
+            out[n, sc[0] ^ k] = mine
+    gain[...] = total
 
 
 QKV_ROWS = 72
-QKV_PAD = 80
 
 
 def d_xa_kernel(sc, d_q, d_kv, q0, q1, q2, q3, k0, k1, k2, k3, cos, sin, lin, keep, send, dq, dkv):
@@ -755,12 +790,11 @@
 
 
 def qkv_grads_kernel(xa, lin, pieces, tmp):
-    zeros = jnp.zeros((QKV_PAD - QKV_ROWS, 128), F32)
     for g in range(4):
         tmp[...] = t_dot(xa[:, DS * g : DS * (g + 1)], lin[...])
         for n in range(32):
             tiles = [tmp[r : r + size, lane : lane + 128] for lane, r, size in flat_pieces(n)]
-            pieces[n, g] = jnp.concatenate(tiles + [zeros], axis=0).astype(BF)
+            pieces[n, g] = jnp.concatenate(tiles, axis=0).astype(BF)
 
 
 def attn_place_kernel(got, wq, wk, wv, gain_in, q, k, v, gain, tmp):
@@ -904,8 +938,8 @@
         [pltpu.VMEM((DS, D), F32)],
         [d_o],
     )
-    keeps, sends = cube_step(keeps, gots, [out_pieces], 5)
-    gots = [swap_cube(s, p + 1) for p, s in enumerate(sends)]
+    sends = first_step(keeps, gots, [out_pieces], 4)
+    more = [swap_cube(s, p + 1) for p, s in enumerate(sends)]
     out_got = exchange(out_pieces, ("y", "z"))
     dq2, dkv = call(
         attention_back_kernel,
@@ -917,19 +951,17 @@
         [sends[0]],
     )
     dkv_tok = exchange(dkv, CTX)
-    keeps, sends = cube_step(keeps, gots, [dq2], 4)
+    keeps, sends = cube_step(list(zip(keeps, gots, more)), [dq2], 5)
     gots = [swap_cube(s, p + 2) for p, s in enumerate(sends)]
     out_sum = call(
-        sum_kernel, sds((OUT_ROWS + 16, 128)), [], [out_got], 2, deps=[sends[0]]
-    )
-    keeps, sends = cube_step(keeps, gots, [out_sum], 3)
+        sum_kernel, sds((OUT_ROWS + 16, 128)), [], [out_got], 40, deps=[sends[0]]
+    )
+    dq = call(fold_dq_kernel, sds(folded), [], [dq2], 2, deps=[out_sum, dkv_tok])
+    dq_tok = exchange(dq, heads)
+    keeps, sends = cube_step(list(zip(keeps, gots)), [out_sum], 3)
     gots = [swap_cube(s, p + 3) for p, s in enumerate(sends)]
-    dq = call(fold_dq_kernel, sds(folded), [], [dq2], 2, deps=[sends[0], dkv_tok])
-    dq_tok = exchange(dq, heads)
-    keep, send = call(mlp_out_kernel, side, [sc], [act, w_down], 5, deps=[dq])
-    mlp_terms, _ = scatter_slots(keep, send)
     total = call(
-        last_step_kernel, sds((GAIN_AT + 16, 128)), [], [*keeps, *gots, out_sum], 2, deps=[keep]
+        last_step_kernel, sds((GAIN_AT + 16, 128)), [], [*keeps, *gots, out_sum], 2
     )
     total_got = swap_e(total)
 
@@ -951,10 +983,9 @@
         deps=[lin],
     )
     gots = [swap_cube(o, p + 3) for p, o in enumerate(owns)]
-    terms, moving = scatter_slots(keep, send)
     pieces = call(
         qkv_grads_kernel,
-        sds((32, 4, QKV_PAD, 128)),
+        sds((32, 4, QKV_ROWS, 128)),
         [],
         [xa, lin],
         5,
@@ -962,46 +993,64 @@
         [owns[0]],
     )
     pieces_got = exchange(pieces, CTX)
-    owns = cube_gather(owns, gots, 2, [pieces])
+    keep, send = call(
+        mlp_out_kernel,
+        [sds((4, ROWS, D))] * 2,
+        [sc],
+        [act, w_down, keep, send],
+        6,
+        deps=[pieces],
+    )
+    got = swap_c(send)
+    far = swap_xl((keep[2:].astype(F32) + got[2:].astype(F32)).astype(BF))
+    owns = cube_gather(owns, gots, 2, [keep])
     gots = [swap_cube(o, p + 2) for p, o in enumerate(owns)]
-    layer_out = call(
-        layer_out_kernel, sds((ROWS, D)), [], [hidden, *mlp_terms], 2, deps=[owns[0]]
-    )
-    d_tokens = call(
-        d_tokens_kernel,
-        sds((ROWS, D), F32),
+    part = call(
+        sum_slots_kernel,
+        [sds((QKV_ROWS + 8, 128))] * 4,
+        [sc],
+        [pieces_got, gains_sum],
+        3,
+        deps=[owns[0]],
+    )
+    part_got = [part[0], swap_c(part[1]), swap_xl(part[2]), swap_both(part[3])]
+    owns = cube_gather(owns, gots, 3, [part[0]])
+    gots = [swap_cube(o, p + 1) for p, o in enumerate(owns)]
+    parts, g_gain_m = call(
+        repeat_kernel,
+        [sds((32, 4, QKV_ROWS, 128)), sds((8, 128), F32)],
+        [sc],
+        part_got,
+        3,
+        deps=[owns[0]],
+    )
+    parts_got = exchange(parts, CTX)
+    owns = cube_gather(owns, gots, 60, [parts])
+    gots = [swap_cube(o, p) for p, o in enumerate(owns)]
+    layer_out, d_tokens = call(
+        last_kernel,
+        [sds((ROWS, D)), sds((ROWS, D), F32)],
         [],
-        [own_x, *terms, d_hidden, gain_a],
-        2,
-        deps=[layer_out],
-    )
-    owns = cube_gather(owns, gots, 3, [d_tokens])
-    gots = [swap_cube(o, p + 1) for p, o in enumerate(owns)]
-
-    part = call(sum_kernel, sds((4, QKV_PAD, 128)), [], [pieces_got], 3, deps=[owns[0]])
-    owns = cube_gather(owns, gots, 5, [part])
-    gots = [swap_cube(o, p) for p, o in enumerate(owns)]
-    part = exchange(part, FSDP)
-    parts = call(repeat_kernel, sds((32, 4, QKV_PAD, 128)), [], [part], 3, deps=[owns[0]])
-    parts = exchange(parts, CTX)
-    g_gain_m = gains_sum[0:12].reshape(4, DS)
-    g_gain_m = [lax.dynamic_index_in_dim(g_gain_m, f ^ k, keepdims=False) for k in range(4)]
-    g_gain_m = g_gain_m[0] + swap_c(g_gain_m[1]) + swap_xl(g_gain_m[2]) + swap_both(g_gain_m[3])
+        [own_x, keep, got, far, hidden, d_hidden, gain_a],
+        5,
+        deps=[owns[0]],
+    )
     g_query, g_key, g_value, g_gain_a = call(
         attn_place_kernel,
         [sds((DS, D), F32), sds((DS, 768), F32), sds((DS, 768), F32), sds((DS, 1), F32)],
         [],
-        [parts, w_query, w_key, w_value, gain_attn.astype(F32).reshape(DS, 1)],
-        5,
+        [parts_got, w_query, w_key, w_value, gain_attn.astype(F32).reshape(DS, 1)],
+        6,
         [pltpu.VMEM((DS, 768), F32)],
-    )
-    g_gate, g_up, g_down, g_out = ffn_place(sc, owns, gots, [g_gain_a])
+        [d_tokens],
+    )
+    g_gate, g_up, g_down, g_out = ffn_place(sc, owns, gots, [g_query])
 
     return (
         layer_out[None],
         d_tokens[None],
         g_gain_a.reshape(DS),
-        g_gain_m.reshape(DS),
+        g_gain_m[0:3].reshape(DS),
         g_query,
         g_key,
         g_value,

time: 516 us -> 485 us (0.940)
  the two profiles are of different devices: /device:TPU:32 before, /device:TPU:1 now
where the time goes in v3:
time: 485 us; the launch traced here: 475 us
  Pallas kernels  172 us (35%)
  starting transfers between devices  150 us (31%)
  waiting for transfers between devices  121 us (25%)
  local copies, waits for them, and re-layouts  23 us (5%)
  other arithmetic  8.14 us (2%)
    pallas_call x26, Pallas kernels, call(): pl.pallas_call(body, out_shape=outs, in_specs=[SMEM_SPEC] * len(smem) + [...  134 us
    ppermute x32, waiting for transfers between devices, swap_cube(): return lax.ppermute(x, axis, pairs)  53.4 us
    all_to_all x9, starting transfers between devices, exchange(): return lax.all_to_all(x, axes, 0, 0, tiled=True)  47.2 us
    ppermute x32, starting transfers between devices, swap_cube(): return lax.ppermute(x, axis, pairs)  43.3 us
    all_to_all x9, waiting for transfers between devices, exchange(): return lax.all_to_all(x, axes, 0, 0, tiled=True)  30.5 us
    ppermute x14, starting transfers between devices, swap_c(): return lax.ppermute(x, 'c', [(0, 1), (1, 0)])  29.4 us
    ppermute x9, waiting for transfers between devices, swap_xl(): return lax.ppermute(x, 'xl', [(0, 1), (1, 0)])  24.3 us
    unnamed x132, local copies, waits for them, and re-layouts  17.4 us
  transfers between devices with their start and end apart: 72, of which 30 were waited for; matrix products, arithmetic and copies ran while one was open for 2% of the time, Pallas kernels for 26%

profile of v3, /device:TPU:1, one launch (start us, length us, event | category | flops | bytes accessed | tf_op | source)
XLA Modules:
  0.0 475.3 jit_solution(14923619984476279760)
XLA Ops:
  6.3 3.3 pack_kernel.1
  9.8 3.2 collective-permute-start.5
  14.7 3.7 collective-permute-done.4.refs_7_.refs_9_
  18.4 2.6 collective-permute-done.5.refs_8_.refs_10_
  22.0 5.1 %kv_kernel.1 = (bf16[512,1536]{1,0:T(8,128)(2,1)}, bf16[8,192,128]{2,1,0:T(8,128)(2,1)}, f32[1,1536]{1,0:T(1,128)}, f32[1,1536]{1,0:T(1,128)}) custom-call(s32[3]{0:T(128)} %pad_add_fusion.1.refs_0_.sc, bf16[128,1536]{1,0:T(8,128)(2,1)} %bitcast.22, bf16[128,1536]{1,0:T(8,128)(2,1)} %copy-done.29, bf16[128,1536]{1,0:T(8,128)(2,1)} %copy-done.28, ...), custom_call_target="tpu_custom_call" | custom-call | flops 5500000256 | bytes 15000000 | tf_op jit(solution)/shard_map/kv_kernel/pallas_call | solution.py:52
  27.0 5.6 %all-to-all-start.1 = ((bf16[8,192,128]{2,1,0:T(8,128)(2,1)}), bf16[8,192,128]{2,1,0:T(8,128)(2,1)S(1)}, u32[]{:S(2)}, u32[]{:S(2)}) async-start(bf16[8,192,128]{2,1,0:T(8,128)(2,1)} %get-tuple-element.117), calls=%async_computation.1 | async-start | bytes 786432 | tf_op jit(solution)/shard_map/all_to_all | solution.py:147
  33.4 4.2 collective-permute-start.7
  37.6 4.5 all-to-all-done.1.refs_3_
  43.8 3.3 collective-permute-start.10
  47.6 3.8 collective-permute-start.9
  51.3 2.6 collective-permute-done.8.refs_5_.refs_6_
  54.6 4.6 q_kernel.1
  59.2 4.1 all-to-all-start
  67.5 4.6 all-to-all-done.refs_2_
  73.8 13.8 %attention_kernel.1 = (bf16[8,192,128]{2,1,0:T(8,128)(2,1)}, bf16[16,128,128]{2,1,0:T(8,128)(2,1)}, bf16[16,128,128]{2,1,0:T(8,128)(2,1)}, f32[16,128,8]{2,1,0:T(8,128)}, bf16[4096,256]{1,0:T(8,128)(2,1)}) custom-call(s32[16]{0:T(128)} %slice.25.refs_0_, s32[64]{0:T(128)} %reshape.78.refs_1_, bf16[8,192,128]{2,1,0:T(8,128)(2,1)} %copy-done.11, ...), custom_call_target="tpu_custom_call" | custom-call | flops 14300000256 | bytes 39000000 | tf_op jit(solution)/shard_map/attention_kernel/pallas_call | solution.py:52
  87.7 3.5 all-to-all-start.2
  91.9 5.5 %d_act_kernel.1.refs_2_.da = f32[512,1024]{1,0:T(8,128)} custom-call(bf16[128,1536]{1,0:T(8,128)(2,1)} %bitcast.15, bf16[128,1536]{1,0:T(8,128)(2,1)} %copy-done.24, bf16[128,1536]{1,0:T(8,128)(2,1)} %copy-done.23, bf16[128,1536]{1,0:T(8,128)(2,1)} %collective-permute-done.14.refs_3_.refs_8_, bf16[1024,1536]{1,0:T(8,128)(2,1)} %refs_2_.4, ...), custom_call_target="tpu_custom_call" | custom-call | flops 4400000000 | bytes 12000000 | tf_op jit(solution)/shard_map/d_act_kernel/pallas_call | solution.py:52
  100.3 3.3 out_kernel.1
  103.7 3.3 collective-permute-start.15
  112.1 9.0 %collective-permute-done.16.refs_3_ = bf16[128,1536]{1,0:T(8,128)(2,1)S(1)} collective-permute-done((bf16[128,1536]{1,0:T(8,128)(2,1)S(1)}, bf16[128,1536]{1,0:T(8,128)(2,1)S(1)}, u32[]{:S(2)}, u32[]{:S(2)}) %collective-permute-start.16) | collective-permute-done | bytes 393248 | tf_op jit(solution)/shard_map/ppermute | solution.py:85
  121.9 2.9 hidden_kernel.1
  127.5 6.9 %collective-permute-done.18.x2.refs_3_ = bf16[128,1536]{1,0:T(8,128)(2,1)S(1)} collective-permute-done((bf16[128,1536]{1,0:T(8,128)(2,1)}, bf16[128,1536]{1,0:T(8,128)(2,1)S(1)}, u32[]{:S(2)}, u32[]{:S(2)}) %collective-permute-start.18) | collective-permute-done | bytes 393248 | tf_op jit(solution)/shard_map/ppermute | solution.py:85
  138.6 13.5 %shard_map.203 = (bf16[512,1024]{1,0:T(8,128)(2,1)}, bf16[512,1024]{1,0:T(8,128)(2,1)}, bf16[512,1024]{1,0:T(8,128)(2,1)}, bf16[2,128,1536]{2,1,0:T(8,128)(2,1)}, bf16[2,128,1536]{2,1,0:T(8,128)(2,1)}) custom-call(s32[3]{0:T(128)} %pad_add_fusion.1.refs_0_.sc, bf16[128,1536]{1,0:T(8,128)(2,1)} %get-tuple-element.122.x0.refs_1_, ...), custom_call_target="tpu_custom_call" | custom-call | flops 12099999744 | bytes 33000000 | tf_op jit(solution)/shard_map/pallas_call | solution.py:495
  157.8 11.1 %ffn_grads_kernel.1 = (bf16[8,576,128]{2,1,0:T(8,128)(2,1)}, bf16[8,576,128]{2,1,0:T(8,128)(2,1)}, bf16[8,576,128]{2,1,0:T(8,128)(2,1)}, bf16[8,576,128]{2,1,0:T...) custom-call(s32[3]{0:T(128)} %pad_add_fusion.1.refs_0_.sc, ...), custom_call_target="tpu_custom_call" | custom-call | flops 9900000256 | bytes 27000000 | tf_op jit(solution)/shard_map/ffn_grads_kernel/pallas_call | solution.py:52
  169.6 3.5 d_hidden_kernel.1
  178.7 4.6 collective-permute-done.23.refs_2_.refs_3_
  186.6 4.2 d_o_kernel.1.refs_6_
  190.8 5.1 %all-to-all-start.3 = ((bf16[8,192,128]{2,1,0:T(8,128)(2,1)}), bf16[8,192,128]{2,1,0:T(8,128)(2,1)}, u32[]{:S(2)}, u32[]{:S(2)}) async-start(bf16[8,192,128]{2,1,0:T(8,128)(2,1)} %d_o_kernel.1.refs_6_), calls=%async_computation.3 | async-start | bytes 786432 | tf_op jit(solution)/shard_map/all_to_all | solution.py:147
  195.9 3.4 out_grads_kernel.1.refs_8_
  199.3 3.9 collective-permute-done.26.refs_3_.refs_8_.refs_9_
  205.1 6.6 %collective-permute-done.25.refs_1_.refs_2_.refs_3_ = bf16[8,576,128]{2,1,0:T(8,128)(2,1)} collective-permute-done((bf16[8,576,128]{2,1,0:T(8,128)(2,1)}, bf16[8,576,128]{2,1,0:T(8,128)(2,1)}, u32[]{:S(2)}, u32[]{:S(2)}) %collective-permute-start.25) | collective-permute-done | bytes 1179680 | tf_op jit(solution)/shard_map/ppermute | solution.py:112
  211.7 4.4 shard_map.204
  221.2 4.7 all-to-all-start.4
  225.9 21.6 %attention_back_kernel.1 = (bf16[16,128,128]{2,1,0:T(8,128)(2,1)}, bf16[32,192,128]{2,1,0:T(8,128)(2,1)}) custom-call(s32[16]{0:T(128)} %slice.25.refs_0_, s32[64]{0:T(128)} %refs_1_.6, bf16[16,128,128]{2,1,0:T(8,128)(2,1)} %get-tuple-element.124.refs_2_, bf16[8,192,128]{2,1,0:T(8,128)(2,1)} %all-to-all-done.3.refs_3_, ...), custom_call_target="tpu_custom_call" | custom-call | flops 26400000000 | bytes 72000000 | tf_op jit(solution)/shard_map/attention_back_kernel/pallas_call | solution.py:52
  249.0 4.5 shard_map.205
  253.5 3.5 collective-permute-start.34
  259.9 5.8 %all-to-all-start.5 = ((bf16[32,192,128]{2,1,0:T(8,128)(2,1)}), bf16[32,192,128]{2,1,0:T(8,128)(2,1)S(1)}, u32[]{:S(2)}, u32[]{:S(2)}) async-start(bf16[32,192,128]{2,1,0:T(8,128)(2,1)} %get-tuple-element.149), calls=%async_computation.5 | async-start | bytes 3145728 | tf_op jit(solution)/shard_map/all_to_all | solution.py:147
  268.8 2.7 shard_map.206
  277.0 6.8 %all-to-all-done.5.refs_2_ = bf16[32,192,128]{2,1,0:T(8,128)(2,1)S(1)} async-done(((bf16[32,192,128]{2,1,0:T(8,128)(2,1)}), bf16[32,192,128]{2,1,0:T(8,128)(2,1)S(1)}, u32[]{:S(2)}, u32[]{:S(2)}) %all-to-all-start.5) | async-done | bytes 1572896 | tf_op jit(solution)/shard_map/all_to_all | solution.py:147
  287.0 4.3 all-to-all-start.6
  294.4 3.2 collective-permute-start.41
  300.4 6.8 %d_xa_kernel.1 = (bf16[512,768]{1,0:T(8,128)(2,1)}, bf16[2,128,1536]{2,1,0:T(8,128)(2,1)}, bf16[2,128,1536]{2,1,0:T(8,128)(2,1)}) custom-call(s32[3]{0:T(128)} %pad_add_fusion.1.refs_0_.sc, bf16[8,192,128]{2,1,0:T(8,128)(2,1)} %copy-done.13, bf16[32,192,128]{2,1,0:T(8,128)(2,1)} %copy-done.9, bf16[384,384]{1,0:T(8,128)(2,1)} %get-tuple-element.113.refs_2_.refs_3_, ...), custom_call_target="tpu_custom_call" | custom-call | flops 7699999744 | bytes 21000000 | tf_op jit(solution)/shard_map/d_xa_kernel/pallas_call | solution.py:52
  310.3 4.4 qkv_grads_kernel.1.refs_5_
  314.7 9.3 %all-to-all-start.7 = ((bf16[32,4,72,128]{3,2,1,0:T(8,128)(2,1)}), bf16[32,4,72,128]{3,2,1,0:T(8,128)(2,1)S(1)}, u32[]{:S(2)}, u32[]{:S(2)}) async-start(bf16[32,4,72,128]{3,2,1,0:T(8,128)(2,1)} %qkv_grads_kernel.1.refs_5_), calls=%async_computation.7 | async-start | bytes 4718592 | tf_op jit(solution)/shard_map/all_to_all | solution.py:147
  324.0 6.1 %mlp_out_kernel.1 = (bf16[4,128,1536]{2,1,0:T(8,128)(2,1)}, bf16[4,128,1536]{2,1,0:T(8,128)(2,1)}) custom-call(s32[3]{0:T(128)} %pad_add_fusion.1.refs_0_.sc, bf16[512,1024]{1,0:T(8,128)(2,1)} %get-tuple-element.123.refs_9_.refs_1_, bf16[1024,1536]{1,0:T(8,128)(2,1)} %refs_2_.4, bf16[2,128,1536]{2,1,0:T(8,128)(2,1)} %get-tuple-element.165.refs_3_, ...), custom_call_target="tpu_custom_call" | custom-call | flops 6600000000 | bytes 18000000 | tf_op jit(solution)/shard_map/mlp_out_kernel/pallas_call | solution.py:52
  330.2 14.3 %collective-permute-start.42 = (bf16[4,128,1536]{2,1,0:T(8,128)(2,1)}, bf16[4,128,1536]{2,1,0:T(8,128)(2,1)}, u32[]{:S(2)}, u32[]{:S(2)}) collective-permute-start(bf16[4,128,1536]{2,1,0:T(8,128)(2,1)} %get-tuple-element.170), channel_id=1, source_target_pairs={{0,1},{1,0},{2,3},{3,2},{4,5},{5,4},{6,7},{7,6},{8,9},{9,8},{10,11... | collective-permute-start | bytes 4718600 | tf_op jit(solution)/shard_map/ppermute | solution.py:81
  350.2 8.9 %collective-permute-done.46.refs_6_ = bf16[1,640,128]{2,1,0:T(8,128)(2,1)S(1)} collective-permute-done((bf16[1,640,128]{2,1,0:T(8,128)(2,1)S(1)}, bf16[1,640,128]{2,1,0:T(8,128)(2,1)S(1)}, u32[]{:S(2)}, u32[]{:S(2)}) %collective-permute-start.46) | collective-permute-done | bytes 163872 | tf_op jit(solution)/shard_map/ppermute | solution.py:112
  364.0 2.8 collective-permute-start.49
  369.8 2.6 sum_slots_kernel.1
  372.4 2.8 collective-permute-done.50.refs_6_
  377.2 2.9 collective-permute-start.58
  380.8 3.3 stack_kernel.4
  389.9 2.5 repeat_kernel.1
  392.4 4.8 %all-to-all-start.8 = ((bf16[32,4,72,128]{3,2,1,0:T(8,128)(2,1)}), bf16[32,4,72,128]{3,2,1,0:T(8,128)(2,1)S(1)}, u32[]{:S(2)}, u32[]{:S(2)}) async-start(bf16[32,4,72,128]{3,2,1,0:T(8,128)(2,1)} %get-tuple-element.189.refs_8_), calls=%async_computation.8 | async-start | bytes 4718592 | tf_op jit(solution)/shard_map/all_to_all | solution.py:147
  397.3 4.5 collective-permute-done.54.refs_6_
  405.0 4.9 %stack_kernel.5 = (bf16[8,656,128]{2,1,0:T(8,128)(2,1)}, bf16[8,656,128]{2,1,0:T(8,128)(2,1)}, bf16[8,640,128]{2,1,0:T(8,128)(2,1)}, bf16[8,640,128]{2,1,0:T(8,128)(2,1)}) custom-call(bf16[4,656,128]{2,1,0:T(8,128)(2,1)} %get-tuple-element.182.refs_5_.refs_0_, bf16[4,656,128]{2,1,0:T(8,128)(2,1)} %get-tuple-element.183.refs_1_, ...), custom_call_target="tpu_custom_call" | custom-call | flops 65999998976 | bytes 180000000 | tf_op jit(solution)/shard_map/stack_kernel/pallas_call | solution.py:52
  410.3 2.6 collective-permute-start.62
  414.1 4.5 collective-permute-start.59
  419.1 4.4 last_kernel.1
  423.6 10.4 %all-to-all-done.8.refs_0_ = bf16[32,4,72,128]{3,2,1,0:T(8,128)(2,1)S(1)} async-done(((bf16[32,4,72,128]{3,2,1,0:T(8,128)(2,1)}), bf16[32,4,72,128]{3,2,1,0:T(8,128)(2,1)S(1)}, u32[]{:S(2)}, u32[]{:S(2)}) %all-to-all-start.8) | async-done | bytes 2359328 | tf_op jit(solution)/shard_map/all_to_all | solution.py:147
  435.3 5.5 %attn_place_kernel.1 = (f32[384,1536]{1,0:T(8,128)}, f32[384,768]{1,0:T(8,128)}, f32[384,768]{1,0:T(8,128)}, f32[384,1]{1,0:T(8,128)}) custom-call(bf16[32,4,72,128]{3,2,1,0:T(8,128)(2,1)} %copy-done.8, bf16[384,1536]{1,0:T(8,128)(2,1)} %refs_1_.7, bf16[384,768]{1,0:T(8,128)(2,1)} %refs_2_.5, bf16[384,768]{1,0:T(8,128)(2,1)} %refs_3_.3, ...), custom_call_target="tpu_custom_call" | custom-call | flops 6600000000 | bytes 18000000 | tf_op jit(solution)/shard_map/attn_place_kernel/pallas_call | solution.py:52
  442.5 15.4 %collective-permute-done.61.refs_7_ = bf16[8,640,128]{2,1,0:T(8,128)(2,1)} collective-permute-done((bf16[8,640,128]{2,1,0:T(8,128)(2,1)}, bf16[8,640,128]{2,1,0:T(8,128)(2,1)}, u32[]{:S(2)}, u32[]{:S(2)}) %collective-permute-start.61) | collective-permute-done | bytes 1310752 | tf_op jit(solution)/shard_map/ppermute | solution.py:112
  458.4 3.9 collective-permute-done.60.refs_6_
  462.3 12.6 %shard_map.207 = (f32[1536,1024]{1,0:T(8,128)}, f32[1536,1024]{1,0:T(8,128)}, f32[1024,1536]{1,0:T(8,128)}, f32[384,1536]{1,0:T(8,128)}) custom-call(s32[3]{0:T(128)} %pad_add_fusion.1.refs_0_.sc, bf16[8,656,128]{2,1,0:T(8,128)(2,1)} %get-tuple-element.190.refs_7_.refs_1_, bf16[8,656,128]{2,1,0:T(8,128)(2,1)} %get-tuple-element.198.refs_2_, ...), custom_call_target="tpu_custom_call" | custom-call | flops 13200000000 | bytes 36000000 | tf_op jit(solution)/shard_map/pallas_call | solution.py:682
  (269 shorter events, 112.6 us)
Async XLA Ops:
  0.6 12.5 %collective-permute-start.1 = (bf16[128,1536]{1,0:T(8,128)(2,1)}, bf16[128,1536]{1,0:T(8,128)(2,1)S(1)}, u32[]{:S(2)}, u32[]{:S(2)}) collective-permute-start(bf16[128,1536]{1,0:T(8,128)(2,1)} %bitcast.20), channel_id=1, source_target_pairs={{0,2},{2,0},{1,3},{3,1},{4,6},{6,4},{5,7},{7,5},{8,10},{10,8},{9,1... | collective-permute-start | bytes 1179656 | tf_op jit(solution)/shard_map/ppermute | solution.py:85
  2.8 18.2 %collective-permute-start = (bf16[128,1536]{1,0:T(8,128)(2,1)}, bf16[128,1536]{1,0:T(8,128)(2,1)S(1)}, u32[]{:S(2)}, u32[]{:S(2)}) collective-permute-start(bf16[128,1536]{1,0:T(8,128)(2,1)} %bitcast.21), channel_id=1, source_target_pairs={{0,1},{1,0},{2,3},{3,2},{4,5},{5,4},{6,7},{7,6},{8,9},{9,8},{10,11... | collective-permute-start | bytes 1179656 | tf_op jit(solution)/shard_map/ppermute | solution.py:81
  9.6 8.8 %collective-permute-start.4 = (bf16[400,384]{1,0:T(8,128)(2,1)}, bf16[400,384]{1,0:T(8,128)(2,1)S(1)}, u32[]{:S(2)}, u32[]{:S(2)}) collective-permute-start(bf16[400,384]{1,0:T(8,128)(2,1)} %get-tuple-element.110), channel_id=1, source_target_pairs={{0,2},{2,0},{1,3},{3,1},{4,6},{6,4},{5,7},{7,5},{8,10},{10,8},{9,1... | collective-permute-start | bytes 921608 | tf_op jit(solution)/shard_map/ppermute | solution.py:85
  9.8 11.1 %collective-permute-start.5 = (bf16[400,384]{1,0:T(8,128)(2,1)}, bf16[400,384]{1,0:T(8,128)(2,1)S(1)}, u32[]{:S(2)}, u32[]{:S(2)}) collective-permute-start(bf16[400,384]{1,0:T(8,128)(2,1)} %get-tuple-element.111), channel_id=1, source_target_pairs={{0,19},{1,18},{2,17},{3,16},{16,3},{17,2},{18,1},{19,0},{4,23},{5,... | collective-permute-start | bytes 921608 | tf_op jit(solution)/shard_map/ppermute | solution.py:98
  27.0 15.1 %all-to-all-start.1 = ((bf16[8,192,128]{2,1,0:T(8,128)(2,1)}), bf16[8,192,128]{2,1,0:T(8,128)(2,1)S(1)}, u32[]{:S(2)}, u32[]{:S(2)}) async-start(bf16[8,192,128]{2,1,0:T(8,128)(2,1)} %get-tuple-element.117), calls=%async_computation.1 | async-start | bytes 786432 | tf_op jit(solution)/shard_map/all_to_all | solution.py:147
  32.6 11.2 %collective-permute-start.6 = (bf16[384,384]{1,0:T(8,128)(2,1)}, bf16[384,384]{1,0:T(8,128)(2,1)S(1)}, u32[]{:S(2)}, u32[]{:S(2)}) collective-permute-start(bf16[384,384]{1,0:T(8,128)(2,1)} %get-tuple-element.114), channel_id=1, source_target_pairs={{0,1},{1,0},{2,3},{3,2},{4,5},{5,4},{6,7},{7,6},{8,9},{9,8},{10,11... | collective-permute-start | bytes 884744 | tf_op jit(solution)/shard_map/ppermute | solution.py:81
  33.4 14.2 %collective-permute-start.7 = (bf16[384,384]{1,0:T(8,128)(2,1)S(1)}, bf16[384,384]{1,0:T(8,128)(2,1)S(1)}, u32[]{:S(2)}, u32[]{:S(2)}) collective-permute-start(bf16[384,384]{1,0:T(8,128)(2,1)S(1)} %copy-done.46), channel_id=1, source_target_pairs={{0,18},{1,19},{2,16},{3,17},{16,2},{17,3},{18,0},{19,1},{4,22},{5,... | collective-permute-start | bytes 884744 | tf_op jit(solution)/shard_map/ppermute | solution.py:98
  37.6 16.3 %collective-permute-start.8 = (bf16[384,384]{1,0:T(8,128)(2,1)}, bf16[384,384]{1,0:T(8,128)(2,1)S(1)}, u32[]{:S(2)}, u32[]{:S(2)}) collective-permute-start(bf16[384,384]{1,0:T(8,128)(2,1)} %get-tuple-element.116), channel_id=1, source_target_pairs={{0,19},{1,18},{2,17},{3,16},{16,3},{17,2},{18,1},{19,0},{4,23},{5,... | collective-permute-start | bytes 884744 | tf_op jit(solution)/shard_map/ppermute | solution.py:98
  37.6 29.6 %collective-permute-start.13 = (bf16[128,1536]{1,0:T(8,128)(2,1)S(1)}, bf16[128,1536]{1,0:T(8,128)(2,1)S(1)}, u32[]{:S(2)}, u32[]{:S(2)}) collective-permute-start(bf16[128,1536]{1,0:T(8,128)(2,1)S(1)} %bitcast.18), channel_id=1, source_target_pairs={{0,2},{2,0},{1,3},{3,1},{4,6},{6,4},{5,7},{7,5},{8,10},{10,8},{9,1... | collective-permute-start | bytes 1179656 | tf_op jit(solution)/shard_map/ppermute | solution.py:85
  42.2 29.9 %collective-permute-start.11 = (bf16[8,192,128]{2,1,0:T(8,128)(2,1)S(1)}, bf16[8,192,128]{2,1,0:T(8,128)(2,1)S(1)}, u32[]{:S(2)}, u32[]{:S(2)}) collective-permute-start(bf16[8,192,128]{2,1,0:T(8,128)(2,1)S(1)} %all-to-all-done.1.refs_3_), channel_id=1, source_target_pairs={{12,0},{0,4},{4,8},{8,12},{13,1},{1,5},{5,9},{9,13},{14,2},{2,6},{... | collective-permute-start | bytes 1179656 | tf_op jit(solution)/shard_map/ppermute | solution.py:143
  43.8 28.3 %collective-permute-start.10 = (bf16[8,192,128]{2,1,0:T(8,128)(2,1)S(1)}, bf16[8,192,128]{2,1,0:T(8,128)(2,1)S(1)}, u32[]{:S(2)}, u32[]{:S(2)}) collective-permute-start(bf16[8,192,128]{2,1,0:T(8,128)(2,1)S(1)} %all-to-all-done.1.refs_3_), channel_id=1, source_target_pairs={{8,0},{12,4},{0,8},{4,12},{9,1},{13,5},{1,9},{5,13},{10,2},{14,6},... | collective-permute-start | bytes 1179656 | tf_op jit(solution)/shard_map/ppermute | solution.py:143
  47.6 24.5 %collective-permute-start.9 = (bf16[8,192,128]{2,1,0:T(8,128)(2,1)S(1)}, bf16[8,192,128]{2,1,0:T(8,128)(2,1)S(1)}, u32[]{:S(2)}, u32[]{:S(2)}) collective-permute-start(bf16[8,192,128]{2,1,0:T(8,128)(2,1)S(1)} %all-to-all-done.1.refs_3_), channel_id=1, source_target_pairs={{4,0},{8,4},{12,8},{0,12},{5,1},{9,5},{13,9},{1,13},{6,2},{10,6},{... | collective-permute-start | bytes 1179656 | tf_op jit(solution)/shard_map/ppermute | solution.py:143
  59.2 12.9 %all-to-all-start = ((bf16[8,192,128]{2,1,0:T(8,128)(2,1)}), bf16[8,192,128]{2,1,0:T(8,128)(2,1)S(1)}, u32[]{:S(2)}, u32[]{:S(2)}) async-start(bf16[8,192,128]{2,1,0:T(8,128)(2,1)} %q_kernel.1), calls=%async_computation | async-start | bytes 786432 | tf_op jit(solution)/shard_map/all_to_all | solution.py:147
  63.3 27.9 %collective-permute-start.12 = (bf16[128,1536]{1,0:T(8,128)(2,1)S(1)}, bf16[128,1536]{1,0:T(8,128)(2,1)S(1)}, u32[]{:S(2)}, u32[]{:S(2)}) collective-permute-start(bf16[128,1536]{1,0:T(8,128)(2,1)S(1)} %bitcast.19), channel_id=1, source_target_pairs={{0,1},{1,0},{2,3},{3,2},{4,5},{5,4},{6,7},{7,6},{8,9},{9,8},{10,11... | collective-permute-start | bytes 1179656 | tf_op jit(solution)/shard_map/ppermute | solution.py:81
  67.3 23.9 %collective-permute-start.14 = (bf16[128,1536]{1,0:T(8,128)(2,1)S(1)}, bf16[128,1536]{1,0:T(8,128)(2,1)}, u32[]{:S(2)}, u32[]{:S(2)}) collective-permute-start(bf16[128,1536]{1,0:T(8,128)(2,1)S(1)} %collective-permute-done.13.refs_2_.refs_7_), channel_id=1, source_target_pairs={{0,1},{1,0},{2,3},{3,2},{4,5},{5,4},{6,7},{7,6},{8,9},{9,8},{10,11... | collective-permute-start | bytes 1179656 | tf_op jit(solution)/shard_map/ppermute | solution.py:81
  87.7 11.9 %all-to-all-start.2 = ((bf16[8,192,128]{2,1,0:T(8,128)(2,1)}), bf16[8,192,128]{2,1,0:T(8,128)(2,1)S(1)}, u32[]{:S(2)}, u32[]{:S(2)}) async-start(bf16[8,192,128]{2,1,0:T(8,128)(2,1)} %get-tuple-element.118.refs_5_), calls=%async_computation.2 | async-start | bytes 786432 | tf_op jit(solution)/shard_map/all_to_all | solution.py:147
  110.5 10.7 %collective-permute-start.16 = (bf16[128,1536]{1,0:T(8,128)(2,1)S(1)}, bf16[128,1536]{1,0:T(8,128)(2,1)S(1)}, u32[]{:S(2)}, u32[]{:S(2)}) collective-permute-start(bf16[128,1536]{1,0:T(8,128)(2,1)S(1)} %fusion), channel_id=1, source_target_pairs={{0,2},{2,0},{1,3},{3,1},{4,6},{6,4},{5,7},{7,5},{8,10},{10,8},{9,1... | collective-permute-start | bytes 1179656 | tf_op jit(solution)/shard_map/ppermute | solution.py:85
  124.7 9.7 %collective-permute-start.18 = (bf16[128,1536]{1,0:T(8,128)(2,1)}, bf16[128,1536]{1,0:T(8,128)(2,1)S(1)}, u32[]{:S(2)}, u32[]{:S(2)}) collective-permute-start(bf16[128,1536]{1,0:T(8,128)(2,1)} %get-tuple-element.122.x0.refs_1_), channel_id=1, source_target_pairs={{0,2},{2,0},{1,3},{3,1},{4,6},{6,4},{5,7},{7,5},{8,10},{10,8},{9,1... | collective-permute-start | bytes 1179656 | tf_op jit(solution)/shard_map/ppermute | solution.py:85
  126.1 10.4 %collective-permute-start.17 = (bf16[128,1536]{1,0:T(8,128)(2,1)}, bf16[128,1536]{1,0:T(8,128)(2,1)S(1)}, u32[]{:S(2)}, u32[]{:S(2)}) collective-permute-start(bf16[128,1536]{1,0:T(8,128)(2,1)} %get-tuple-element.122.x0.refs_1_), channel_id=1, source_target_pairs={{0,1},{1,0},{2,3},{3,2},{4,5},{5,4},{6,7},{7,6},{8,9},{9,8},{10,11... | collective-permute-start | bytes 1179656 | tf_op jit(solution)/shard_map/ppermute | solution.py:81
  156.0 12.9 %collective-permute-start.21 = (bf16[128,1536]{1,0:T(8,128)(2,1)S(1)}, bf16[128,1536]{1,0:T(8,128)(2,1)S(1)}, u32[]{:S(2)}, u32[]{:S(2)}) collective-permute-start(bf16[128,1536]{1,0:T(8,128)(2,1)S(1)} %fusion.1.refs_12_), channel_id=1, source_target_pairs={{0,2},{2,0},{1,3},{3,1},{4,6},{6,4},{5,7},{7,5},{8,10},{10,8},{9,1... | collective-permute-start | bytes 1179656 | tf_op jit(solution)/shard_map/ppermute | solution.py:85
  173.1 10.2 %collective-permute-start.23 = (bf16[128,1536]{1,0:T(8,128)(2,1)}, bf16[128,1536]{1,0:T(8,128)(2,1)S(1)}, u32[]{:S(2)}, u32[]{:S(2)}) collective-permute-start(bf16[128,1536]{1,0:T(8,128)(2,1)} %get-tuple-element.131.refs_0_.refs_1_), channel_id=1, source_target_pairs={{0,2},{2,0},{1,3},{3,1},{4,6},{6,4},{5,7},{7,5},{8,10},{10,8},{9,1... | collective-permute-start | bytes 1179656 | tf_op jit(solution)/shard_map/ppermute | solution.py:85
  173.4 10.0 %collective-permute-start.22 = (bf16[128,1536]{1,0:T(8,128)(2,1)}, bf16[128,1536]{1,0:T(8,128)(2,1)}, u32[]{:S(2)}, u32[]{:S(2)}) collective-permute-start(bf16[128,1536]{1,0:T(8,128)(2,1)} %get-tuple-element.131.refs_0_.refs_1_), channel_id=1, source_target_pairs={{0,1},{1,0},{2,3},{3,2},{4,5},{5,4},{6,7},{7,6},{8,9},{9,8},{10,11... | collective-permute-start | bytes 1179656 | tf_op jit(solution)/shard_map/ppermute | solution.py:81
  174.2 29.0 %collective-permute-start.26 = (bf16[8,576,128]{2,1,0:T(8,128)(2,1)}, bf16[8,576,128]{2,1,0:T(8,128)(2,1)S(1)}, u32[]{:S(2)}, u32[]{:S(2)}) collective-permute-start(bf16[8,576,128]{2,1,0:T(8,128)(2,1)} %get-tuple-element.137), channel_id=1, source_target_pairs={{32,64},{64,32},{0,96},{96,0},{33,65},{65,33},{1,97},{97,1},{34,66... | collective-permute-start | bytes 3538952 | tf_op jit(solution)/shard_map/ppermute | solution.py:112
  174.8 28.5 %collective-permute-start.27 = (bf16[8,576,128]{2,1,0:T(8,128)(2,1)}, bf16[8,576,128]{2,1,0:T(8,128)(2,1)S(1)}, u32[]{:S(2)}, u32[]{:S(2)}) collective-permute-start(bf16[8,576,128]{2,1,0:T(8,128)(2,1)} %get-tuple-element.139), channel_id=1, source_target_pairs={{0,4},{4,0},{8,12},{12,8},{1,5},{5,1},{9,13},{13,9},{2,6},{6,2},{1... | collective-permute-start | bytes 3538952 | tf_op jit(solution)/shard_map/ppermute | solution.py:112
  176.6 28.5 %collective-permute-start.28 = (bf16[8,576,128]{2,1,0:T(8,128)(2,1)}, bf16[8,576,128]{2,1,0:T(8,128)(2,1)S(1)}, u32[]{:S(2)}, u32[]{:S(2)}) collective-permute-start(bf16[8,576,128]{2,1,0:T(8,128)(2,1)} %get-tuple-element.141), channel_id=1, source_target_pairs={{4,8},{8,4},{0,12},{12,0},{5,9},{9,5},{1,13},{13,1},{6,10},{10,6},... | collective-permute-start | bytes 3538952 | tf_op jit(solution)/shard_map/ppermute | solution.py:112
  183.4 28.4 %collective-permute-start.25 = (bf16[8,576,128]{2,1,0:T(8,128)(2,1)}, bf16[8,576,128]{2,1,0:T(8,128)(2,1)}, u32[]{:S(2)}, u32[]{:S(2)}) collective-permute-start(bf16[8,576,128]{2,1,0:T(8,128)(2,1)} %get-tuple-element.130.refs_6_), channel_id=1, source_target_pairs={{0,32},{32,0},{64,96},{96,64},{1,33},{33,1},{65,97},{97,65},{2,34}... | collective-permute-start | bytes 3538952 | tf_op jit(solution)/shard_map/ppermute | solution.py:112
  190.8 30.4 %all-to-all-start.3 = ((bf16[8,192,128]{2,1,0:T(8,128)(2,1)}), bf16[8,192,128]{2,1,0:T(8,128)(2,1)}, u32[]{:S(2)}, u32[]{:S(2)}) async-start(bf16[8,192,128]{2,1,0:T(8,128)(2,1)} %d_o_kernel.1.refs_6_), calls=%async_computation.3 | async-start | bytes 786432 | tf_op jit(solution)/shard_map/all_to_all | solution.py:147
  216.1 31.4 %collective-permute-start.30 = (bf16[4,576,128]{2,1,0:T(8,128)(2,1)}, bf16[4,576,128]{2,1,0:T(8,128)(2,1)S(1)}, u32[]{:S(2)}, u32[]{:S(2)}) collective-permute-start(bf16[4,576,128]{2,1,0:T(8,128)(2,1)} %get-tuple-element.145), channel_id=1, source_target_pairs={{0,4},{4,0},{8,12},{12,8},{1,5},{5,1},{9,13},{13,9},{2,6},{6,2},{1... | collective-permute-start | bytes 1769480 | tf_op jit(solution)/shard_map/ppermute | solution.py:112
  218.1 29.4 %collective-permute-start.31 = (bf16[4,576,128]{2,1,0:T(8,128)(2,1)}, bf16[4,576,128]{2,1,0:T(8,128)(2,1)S(1)}, u32[]{:S(2)}, u32[]{:S(2)}) collective-permute-start(bf16[4,576,128]{2,1,0:T(8,128)(2,1)} %get-tuple-element.146), channel_id=1, source_target_pairs={{4,8},{8,4},{0,12},{12,0},{5,9},{9,5},{1,13},{13,1},{6,10},{10,6},... | collective-permute-start | bytes 1769480 | tf_op jit(solution)/shard_map/ppermute | solution.py:112
  220.3 27.3 %collective-permute-start.32 = (bf16[4,576,128]{2,1,0:T(8,128)(2,1)}, bf16[4,576,128]{2,1,0:T(8,128)(2,1)S(1)}, u32[]{:S(2)}, u32[]{:S(2)}) collective-permute-start(bf16[4,576,128]{2,1,0:T(8,128)(2,1)} %get-tuple-element.147), channel_id=1, source_target_pairs={{0,32},{32,0},{64,96},{96,64},{1,33},{33,1},{65,97},{97,65},{2,34}... | collective-permute-start | bytes 1769480 | tf_op jit(solution)/shard_map/ppermute | solution.py:112
  220.3 27.3 %collective-permute-start.29 = (bf16[4,576,128]{2,1,0:T(8,128)(2,1)}, bf16[4,576,128]{2,1,0:T(8,128)(2,1)S(1)}, u32[]{:S(2)}, u32[]{:S(2)}) collective-permute-start(bf16[4,576,128]{2,1,0:T(8,128)(2,1)} %get-tuple-element.143.refs_7_), channel_id=1, source_target_pairs={{32,64},{64,32},{0,96},{96,0},{33,65},{65,33},{1,97},{97,1},{34,66... | collective-permute-start | bytes 1769480 | tf_op jit(solution)/shard_map/ppermute | solution.py:112
  221.2 38.7 %all-to-all-start.4 = ((bf16[16,304,128]{2,1,0:T(8,128)(2,1)}), bf16[16,304,128]{2,1,0:T(8,128)(2,1)}, u32[]{:S(2)}, u32[]{:S(2)}) async-start(bf16[16,304,128]{2,1,0:T(8,128)(2,1)} %out_grads_kernel.1.refs_8_), calls=%async_computation.4 | async-start | bytes 2490368 | tf_op jit(solution)/shard_map/all_to_all | solution.py:147
  253.5 14.4 %collective-permute-start.34 = (bf16[2,576,128]{2,1,0:T(8,128)(2,1)}, bf16[2,576,128]{2,1,0:T(8,128)(2,1)S(1)}, u32[]{:S(2)}, u32[]{:S(2)}) collective-permute-start(bf16[2,576,128]{2,1,0:T(8,128)(2,1)} %get-tuple-element.152), channel_id=1, source_target_pairs={{4,8},{8,4},{0,12},{12,0},{5,9},{9,5},{1,13},{13,1},{6,10},{10,6},... | collective-permute-start | bytes 884744 | tf_op jit(solution)/shard_map/ppermute | solution.py:112
  256.9 10.9 %collective-permute-start.35 = (bf16[2,576,128]{2,1,0:T(8,128)(2,1)}, bf16[2,576,128]{2,1,0:T(8,128)(2,1)S(1)}, u32[]{:S(2)}, u32[]{:S(2)}) collective-permute-start(bf16[2,576,128]{2,1,0:T(8,128)(2,1)} %get-tuple-element.154), channel_id=1, source_target_pairs={{0,32},{32,0},{64,96},{96,64},{1,33},{33,1},{65,97},{97,65},{2,34}... | collective-permute-start | bytes 884744 | tf_op jit(solution)/shard_map/ppermute | solution.py:112
  258.1 9.7 %collective-permute-start.36 = (bf16[2,576,128]{2,1,0:T(8,128)(2,1)}, bf16[2,576,128]{2,1,0:T(8,128)(2,1)S(1)}, u32[]{:S(2)}, u32[]{:S(2)}) collective-permute-start(bf16[2,576,128]{2,1,0:T(8,128)(2,1)} %get-tuple-element.156), channel_id=1, source_target_pairs={{32,64},{64,32},{0,96},{96,0},{33,65},{65,33},{1,97},{97,1},{34,66... | collective-permute-start | bytes 884744 | tf_op jit(solution)/shard_map/ppermute | solution.py:112
  259.9 23.9 %all-to-all-start.5 = ((bf16[32,192,128]{2,1,0:T(8,128)(2,1)}), bf16[32,192,128]{2,1,0:T(8,128)(2,1)S(1)}, u32[]{:S(2)}, u32[]{:S(2)}) async-start(bf16[32,192,128]{2,1,0:T(8,128)(2,1)} %get-tuple-element.149), calls=%async_computation.5 | async-start | bytes 3145728 | tf_op jit(solution)/shard_map/all_to_all | solution.py:147
  271.6 19.7 %collective-permute-start.37 = (bf16[1,576,128]{2,1,0:T(8,128)(2,1)}, bf16[1,576,128]{2,1,0:T(8,128)(2,1)S(1)}, u32[]{:S(2)}, u32[]{:S(2)}) collective-permute-start(bf16[1,576,128]{2,1,0:T(8,128)(2,1)} %get-tuple-element.161), channel_id=1, source_target_pairs={{4,8},{8,4},{0,12},{12,0},{5,9},{9,5},{1,13},{13,1},{6,10},{10,6},... | collective-permute-start | bytes 442376 | tf_op jit(solution)/shard_map/ppermute | solution.py:112
  274.1 17.3 %collective-permute-start.38 = (bf16[1,576,128]{2,1,0:T(8,128)(2,1)}, bf16[1,576,128]{2,1,0:T(8,128)(2,1)S(1)}, u32[]{:S(2)}, u32[]{:S(2)}) collective-permute-start(bf16[1,576,128]{2,1,0:T(8,128)(2,1)} %get-tuple-element.162), channel_id=1, source_target_pairs={{0,32},{32,0},{64,96},{96,64},{1,33},{33,1},{65,97},{97,65},{2,34}... | collective-permute-start | bytes 442376 | tf_op jit(solution)/shard_map/ppermute | solution.py:112
  275.3 16.1 %collective-permute-start.39 = (bf16[1,576,128]{2,1,0:T(8,128)(2,1)}, bf16[1,576,128]{2,1,0:T(8,128)(2,1)S(1)}, u32[]{:S(2)}, u32[]{:S(2)}) collective-permute-start(bf16[1,576,128]{2,1,0:T(8,128)(2,1)} %get-tuple-element.163), channel_id=1, source_target_pairs={{32,64},{64,32},{0,96},{96,0},{33,65},{65,33},{1,97},{97,1},{34,66... | collective-permute-start | bytes 442376 | tf_op jit(solution)/shard_map/ppermute | solution.py:112
  277.0 14.3 %collective-permute-start.40 = (bf16[1,576,128]{2,1,0:T(8,128)(2,1)}, bf16[1,576,128]{2,1,0:T(8,128)(2,1)S(1)}, u32[]{:S(2)}, u32[]{:S(2)}) collective-permute-start(bf16[1,576,128]{2,1,0:T(8,128)(2,1)} %get-tuple-element.164), channel_id=1, source_target_pairs={{0,4},{4,0},{8,12},{12,8},{1,5},{5,1},{9,13},{13,9},{2,6},{6,2},{1... | collective-permute-start | bytes 442376 | tf_op jit(solution)/shard_map/ppermute | solution.py:112
  287.0 12.7 %all-to-all-start.6 = ((bf16[8,192,128]{2,1,0:T(8,128)(2,1)}), bf16[8,192,128]{2,1,0:T(8,128)(2,1)S(1)}, u32[]{:S(2)}, u32[]{:S(2)}) async-start(bf16[8,192,128]{2,1,0:T(8,128)(2,1)} %fold_dq_kernel.1), calls=%async_computation.6 | async-start | bytes 786432 | tf_op jit(solution)/shard_map/all_to_all | solution.py:147
  294.4 12.8 %collective-permute-start.41 = (bf16[2608,128]{1,0:T(8,128)(2,1)}, bf16[2608,128]{1,0:T(8,128)(2,1)S(1)}, u32[]{:S(2)}, u32[]{:S(2)}) collective-permute-start(bf16[2608,128]{1,0:T(8,128)(2,1)} %last_step_kernel.1.refs_13_.refs_0_), channel_id=1, source_target_pairs={{0,16},{16,0},{1,17},{17,1},{2,18},{18,2},{3,19},{19,3},{4,20},{20... | collective-permute-start | bytes 2002952 | tf_op jit(solution)/shard_map/ppermute | solution.py:102
  314.7 53.7 %all-to-all-start.7 = ((bf16[32,4,72,128]{3,2,1,0:T(8,128)(2,1)}), bf16[32,4,72,128]{3,2,1,0:T(8,128)(2,1)S(1)}, u32[]{:S(2)}, u32[]{:S(2)}) async-start(bf16[32,4,72,128]{3,2,1,0:T(8,128)(2,1)} %qkv_grads_kernel.1.refs_5_), calls=%async_computation.7 | async-start | bytes 4718592 | tf_op jit(solution)/shard_map/all_to_all | solution.py:147
  330.2 54.9 %collective-permute-start.42 = (bf16[4,128,1536]{2,1,0:T(8,128)(2,1)}, bf16[4,128,1536]{2,1,0:T(8,128)(2,1)}, u32[]{:S(2)}, u32[]{:S(2)}) collective-permute-start(bf16[4,128,1536]{2,1,0:T(8,128)(2,1)} %get-tuple-element.170), channel_id=1, source_target_pairs={{0,1},{1,0},{2,3},{3,2},{4,5},{5,4},{6,7},{7,6},{8,9},{9,8},{10,11... | collective-permute-start | bytes 4718600 | tf_op jit(solution)/shard_map/ppermute | solution.py:81
  344.5 14.8 %collective-permute-start.45 = (bf16[1,656,128]{2,1,0:T(8,128)(2,1)S(1)}, bf16[1,656,128]{2,1,0:T(8,128)(2,1)S(1)}, u32[]{:S(2)}, u32[]{:S(2)}) collective-permute-start(bf16[1,656,128]{2,1,0:T(8,128)(2,1)S(1)} %copy-done.52), channel_id=1, source_target_pairs={{0,32},{32,0},{64,96},{96,64},{1,33},{33,1},{65,97},{97,65},{2,34}... | collective-permute-start | bytes 503816 | tf_op jit(solution)/shard_map/ppermute | solution.py:112
  346.0 14.8 %collective-permute-start.44 = (bf16[1,656,128]{2,1,0:T(8,128)(2,1)S(1)}, bf16[1,656,128]{2,1,0:T(8,128)(2,1)S(1)}, u32[]{:S(2)}, u32[]{:S(2)}) collective-permute-start(bf16[1,656,128]{2,1,0:T(8,128)(2,1)S(1)} %copy-done.51), channel_id=1, source_target_pairs={{4,8},{8,4},{0,12},{12,0},{5,9},{9,5},{1,13},{13,1},{6,10},{10,6},... | collective-permute-start | bytes 503816 | tf_op jit(solution)/shard_map/ppermute | solution.py:112
  348.4 10.7 %collective-permute-start.46 = (bf16[1,640,128]{2,1,0:T(8,128)(2,1)S(1)}, bf16[1,640,128]{2,1,0:T(8,128)(2,1)S(1)}, u32[]{:S(2)}, u32[]{:S(2)}) collective-permute-start(bf16[1,640,128]{2,1,0:T(8,128)(2,1)S(1)} %copy-done.55), channel_id=1, source_target_pairs={{32,64},{64,32},{0,96},{96,0},{33,65},{65,33},{1,97},{97,1},{34,66... | collective-permute-start | bytes 491528 | tf_op jit(solution)/shard_map/ppermute | solution.py:112
  350.2 9.0 %collective-permute-start.47 = (bf16[1,640,128]{2,1,0:T(8,128)(2,1)S(1)}, bf16[1,640,128]{2,1,0:T(8,128)(2,1)S(1)}, u32[]{:S(2)}, u32[]{:S(2)}) collective-permute-start(bf16[1,640,128]{2,1,0:T(8,128)(2,1)S(1)} %copy-done.56), channel_id=1, source_target_pairs={{0,4},{4,0},{8,12},{12,8},{1,5},{5,1},{9,13},{13,9},{2,6},{6,2},{1... | collective-permute-start | bytes 491528 | tf_op jit(solution)/shard_map/ppermute | solution.py:112
  364.0 13.2 %collective-permute-start.49 = (bf16[2,656,128]{2,1,0:T(8,128)(2,1)}, bf16[2,656,128]{2,1,0:T(8,128)(2,1)S(1)}, u32[]{:S(2)}, u32[]{:S(2)}) collective-permute-start(bf16[2,656,128]{2,1,0:T(8,128)(2,1)} %get-tuple-element.177.refs_1_), channel_id=1, source_target_pairs={{4,8},{8,4},{0,12},{12,0},{5,9},{9,5},{1,13},{13,1},{6,10},{10,6},... | collective-permute-start | bytes 1007624 | tf_op jit(solution)/shard_map/ppermute | solution.py:112
  366.8 13.3 %collective-permute-start.48 = (bf16[2,656,128]{2,1,0:T(8,128)(2,1)}, bf16[2,656,128]{2,1,0:T(8,128)(2,1)S(1)}, u32[]{:S(2)}, u32[]{:S(2)}) collective-permute-start(bf16[2,656,128]{2,1,0:T(8,128)(2,1)} %get-tuple-element.176.refs_3_.refs_0_), channel_id=1, source_target_pairs={{0,4},{4,0},{8,12},{12,8},{1,5},{5,1},{9,13},{13,9},{2,6},{6,2},{1... | collective-permute-start | bytes 1007624 | tf_op jit(solution)/shard_map/ppermute | solution.py:112
  366.8 10.3 %collective-permute-start.51 = (bf16[2,640,128]{2,1,0:T(8,128)(2,1)}, bf16[2,640,128]{2,1,0:T(8,128)(2,1)}, u32[]{:S(2)}, u32[]{:S(2)}) collective-permute-start(bf16[2,640,128]{2,1,0:T(8,128)(2,1)} %get-tuple-element.179.refs_3_), channel_id=1, source_target_pairs={{32,64},{64,32},{0,96},{96,0},{33,65},{65,33},{1,97},{97,1},{34,66... | collective-permute-start | bytes 983048 | tf_op jit(solution)/shard_map/ppermute | solution.py:112
  375.2 9.9 %collective-permute-start.56 = (bf16[80,128]{1,0:T(8,128)(2,1)}, bf16[80,128]{1,0:T(8,128)(2,1)S(1)}, u32[]{:S(2)}, u32[]{:S(2)}) collective-permute-start(bf16[80,128]{1,0:T(8,128)(2,1)} %get-tuple-element.186), channel_id=1, source_target_pairs={{0,1},{1,0},{2,3},{3,2},{4,5},{5,4},{6,7},{7,6},{8,9},{9,8},{10,11... | collective-permute-start | bytes 61448 | tf_op jit(solution)/shard_map/ppermute | solution.py:81
  377.1 8.9 %collective-permute-start.57 = (bf16[80,128]{1,0:T(8,128)(2,1)}, bf16[80,128]{1,0:T(8,128)(2,1)S(1)}, u32[]{:S(2)}, u32[]{:S(2)}) collective-permute-start(bf16[80,128]{1,0:T(8,128)(2,1)} %get-tuple-element.187), channel_id=1, source_target_pairs={{0,2},{2,0},{1,3},{3,1},{4,6},{6,4},{5,7},{7,5},{8,10},{10,8},{9,1... | collective-permute-start | bytes 61448 | tf_op jit(solution)/shard_map/ppermute | solution.py:85
  377.2 12.2 %collective-permute-start.58 = (bf16[80,128]{1,0:T(8,128)(2,1)}, bf16[80,128]{1,0:T(8,128)(2,1)S(1)}, u32[]{:S(2)}, u32[]{:S(2)}) collective-permute-start(bf16[80,128]{1,0:T(8,128)(2,1)} %get-tuple-element.188), channel_id=1, source_target_pairs={{0,3},{1,2},{2,1},{3,0},{4,7},{5,6},{6,5},{7,4},{8,11},{9,10},{10,... | collective-permute-start | bytes 61448 | tf_op jit(solution)/shard_map/ppermute | solution.py:89
  384.1 17.7 %collective-permute-start.54 = (bf16[4,640,128]{2,1,0:T(8,128)(2,1)}, bf16[4,640,128]{2,1,0:T(8,128)(2,1)}, u32[]{:S(2)}, u32[]{:S(2)}) collective-permute-start(bf16[4,640,128]{2,1,0:T(8,128)(2,1)} %get-tuple-element.184.refs_2_), channel_id=1, source_target_pairs={{4,8},{8,4},{0,12},{12,0},{5,9},{9,5},{1,13},{13,1},{6,10},{10,6},... | collective-permute-start | bytes 1966088 | tf_op jit(solution)/shard_map/ppermute | solution.py:112
  385.1 16.7 %collective-permute-start.55 = (bf16[4,640,128]{2,1,0:T(8,128)(2,1)}, bf16[4,640,128]{2,1,0:T(8,128)(2,1)}, u32[]{:S(2)}, u32[]{:S(2)}) collective-permute-start(bf16[4,640,128]{2,1,0:T(8,128)(2,1)} %get-tuple-element.185.refs_3_), channel_id=1, source_target_pairs={{0,32},{32,0},{64,96},{96,64},{1,33},{33,1},{65,97},{97,65},{2,34}... | collective-permute-start | bytes 1966088 | tf_op jit(solution)/shard_map/ppermute | solution.py:112
  385.1 17.5 %collective-permute-start.53 = (bf16[4,656,128]{2,1,0:T(8,128)(2,1)}, bf16[4,656,128]{2,1,0:T(8,128)(2,1)}, u32[]{:S(2)}, u32[]{:S(2)}) collective-permute-start(bf16[4,656,128]{2,1,0:T(8,128)(2,1)} %get-tuple-element.183.refs_1_), channel_id=1, source_target_pairs={{0,4},{4,0},{8,12},{12,8},{1,5},{5,1},{9,13},{13,9},{2,6},{6,2},{1... | collective-permute-start | bytes 2015240 | tf_op jit(solution)/shard_map/ppermute | solution.py:112
  386.0 19.0 %collective-permute-start.52 = (bf16[4,656,128]{2,1,0:T(8,128)(2,1)}, bf16[4,656,128]{2,1,0:T(8,128)(2,1)}, u32[]{:S(2)}, u32[]{:S(2)}) collective-permute-start(bf16[4,656,128]{2,1,0:T(8,128)(2,1)} %get-tuple-element.182.refs_5_.refs_0_), channel_id=1, source_target_pairs={{32,64},{64,32},{0,96},{96,0},{33,65},{65,33},{1,97},{97,1},{34,66... | collective-permute-start | bytes 2015240 | tf_op jit(solution)/shard_map/ppermute | solution.py:112
  389.3 29.8 %collective-permute-start.43 = (bf16[2,128,1536]{2,1,0:T(8,128)(2,1)S(1)}, bf16[2,128,1536]{2,1,0:T(8,128)(2,1)}, u32[]{:S(2)}, u32[]{:S(2)}) collective-permute-start(bf16[2,128,1536]{2,1,0:T(8,128)(2,1)S(1)} %add_convert_fusion), channel_id=1, source_target_pairs={{0,2},{2,0},{1,3},{3,1},{4,6},{6,4},{5,7},{7,5},{8,10},{10,8},{9,1... | collective-permute-start | bytes 2359304 | tf_op jit(solution)/shard_map/ppermute | solution.py:85
  392.4 41.5 %all-to-all-start.8 = ((bf16[32,4,72,128]{3,2,1,0:T(8,128)(2,1)}), bf16[32,4,72,128]{3,2,1,0:T(8,128)(2,1)S(1)}, u32[]{:S(2)}, u32[]{:S(2)}) async-start(bf16[32,4,72,128]{3,2,1,0:T(8,128)(2,1)} %get-tuple-element.189.refs_8_), calls=%async_computation.8 | async-start | bytes 4718592 | tf_op jit(solution)/shard_map/all_to_all | solution.py:147
  409.9 48.1 %collective-permute-start.61 = (bf16[8,640,128]{2,1,0:T(8,128)(2,1)}, bf16[8,640,128]{2,1,0:T(8,128)(2,1)}, u32[]{:S(2)}, u32[]{:S(2)}) collective-permute-start(bf16[8,640,128]{2,1,0:T(8,128)(2,1)} %get-tuple-element.199.refs_3_), channel_id=1, source_target_pairs={{0,4},{4,0},{8,12},{12,8},{1,5},{5,1},{9,13},{13,9},{2,6},{6,2},{1... | collective-permute-start | bytes 3932168 | tf_op jit(solution)/shard_map/ppermute | solution.py:112
  410.3 48.1 %collective-permute-start.62 = (bf16[8,640,128]{2,1,0:T(8,128)(2,1)}, bf16[8,640,128]{2,1,0:T(8,128)(2,1)}, u32[]{:S(2)}, u32[]{:S(2)}) collective-permute-start(bf16[8,640,128]{2,1,0:T(8,128)(2,1)} %get-tuple-element.200.refs_4_), channel_id=1, source_target_pairs={{4,8},{8,4},{0,12},{12,0},{5,9},{9,5},{1,13},{13,1},{6,10},{10,6},... | collective-permute-start | bytes 3932168 | tf_op jit(solution)/shard_map/ppermute | solution.py:112
  412.8 49.4 %collective-permute-start.60 = (bf16[8,656,128]{2,1,0:T(8,128)(2,1)}, bf16[8,656,128]{2,1,0:T(8,128)(2,1)}, u32[]{:S(2)}, u32[]{:S(2)}) collective-permute-start(bf16[8,656,128]{2,1,0:T(8,128)(2,1)} %get-tuple-element.198.refs_2_), channel_id=1, source_target_pairs={{32,64},{64,32},{0,96},{96,0},{33,65},{65,33},{1,97},{97,1},{34,66... | collective-permute-start | bytes 4030472 | tf_op jit(solution)/shard_map/ppermute | solution.py:112
  414.1 48.2 %collective-permute-start.59 = (bf16[8,656,128]{2,1,0:T(8,128)(2,1)}, bf16[8,656,128]{2,1,0:T(8,128)(2,1)}, u32[]{:S(2)}, u32[]{:S(2)}) collective-permute-start(bf16[8,656,128]{2,1,0:T(8,128)(2,1)} %get-tuple-element.190.refs_7_.refs_1_), channel_id=1, source_target_pairs={{0,32},{32,0},{64,96},{96,64},{1,33},{33,1},{65,97},{97,65},{2,34}... | collective-permute-start | bytes 4030472 | tf_op jit(solution)/shard_map/ppermute | solution.py:112
  (74 other events, 385.0 us)
